TPU v7x, 32 devices: a whole 2x2x4 slice. The times are simulated.
32 devices in a mesh: dp: 2 (over y), fsdp: 16 (over z, x, core).
Axes of the slice: x: 2, y: 2, z: 4, core: 2. Of those that a mesh axis runs over, the one named last changes fastest.
Arguments:
- images: bfloat16 [32, 64, 64, 256], P(('dp', 'fsdp')), may hold values from -6 to 6
- embedding: bfloat16 [32, 512], P(('dp', 'fsdp')), may hold values from -6 to 6
- conv_first: bfloat16 [589824], P(('dp', 'fsdp')), may hold values from -0.125 to 0.125
- conv_second: bfloat16 [589824], P(('dp', 'fsdp')), may hold values from -0.125 to 0.125
- projection: bfloat16 [131072], P(('dp', 'fsdp')), may hold values from -0.25 to 0.25
- vectors: bfloat16 [1536], P(('dp', 'fsdp')), may hold values from -1 to 1.5, as said below
- cotangent: bfloat16 [32, 64, 64, 256], P(('dp', 'fsdp')), may hold values from -6 to 6
Outputs:
- output: bfloat16 [32, 64, 64, 256], P(('dp', 'fsdp'))
- input_grad: float32 [32, 64, 64, 256], P(('dp', 'fsdp'))
- embedding_grad: float32 [32, 512], P(('dp', 'fsdp'))
- conv_first_grad: float32 [589824], P(('dp', 'fsdp'))
- conv_second_grad: float32 [589824], P(('dp', 'fsdp'))
- projection_grad: float32 [131072], P(('dp', 'fsdp'))
- vectors_grad: float32 [1536], P(('dp', 'fsdp'))
Inputs may be any that keep to these rules, and one draw needn't show every extreme that they name: `vectors`: rows 0 and 3 (gains) lie near 1, the other rows near 0.
All inputs are finite; a program needn't handle non-finite values.
Results may differ from a plain program's by a relative error of at most 0.0056.
Values may be sent and summed in bfloat16 or wider, within the bound.
No kernel may reach another device: no remote copies, remote signals or barrier semaphores. Data moves between devices by JAX's collectives and lax.ppermute only.
A program may use at most 128 MiB of HBM per device.

v0:
```python
import functools
import math

import jax
import jax.numpy as jnp
from jax import lax
from jax.experimental import pallas as pl
from jax.experimental.pallas import tpu as pltpu
from jax.sharding import PartitionSpec as P

GROUPS = 32
EPS = 1e-05
AXES = ("dp", "fsdp")


class Wires:
    def __init__(self, n_dp, n_fsdp):
        self.n = n_dp * n_fsdp
        self.bits = int(math.log2(self.n))
        fsdp_bits = int(math.log2(n_fsdp))
        assert 1 << self.bits == self.n and 1 << fsdp_bits == n_fsdp and fsdp_bits >= 2 and n_dp >= 2
        self.cross_a = 1
        self.cross_b = fsdp_bits
        self.far = [b for b in range(self.bits - 1, 0, -1) if b not in (self.cross_a, self.cross_b)]
        self.me = lax.axis_index(AXES)
        self.core = self.me & 1

    def bit(self, b):
        return (self.me >> b) & 1

    def swap(self, value, b):
        return lax.ppermute(value, AXES, [(i, i ^ (1 << b)) for i in range(self.n)])

    def swap_cross(self, value, first):
        even, odd = (self.cross_a, self.cross_b) if first else (self.cross_b, self.cross_a)
        return lax.ppermute(
            value, AXES, [(i, i ^ (1 << (odd if i & 1 else even))) for i in range(self.n)]
        )

    def cross_bit(self, first):
        a, b = self.bit(self.cross_a), self.bit(self.cross_b)
        return jnp.where(self.core == (0 if first else 1), a, b)


def merge(mine, other, axis, bit):
    mine, other = jnp.expand_dims(mine, axis), jnp.expand_dims(other, axis)
    shape = list(mine.shape)
    shape[axis] = 2
    place = lax.broadcasted_iota(jnp.int32, shape, axis)
    return jnp.where(place == bit, mine, other)


def gather(wires, parts):
    bufs = list(parts)
    far = sorted(wires.far, reverse=True)
    for at, b in enumerate(far):
        got = [wires.swap(v, b) for v in bufs]
        bufs = [merge(v, r, at, wires.bit(b)) for v, r in zip(bufs, got)]
    depth = len(far)
    got = [wires.swap_cross(v, True) for v in bufs]
    bufs = [merge(v, r, depth, wires.cross_bit(True)) for v, r in zip(bufs, got)]
    got = [wires.swap_cross(v, False) for v in bufs]
    bufs = [merge(v, r, 0, wires.cross_bit(False)) for v, r in zip(bufs, got)]
    bufs = [jnp.where(wires.core == 0, v, jnp.swapaxes(v, 0, depth + 1)) for v in bufs]
    got = [wires.swap(v, 0) for v in bufs]
    bufs = [merge(v, r, depth + 2, wires.core) for v, r in zip(bufs, got)]
    order = [wires.cross_b, *far, wires.cross_a, 0]
    want = sorted(order, reverse=True)
    out = []
    for v in bufs:
        rest = list(range(len(order), v.ndim))
        v = v.transpose([order.index(b) for b in want] + rest)
        out.append(v.reshape((wires.n,) + v.shape[len(order):]))
    return out


def pick(value, axis, index):
    return lax.dynamic_index_in_dim(value, index, axis, keepdims=False)


def reduce_scatter(wires, value):
    far = sorted(wires.far, reverse=True)
    order = [wires.cross_b, *far, wires.cross_a, 0]
    want = sorted(order, reverse=True)
    v = value.reshape((2,) * len(order) + value.shape[1:])
    rest = list(range(len(order), v.ndim))
    v = v.transpose([want.index(b) for b in order] + rest)
    depth = len(far)

    def step(v, axis, bit, swap):
        sent = pick(v, axis, 1 - bit).astype(jnp.bfloat16)
        return pick(v, axis, bit) + swap(sent).astype(jnp.float32)

    v = step(v, depth + 2, wires.core, lambda s: wires.swap(s, 0))
    v = jnp.where(wires.core == 0, v, jnp.swapaxes(v, 0, depth + 1))
    v = step(v, depth + 1, wires.cross_bit(True), lambda s: wires.swap_cross(s, True))
    v = step(v, 0, wires.cross_bit(False), lambda s: wires.swap_cross(s, False))
    for at in range(len(far) - 1, -1, -1):
        b = far[at]
        v = step(v, at, wires.bit(b), lambda s, b=b: wires.swap(s, b))
    return v


ROWS = 16
F32 = jnp.float32
BF16 = jnp.bfloat16
VMEM_BYTES = 44 * 1024 * 1024


def group_sum(totals):
    channels = totals.shape[1]
    lane = lax.broadcasted_iota(jnp.int32, totals.shape, 1)
    span = 1
    while span < channels // GROUPS:
        up = pltpu.roll(totals, channels - span, 1)
        down = pltpu.roll(totals, span, 1)
        totals = totals + jnp.where((lane & span) == 0, up, down)
        span *= 2
    return totals


def fold(values):
    channels = values.shape[-1]
    return jnp.sum(values.reshape(-1, 8, channels), 0)


def total(partial):
    return jnp.sum(partial, 0, keepdims=True)


def sigmoid(v):
    return 0.5 * jnp.tanh(0.5 * v) + 0.5


def clear_edges(three):
    height = three.shape[1] - 2
    zero = jnp.zeros((3, 1) + three.shape[2:], three.dtype)
    three[:, 0:1] = zero
    three[:, height + 1 : height + 2] = zero


def store_three(three, row, value):
    width = value.shape[0]
    column = lax.broadcasted_iota(jnp.int32, value.shape, 0)
    left = jnp.where(column == 0, 0.0, pltpu.roll(value, 1, 0))
    right = jnp.where(column == width - 1, 0.0, pltpu.roll(value, width - 1, 0))
    three[0, row + 1] = left.astype(three.dtype)
    three[1, row + 1] = value.astype(three.dtype)
    three[2, row + 1] = right.astype(three.dtype)


def conv_rows(three, kernel, start, back):
    width, channels = three.shape[2:]
    acc = None
    for tap in range(9):
        lhs = three[tap % 3, pl.ds(start + tap // 3, ROWS)].reshape(ROWS * width, channels)
        at = (8 - tap if back else tap) * channels
        rhs = kernel[at : at + channels, :]
        part = lax.dot_general(
            lhs, rhs, (((1,), (1 if back else 0,)), ((), ())), preferred_element_type=F32
        )
        acc = part if acc is None else acc + part
    return acc


def kernel_grad(acts, three, out):
    height, width, channels = acts.shape

    def step(tap, _):
        row = tap // 3
        col = tap - 3 * row
        lhs = acts[...].reshape(height * width, channels)
        rhs = three[2 - col, pl.ds(2 - row, height)].reshape(height * width, channels)
        out[pl.ds(pl.multiple_of(tap * channels, channels), channels), :] = lax.dot_general(
            lhs, rhs, (((0,), (0,)), ((), ())), preferred_element_type=F32
        )
        return 0

    lax.fori_loop(0, 9, step, 0)


def prepare_kernel(x, g, stats, three, g_sum):
    height, width, channels = x.shape
    count = height * width * (channels // GROUPS)
    zero = jnp.zeros((8, channels), F32)
    clear_edges(three)

    def first(i, carry):
        s, gs = carry
        row = i * 4
        s = s + fold(x[pl.ds(row, 4)].astype(F32))
        rows = g[pl.ds(row, 4)].astype(F32)
        for j in range(4):
            store_three(three, row + j, rows[j])
        return s, gs + fold(rows)

    s, gs = lax.fori_loop(0, height // 4, first, (zero, zero))
    g_sum[...] = total(gs)
    mean = group_sum(total(s)) / count

    def second(i, v):
        d = x[pl.ds(i * 4, 4)].astype(F32) - mean
        return v + fold(d * d)

    v = lax.fori_loop(0, height // 4, second, zero)
    inv = lax.rsqrt(group_sum(total(v)) / count + EPS)
    stats[0:1, :] = mean
    stats[1:2, :] = inv


def first_kernel(x, stats, vec, time, kernel, act, centred, stats_out, three):
    height, width, channels = x.shape
    count = height * width * (channels // GROUPS)
    mean, scale, shift = stats[0:1, :], stats[1:2, :] * vec[0:1, :], vec[1:2, :]
    offset = vec[2:3, :] + time[...]
    zero = jnp.zeros((8, channels), F32)
    clear_edges(three)

    def activate(i, _):
        row = i * 4
        h = (x[pl.ds(row, 4)].astype(F32) - mean) * scale + shift
        a = h * sigmoid(h)
        act[pl.ds(row, 4)] = a.astype(BF16)
        for j in range(4):
            store_three(three, row + j, a[j])
        return 0

    lax.fori_loop(0, height // 4, activate, 0)

    def conv(i, s):
        row = pl.multiple_of(i * ROWS, ROWS)
        acc = conv_rows(three, kernel, row, False)
        centred[pl.ds(row * width, ROWS * width), :] = acc
        return s + fold(acc)

    s = lax.fori_loop(0, height // ROWS, conv, zero)
    mean_two = group_sum(total(s) / (height * width) + offset) / (channels // GROUPS)
    move = offset - mean_two

    def centre(i, v):
        at = pl.ds(i * 256, 256)
        d = centred[at, :] + move
        centred[at, :] = d
        return v + fold(d * d)

    v = lax.fori_loop(0, height * width // 256, centre, zero)
    stats_out[...] = lax.rsqrt(group_sum(total(v)) / count + EPS)


def second_kernel(three, centred, inv, vec, kernel, dh, act, sums, grad):
    height, width, channels = act.shape
    scale, shift = inv[...] * vec[3:4, :], vec[4:5, :]
    zero = jnp.zeros((8, channels), F32)

    def conv(i, carry):
        s, sc = carry
        row = pl.multiple_of(i * ROWS, ROWS)
        at = pl.ds(row * width, ROWS * width)
        acc = conv_rows(three, kernel, row, True)
        c = centred[at, :]
        h = c * scale + shift
        sig = sigmoid(h)
        a = h * sig
        act[pl.ds(row, ROWS)] = a.astype(BF16).reshape(ROWS, width, channels)
        d = acc * (sig + a * (1.0 - sig))
        dh[at, :] = d
        return s + fold(d), sc + fold(d * c)

    s, sc = lax.fori_loop(0, height // ROWS, conv, (zero, zero))
    sums[0:1, :] = total(sc) * inv[...]
    sums[1:2, :] = total(s)
    kernel_grad(act, three, grad)


def third_kernel(dh, centred, inv, sums, vec, act, three, dc_sum, grad):
    height, width, channels = act.shape
    count = height * width * (channels // GROUPS)
    gain = vec[3:4, :]
    mean_u = group_sum(sums[1:2, :] * gain) / count
    mean_un = group_sum(sums[0:1, :] * gain) / count
    scale = inv[...] * gain
    base = inv[...] * mean_u
    slope = inv[...] * inv[...] * mean_un
    clear_edges(three)

    def back(i, s):
        row = i * 4
        at = pl.ds(row * width, 4 * width)
        d = dh[at, :] * scale - base - centred[at, :] * slope
        rows = d.reshape(4, width, channels)
        for j in range(4):
            store_three(three, row + j, rows[j])
        return s + fold(d)

    dc_sum[...] = total(lax.fori_loop(0, height // 4, back, jnp.zeros((8, channels), F32)))
    kernel_grad(act, three, grad)


def fourth_kernel(three, x, g, stats, vec, kernel, result, sums, dh):
    height, width, channels = x.shape
    count = height * width * (channels // GROUPS)
    mean, inv, gain, shift = stats[0:1, :], stats[1:2, :], vec[0:1, :], vec[1:2, :]
    scale = inv * gain
    zero = jnp.zeros((8, channels), F32)

    def conv(i, carry):
        s, sn = carry
        row = pl.multiple_of(i * ROWS, ROWS)
        acc = conv_rows(three, kernel, row, True)
        c = x[pl.ds(row, ROWS)].astype(F32).reshape(ROWS * width, channels) - mean
        h = c * scale + shift
        sig = sigmoid(h)
        d = acc * (sig + h * sig * (1.0 - sig))
        dh[pl.ds(row * width, ROWS * width), :] = d
        return s + fold(d), sn + fold(d * c)

    s, sn = lax.fori_loop(0, height // ROWS, conv, (zero, zero))
    s, sn = total(s), total(sn) * inv
    sums[0:1, :] = sn
    sums[1:2, :] = s
    base = inv * (group_sum(s * gain) / count)
    slope = inv * inv * (group_sum(sn * gain) / count)

    def back(i, _):
        row = i * 4
        d = dh[pl.ds(row * width, 4 * width), :].reshape(4, width, channels)
        c = x[pl.ds(row, 4)].astype(F32) - mean
        result[pl.ds(row, 4)] = g[pl.ds(row, 4)].astype(F32) + (d * scale - base - c * slope)
        return 0

    lax.fori_loop(0, height // 4, back, 0)


def last_kernel(act, x, vec, kernel, result, three):
    height, width, channels = x.shape
    bias = vec[5:6, :]
    clear_edges(three)

    def spread(i, _):
        rows = act[pl.ds(i * 4, 4)].astype(F32)
        for j in range(4):
            store_three(three, i * 4 + j, rows[j])
        return 0

    lax.fori_loop(0, height // 4, spread, 0)

    def conv(i, _):
        row = pl.multiple_of(i * ROWS, ROWS)
        acc = conv_rows(three, kernel, row, False).reshape(ROWS, width, channels)
        result[pl.ds(row, ROWS)] = (x[pl.ds(row, ROWS)].astype(F32) + acc + bias).astype(BF16)
        return 0

    lax.fori_loop(0, height // ROWS, conv, 0)


def call(body, outs, *args, scratch=(), flops=0):
    return pl.pallas_call(
        body,
        out_shape=[jax.ShapeDtypeStruct(shape, dtype) for shape, dtype in outs],
        scratch_shapes=[pltpu.VMEM(shape, dtype) for shape, dtype in scratch],
        compiler_params=pltpu.CompilerParams(vmem_limit_bytes=VMEM_BYTES),
        cost_estimate=pl.CostEstimate(flops=flops, bytes_accessed=4 << 20, transcendentals=0),
    )(*args)


def swish_slope(values):
    sigma = jax.nn.sigmoid(values)
    return sigma * (1.0 + values * (1.0 - sigma))


def local(sizes, images, embedding, conv_first, conv_second, projection, vectors, cotangent):
    count, height, width, channels = images.shape
    assert count == 1
    emb_width = embedding.shape[-1]
    wires = Wires(*sizes)
    n = wires.n
    n_vec = vectors.shape[0]
    rows_conv = conv_first.shape[0] // channels
    rows_proj = projection.shape[0] // channels
    rows_vec = -(-n_vec // channels)
    pixels = height * width
    three = ((3, height + 2, width, channels), BF16)
    maps = ((height, width, channels), BF16)
    flat = ((pixels, channels), F32)
    line = ((1, channels), F32)
    pair = ((2, channels), F32)
    taps = ((9 * channels, channels), F32)
    conv_flops = 2 * 9 * pixels * channels * channels

    def vec_rows(v):
        return jnp.pad(v, ((0, 0), (0, rows_vec * channels - n_vec))).reshape(-1, rows_vec, channels)

    x, g = images[0], cotangent[0]
    stats_one, g_three, g_sum = call(prepare_kernel, [pair, three, line], x, g)

    small = jnp.concatenate([projection.reshape(rows_proj, channels), vec_rows(vectors[None])[0]])
    one, small = gather(wires, [conv_first.reshape(rows_conv, channels), small])
    two, = gather(wires, [conv_second.reshape(rows_conv, channels)])
    kernel_one = one.reshape(9 * channels, channels)
    kernel_two = two.reshape(9 * channels, channels)
    project = small[:, :rows_proj].reshape(emb_width, channels)
    vector = small[:, rows_proj:].reshape(n, -1)[:, :n_vec].reshape(6, channels).astype(F32)

    emb_float = embedding.astype(F32)
    emb_act = jax.nn.silu(emb_float).astype(BF16)
    time = jnp.dot(emb_act, project, preferred_element_type=F32)
    act_one, centred, inv_two = call(
        first_kernel, [maps, flat, line], x, stats_one, vector, time, kernel_one, scratch=[three], flops=conv_flops
    )
    dh, act_two, sums_two, grad_two = call(
        second_kernel,
        [flat, maps, pair, taps],
        g_three,
        centred,
        inv_two,
        vector,
        kernel_two,
        flops=2 * conv_flops,
    )
    second_sum = reduce_scatter(wires, grad_two.reshape(n, rows_conv, channels))
    e_three, dc_sum, grad_one = call(
        third_kernel, [three, line, taps], dh, centred, inv_two, sums_two, vector, act_one, flops=conv_flops
    )
    first_sum = reduce_scatter(wires, grad_one.reshape(n, rows_conv, channels))
    project_grad = emb_act.astype(F32).reshape(emb_width, 1) * dc_sum
    grad_emb_act = jnp.dot(dc_sum, project.astype(F32).T, precision=lax.Precision.HIGHEST)
    embedding_grad = grad_emb_act * swish_slope(emb_float)
    input_grad, sums_one = call(
        fourth_kernel, [(maps[0], F32), pair], e_three, x, g, stats_one, vector, kernel_one, scratch=[flat], flops=conv_flops
    )
    vector_grad = jnp.concatenate([sums_one, dc_sum, sums_two, g_sum]).reshape(-1)
    small_grad = jnp.concatenate(
        [project_grad.reshape(n, rows_proj, channels), vec_rows(vector_grad.reshape(n, n_vec))], axis=1
    )
    small_sum = reduce_scatter(wires, small_grad)
    output, = call(last_kernel, [maps], act_two, x, vector, kernel_two, scratch=[three], flops=conv_flops)
    return (
        output[None],
        input_grad[None],
        embedding_grad,
        first_sum.reshape(-1),
        second_sum.reshape(-1),
        small_sum[:rows_proj].reshape(-1),
        small_sum[rows_proj:].reshape(-1)[:n_vec],
    )


def solution(mesh):
    sizes = (mesh.shape["dp"], mesh.shape["fsdp"])
    split = P(AXES)
    maps = P(AXES, None, None, None)
    in_specs = (maps, P(AXES, None), split, split, split, split, maps)
    out_specs = (maps, maps, P(AXES, None), split, split, split, split)

    def body(*args):
        return local(sizes, *args)

    return jax.shard_map(body, mesh=mesh, in_specs=in_specs, out_specs=out_specs, check_vma=False)
```

profile of v0, /device:TPU:0, one launch (start us, length us, event | category | flops | bytes accessed | tf_op | source)
XLA Modules:
  0.0 165.1 jit_solution(17837154100104666976)
XLA Ops:
  2.0 4.0 %collective-permute-start = (bf16[17,256]{1,0:T(8,128)(2,1)S(1)}, bf16[17,256]{1,0:T(8,128)(2,1)S(1)}, u32[]{:S(2)}, u32[]{:S(2)}) collective-permute-start(bf16[17,256]{1,0:T(8,128)(2,1)S(1)} %fusion.22), channel_id=1, source_target_pairs={{0,8},{1,9},{2,10},{3,11},{4,12},{5,13},{6,14},{7,15},{8,0},{9,1},... | collective-permute-start | bytes 26120 | tf_op jit(solution)/shard_map/ppermute | solution.py:32
  7.7 3.0 %collective-permute-start.5 = (bf16[72,256]{1,0:T(8,128)(2,1)S(1)}, bf16[72,256]{1,0:T(8,128)(2,1)S(1)}, u32[]{:S(2)}, u32[]{:S(2)}) collective-permute-start(bf16[72,256]{1,0:T(8,128)(2,1)S(1)} %broadcast_in_dim.311), channel_id=1, source_target_pairs={{0,8},{1,9},{2,10},{3,11},{4,12},{5,13},{6,14},{7,15},{8,0},{9,1},... | collective-permute-start | bytes 110600 | tf_op jit(solution)/shard_map/ppermute | solution.py:32
  14.1 1.6 copy-done
  17.3 5.0 %shard_map.126 = (f32[2,256]{1,0:T(2,128)S(1)}, bf16[3,66,64,256]{3,2,1,0:T(8,128)(2,1)}, f32[1,256]{1,0:T(1,128)S(1)}) custom-call(bf16[64,64,256]{2,1,0:T(8,128)(2,1)S(1)} %bitcast.121, bf16[64,64,256]{2,1,0:T(8,128)(2,1)S(1)} %bitcast.119), custom_call_target="tpu_custom_call" | custom-call | bytes 4194304 | tf_op jit(solution)/shard_map/pallas_call | solution.py:357
  26.6 1.6 collective-permute-start.3
  39.1 3.9 %collective-permute-done.13 = bf16[2,2,2,72,256]{4,3,1,0,2:T(8,128)(2,1)S(1)} collective-permute-done((bf16[2,2,2,72,256]{4,3,1,0,2:T(8,128)(2,1)S(1)}, bf16[2,2,2,72,256]{4,3,1,0,2:T(8,128)(2,1)S(1)}, u32[]{:S(2)}, u32[]{:S(2)}) %collective-permute-start.13) | collective-permute-done | bytes 294944 | tf_op jit(solution)/shard_map/ppermute | solution.py:36
  43.0 3.2 %collective-permute-done.8 = bf16[2,2,2,72,256]{4,3,1,0,2:T(8,128)(2,1)S(1)} collective-permute-done((bf16[2,2,2,72,256]{4,3,1,0,2:T(8,128)(2,1)S(1)}, bf16[2,2,2,72,256]{4,3,1,0,2:T(8,128)(2,1)S(1)}, u32[]{:S(2)}, u32[]{:S(2)}) %collective-permute-start.8) | collective-permute-done | bytes 294944 | tf_op jit(solution)/shard_map/ppermute | solution.py:36
  49.9 2.0 %bitcast_select_fusion.2 = (bf16[2304,256]{1,0:T(8,128)(2,1)S(1)}, bf16[2304,256]{1,0:T(8,128)(2,1)S(1)}) fusion(pred[2304]{0:T(1024)(128)(4,1)S(1)} %iota.91, bf16[2,2,2,2,72,256]{5,4,3,2,1,0:T(8,128)(2,1)} %collective-permute-done.14, bf16[2,2,2,2,72,256]{5,4,3,2,1,0:T(8,128)(2,1)} %copy-done.12, bf16[2,2,2,2,72,256]{5,4,3,2,1,0:T(8,128)(2,1)} %collective-permute-done.9, ...), kind=kLoop, calls=%fused_computation.5 | loop fusion | flops 1179648 | bytes 4720896 | tf_op jit(solution)/shard_map/jit(_where)/select_n | solution.py:50
  51.9 8.7 %shard_map.127 = (bf16[64,64,256]{2,1,0:T(8,128)(2,1)S(1)}, f32[4096,256]{1,0:T(8,128)S(1)}, f32[1,256]{1,0:T(1,128)S(1)}) custom-call(bf16[64,64,256]{2,1,0:T(8,128)(2,1)S(1)} %bitcast.122, f32[2,256]{1,0:T(2,128)S(1)} %get-tuple-element.23.stats, f32[6,256]{1,0:T(8,128)S(1)} %reshape.148.vec, f32[1,256]{1,0:T(1,128)S(1)} %fusion.24.time, ...), custom_call_target="tpu_custom_call" | custom-call | flops 4831838208 | bytes 4194304 | tf_op jit(solution)/shard_map/pallas_call | solution.py:357
  60.6 2.0 %copy-done.8 = f32[4096,256]{1,0:T(8,128)} copy-done((f32[4096,256]{1,0:T(8,128)}, f32[4096,256]{1,0:T(8,128)S(1)}, u32[]{:S(2)}) %copy-start.8) | copy-done | bytes 4194328
  62.6 17.5 %shard_map.128 = (f32[4096,256]{1,0:T(8,128)S(1)}, bf16[64,64,256]{2,1,0:T(8,128)(2,1)S(1)}, f32[2,256]{1,0:T(2,128)S(1)}, f32[2304,256]{1,0:T(8,128)S(1)}) custom-call(bf16[3,66,64,256]{3,2,1,0:T(8,128)(2,1)} %get-tuple-element.22.three, f32[4096,256]{1,0:T(8,128)} %copy-done.8, f32[1,256]{1,0:T(1,128)S(1)} %get-tuple-element.25.inv, ...), custom_call_target="tpu_custom_call" | custom-call | flops 9663676416 | bytes 4194304 | tf_op jit(solution)/shard_map/pallas_call | solution.py:357
  83.0 12.9 %shard_map.130 = (bf16[3,66,64,256]{3,2,1,0:T(8,128)(2,1)}, f32[1,256]{1,0:T(1,128)S(1)}, f32[2304,256]{1,0:T(8,128)S(1)}) custom-call(f32[4096,256]{1,0:T(8,128)S(1)} %get-tuple-element.27.dh, f32[4096,256]{1,0:T(8,128)} %copy-done.8, f32[1,256]{1,0:T(1,128)S(1)} %get-tuple-element.25.inv, f32[2,256]{1,0:T(2,128)S(1)} %get-tuple-element.28.sums, ...), custom_call_target="tpu_custom_call" | custom-call | flops 4831838208 | bytes 4194304 | tf_op jit(solution)/shard_map/pallas_call | solution.py:357
  95.9 13.8 %shard_map.131 = (f32[64,64,256]{2,1,0:T(8,128)}, f32[2,256]{1,0:T(2,128)S(1)}) custom-call(bf16[3,66,64,256]{3,2,1,0:T(8,128)(2,1)} %get-tuple-element.30.three, bf16[64,64,256]{2,1,0:T(8,128)(2,1)S(1)} %bitcast.123, bf16[64,64,256]{2,1,0:T(8,128)(2,1)S(1)} %bitcast.120, f32[2,256]{1,0:T(2,128)S(1)} %get-tuple-element.23.stats, f32[6,256]{1,0:T(8,128)S(1)} %reshape.148.vec, ...), custom_call_target="tpu_custom_call" | custom-call | flops 4831838208 | bytes 4194304 | tf_op jit(solution)/shard_map/pallas_call | solution.py:357
  114.2 8.0 %shard_map.129 = bf16[64,64,256]{2,1,0:T(8,128)(2,1)} custom-call(bf16[64,64,256]{2,1,0:T(8,128)(2,1)S(1)} %copy-done.10, bf16[64,64,256]{2,1,0:T(8,128)(2,1)S(1)} %bitcast.124, f32[6,256]{1,0:T(8,128)S(1)} %reshape.148.vec, bf16[2304,256]{1,0:T(8,128)(2,1)S(1)} %get-tuple-element.37.kernel), custom_call_target="tpu_custom_call" | custom-call | flops 4831838208 | bytes 4194304 | tf_op jit(solution)/shard_map/pallas_call | solution.py:357
  124.7 1.7 %collective-permute-done.27 = bf16[2,2,17,256]{3,2,0,1:T(8,128)(2,1)S(1)} collective-permute-done((bf16[2,2,17,256]{3,2,0,1:T(8,128)(2,1)S(1)}, bf16[2,2,17,256]{3,2,0,1:T(8,128)(2,1)S(1)}, u32[]{:S(2)}, u32[]{:S(2)}) %collective-permute-start.27) | collective-permute-done | bytes 34848 | tf_op jit(solution)/shard_map/ppermute | solution.py:36
  127.9 2.5 %collective-permute-done.28 = bf16[2,17,256]{2,1,0:T(8,128)(2,1)S(1)} collective-permute-done((bf16[2,17,256]{2,1,0:T(8,128)(2,1)S(1)}, bf16[2,17,256]{2,1,0:T(8,128)(2,1)S(1)}, u32[]{:S(2)}, u32[]{:S(2)}) %collective-permute-start.28) | collective-permute-done | bytes 17440 | tf_op jit(solution)/shard_map/ppermute | solution.py:32
  130.9 4.1 %collective-permute-done.29 = bf16[17,256]{1,0:T(8,128)(2,1)S(1)} collective-permute-done((bf16[17,256]{1,0:T(8,128)(2,1)S(1)}, bf16[17,256]{1,0:T(8,128)(2,1)S(1)}, u32[]{:S(2)}, u32[]{:S(2)}) %collective-permute-start.29) | collective-permute-done | bytes 8736 | tf_op jit(solution)/shard_map/ppermute | solution.py:32
  139.0 5.0 %collective-permute-done.16 = bf16[2,2,2,72,256]{4,3,2,1,0:T(8,128)(2,1)S(1)} collective-permute-done((bf16[2,2,2,72,256]{4,3,2,1,0:T(8,128)(2,1)S(1)}, bf16[2,2,2,72,256]{4,3,2,1,0:T(8,128)(2,1)S(1)}, u32[]{:S(2)}, u32[]{:S(2)}) %collective-permute-start.16) | collective-permute-done | bytes 294944 | tf_op jit(solution)/shard_map/ppermute | solution.py:36
  144.1 2.1 %collective-permute-start.17 = (bf16[2,2,72,256]{3,2,1,0:T(8,128)(2,1)S(1)}, bf16[2,2,72,256]{3,2,1,0:T(8,128)(2,1)S(1)}, u32[]{:S(2)}, u32[]{:S(2)}) collective-permute-start(bf16[2,2,72,256]{3,2,1,0:T(8,128)(2,1)S(1)} %fusion.10), channel_id=1, source_target_pairs={{0,16},{1,3},{2,18},{3,1},{4,20},{5,7},{6,22},{7,5},{8,24},{9,11},... | collective-permute-start | bytes 442376 | tf_op jit(solution)/shard_map/ppermute | solution.py:36
  146.2 3.5 %collective-permute-done.21 = bf16[2,2,2,72,256]{4,3,2,1,0:T(8,128)(2,1)S(1)} collective-permute-done((bf16[2,2,2,72,256]{4,3,2,1,0:T(8,128)(2,1)S(1)}, bf16[2,2,2,72,256]{4,3,2,1,0:T(8,128)(2,1)S(1)}, u32[]{:S(2)}, u32[]{:S(2)}) %collective-permute-start.21) | collective-permute-done | bytes 294944 | tf_op jit(solution)/shard_map/ppermute | solution.py:36
  152.8 2.2 %collective-permute-done.22 = bf16[2,2,72,256]{3,2,1,0:T(8,128)(2,1)S(1)} collective-permute-done((bf16[2,2,72,256]{3,2,1,0:T(8,128)(2,1)S(1)}, bf16[2,2,72,256]{3,2,1,0:T(8,128)(2,1)S(1)}, u32[]{:S(2)}, u32[]{:S(2)}) %collective-permute-start.22) | collective-permute-done | bytes 147488 | tf_op jit(solution)/shard_map/ppermute | solution.py:36
  156.4 3.0 %collective-permute-done.23 = bf16[2,72,256]{2,1,0:T(8,128)(2,1)S(1)} collective-permute-done((bf16[2,72,256]{2,1,0:T(8,128)(2,1)S(1)}, bf16[2,72,256]{2,1,0:T(8,128)(2,1)S(1)}, u32[]{:S(2)}, u32[]{:S(2)}) %collective-permute-start.23) | collective-permute-done | bytes 73760 | tf_op jit(solution)/shard_map/ppermute | solution.py:32
  159.5 1.7 %collective-permute-done.19 = bf16[72,256]{1,0:T(8,128)(2,1)S(1)} collective-permute-done((bf16[72,256]{1,0:T(8,128)(2,1)S(1)}, bf16[72,256]{1,0:T(8,128)(2,1)S(1)}, u32[]{:S(2)}, u32[]{:S(2)}) %collective-permute-start.19) | collective-permute-done | bytes 36896 | tf_op jit(solution)/shard_map/ppermute | solution.py:32
  161.9 2.5 %collective-permute-done.24 = bf16[72,256]{1,0:T(8,128)(2,1)S(1)} collective-permute-done((bf16[72,256]{1,0:T(8,128)(2,1)S(1)}, bf16[72,256]{1,0:T(8,128)(2,1)S(1)}, u32[]{:S(2)}, u32[]{:S(2)}) %collective-permute-start.24) | collective-permute-done | bytes 36896 | tf_op jit(solution)/shard_map/ppermute | solution.py:32
  (165 shorter events, 48.5 us)
Async XLA Ops:
  2.0 9.4 %collective-permute-start = (bf16[17,256]{1,0:T(8,128)(2,1)S(1)}, bf16[17,256]{1,0:T(8,128)(2,1)S(1)}, u32[]{:S(2)}, u32[]{:S(2)}) collective-permute-start(bf16[17,256]{1,0:T(8,128)(2,1)S(1)} %fusion.22), channel_id=1, source_target_pairs={{0,8},{1,9},{2,10},{3,11},{4,12},{5,13},{6,14},{7,15},{8,0},{9,1},... | collective-permute-start | bytes 26120 | tf_op jit(solution)/shard_map/ppermute | solution.py:32
  6.8 17.1 %collective-permute-start.10 = (bf16[72,256]{1,0:T(8,128)(2,1)S(1)}, bf16[72,256]{1,0:T(8,128)(2,1)S(1)}, u32[]{:S(2)}, u32[]{:S(2)}) collective-permute-start(bf16[72,256]{1,0:T(8,128)(2,1)S(1)} %broadcast_in_dim.329), channel_id=1, source_target_pairs={{0,8},{1,9},{2,10},{3,11},{4,12},{5,13},{6,14},{7,15},{8,0},{9,1},... | collective-permute-start | bytes 110600 | tf_op jit(solution)/shard_map/ppermute | solution.py:32
  7.7 16.2 %collective-permute-start.5 = (bf16[72,256]{1,0:T(8,128)(2,1)S(1)}, bf16[72,256]{1,0:T(8,128)(2,1)S(1)}, u32[]{:S(2)}, u32[]{:S(2)}) collective-permute-start(bf16[72,256]{1,0:T(8,128)(2,1)S(1)} %broadcast_in_dim.311), channel_id=1, source_target_pairs={{0,8},{1,9},{2,10},{3,11},{4,12},{5,13},{6,14},{7,15},{8,0},{9,1},... | collective-permute-start | bytes 110600 | tf_op jit(solution)/shard_map/ppermute | solution.py:32
  11.5 10.8 %collective-permute-start.1 = (bf16[2,17,256]{2,1,0:T(8,128)(2,1)S(1)}, bf16[2,17,256]{2,1,0:T(8,128)(2,1)S(1)}, u32[]{:S(2)}, u32[]{:S(2)}) collective-permute-start(bf16[2,17,256]{2,1,0:T(8,128)(2,1)S(1)} %broadcast_select_fusion.12), channel_id=1, source_target_pairs={{0,4},{1,5},{2,6},{3,7},{4,0},{5,1},{6,2},{7,3},{8,12},{9,13},{10,... | collective-permute-start | bytes 52232 | tf_op jit(solution)/shard_map/ppermute | solution.py:32
  24.0 4.4 %collective-permute-start.11 = (bf16[2,72,256]{2,1,0:T(8,128)(2,1)S(1)}, bf16[2,72,256]{2,1,0:T(8,128)(2,1)S(1)}, u32[]{:S(2)}, u32[]{:S(2)}) collective-permute-start(bf16[2,72,256]{2,1,0:T(8,128)(2,1)S(1)} %get-tuple-element.47), channel_id=1, source_target_pairs={{0,4},{1,5},{2,6},{3,7},{4,0},{5,1},{6,2},{7,3},{8,12},{9,13},{10,... | collective-permute-start | bytes 221192 | tf_op jit(solution)/shard_map/ppermute | solution.py:32
  24.5 4.7 %collective-permute-start.6 = (bf16[2,72,256]{2,1,0:T(8,128)(2,1)S(1)}, bf16[2,72,256]{2,1,0:T(8,128)(2,1)S(1)}, u32[]{:S(2)}, u32[]{:S(2)}) collective-permute-start(bf16[2,72,256]{2,1,0:T(8,128)(2,1)S(1)} %get-tuple-element.48), channel_id=1, source_target_pairs={{0,4},{1,5},{2,6},{3,7},{4,0},{5,1},{6,2},{7,3},{8,12},{9,13},{10,... | collective-permute-start | bytes 221192 | tf_op jit(solution)/shard_map/ppermute | solution.py:32
  26.6 5.7 %collective-permute-start.3 = (bf16[2,2,2,17,256]{4,3,0,1,2:T(8,128)(2,1)S(1)}, bf16[2,2,2,17,256]{4,3,0,1,2:T(8,128)(2,1)S(1)}, u32[]{:S(2)}, u32[]{:S(2)}) collective-permute-start(bf16[2,2,2,17,256]{4,3,0,1,2:T(8,128)(2,1)S(1)} %broadcast_select_fusion.8), channel_id=1, source_target_pairs={{0,16},{1,3},{2,18},{3,1},{4,20},{5,7},{6,22},{7,5},{8,24},{9,11},... | collective-permute-start | bytes 208904 | tf_op jit(solution)/shard_map/ppermute | solution.py:36
  29.3 5.2 %collective-permute-start.12 = (bf16[2,2,72,256]{3,2,1,0:T(8,128)(2,1)S(1)}, bf16[2,2,72,256]{3,2,1,0:T(8,128)(2,1)S(1)}, u32[]{:S(2)}, u32[]{:S(2)}) collective-permute-start(bf16[2,2,72,256]{3,2,1,0:T(8,128)(2,1)S(1)} %get-tuple-element.45), channel_id=1, source_target_pairs={{0,2},{1,17},{2,0},{3,19},{4,6},{5,21},{6,4},{7,23},{8,10},{9,25},... | collective-permute-start | bytes 442376 | tf_op jit(solution)/shard_map/ppermute | solution.py:36
  29.9 6.2 %collective-permute-start.7 = (bf16[2,2,72,256]{3,2,1,0:T(8,128)(2,1)S(1)}, bf16[2,2,72,256]{3,2,1,0:T(8,128)(2,1)S(1)}, u32[]{:S(2)}, u32[]{:S(2)}) collective-permute-start(bf16[2,2,72,256]{3,2,1,0:T(8,128)(2,1)S(1)} %get-tuple-element.46), channel_id=1, source_target_pairs={{0,2},{1,17},{2,0},{3,19},{4,6},{5,21},{6,4},{7,23},{8,10},{9,25},... | collective-permute-start | bytes 442376 | tf_op jit(solution)/shard_map/ppermute | solution.py:36
  32.6 5.9 %collective-permute-start.4 = (bf16[2,2,2,2,17,256]{5,4,1,2,0,3:T(8,128)(2,1)S(1)}, bf16[2,2,2,2,17,256]{5,4,1,2,0,3:T(8,128)(2,1)S(1)}, u32[]{:S(2)}, u32[]{:S(2)}) collective-permute-start(bf16[2,2,2,2,17,256]{5,4,1,2,0,3:T(8,128)(2,1)S(1)} %select_select_fusion.2), channel_id=1, source_target_pairs={{0,1},{1,0},{2,3},{3,2},{4,5},{5,4},{6,7},{7,6},{8,9},{9,8},{10,11... | collective-permute-start | bytes 417800 | tf_op jit(solution)/shard_map/ppermute | solution.py:32
  36.2 6.8 %collective-permute-start.13 = (bf16[2,2,2,72,256]{4,3,1,0,2:T(8,128)(2,1)S(1)}, bf16[2,2,2,72,256]{4,3,1,0,2:T(8,128)(2,1)S(1)}, u32[]{:S(2)}, u32[]{:S(2)}) collective-permute-start(bf16[2,2,2,72,256]{4,3,1,0,2:T(8,128)(2,1)S(1)} %get-tuple-element.43), channel_id=1, source_target_pairs={{0,16},{1,3},{2,18},{3,1},{4,20},{5,7},{6,22},{7,5},{8,24},{9,11},... | collective-permute-start | bytes 884744 | tf_op jit(solution)/shard_map/ppermute | solution.py:36
  37.8 8.4 %collective-permute-start.8 = (bf16[2,2,2,72,256]{4,3,1,0,2:T(8,128)(2,1)S(1)}, bf16[2,2,2,72,256]{4,3,1,0,2:T(8,128)(2,1)S(1)}, u32[]{:S(2)}, u32[]{:S(2)}) collective-permute-start(bf16[2,2,2,72,256]{4,3,1,0,2:T(8,128)(2,1)S(1)} %get-tuple-element.44), channel_id=1, source_target_pairs={{0,16},{1,3},{2,18},{3,1},{4,20},{5,7},{6,22},{7,5},{8,24},{9,11},... | collective-permute-start | bytes 884744 | tf_op jit(solution)/shard_map/ppermute | solution.py:36
  113.6 8.7 %collective-permute-start.26 = (bf16[2,2,2,17,256]{4,3,1,2,0:T(8,128)(2,1)S(1)}, bf16[2,2,2,17,256]{4,3,1,2,0:T(8,128)(2,1)S(1)}, u32[]{:S(2)}, u32[]{:S(2)}) collective-permute-start(bf16[2,2,2,17,256]{4,3,1,2,0:T(8,128)(2,1)S(1)} %fusion.12), channel_id=1, source_target_pairs={{0,2},{1,17},{2,0},{3,19},{4,6},{5,21},{6,4},{7,23},{8,10},{9,25},... | collective-permute-start | bytes 208904 | tf_op jit(solution)/shard_map/ppermute | solution.py:36
  127.8 8.4 %collective-permute-start.15 = (bf16[2,2,2,2,72,256]{5,4,3,2,1,0:T(8,128)(2,1)S(1)}, bf16[2,2,2,2,72,256]{5,4,3,2,1,0:T(8,128)(2,1)S(1)}, u32[]{:S(2)}, u32[]{:S(2)}) collective-permute-start(bf16[2,2,2,2,72,256]{5,4,3,2,1,0:T(8,128)(2,1)S(1)} %fusion), channel_id=1, source_target_pairs={{0,1},{1,0},{2,3},{3,2},{4,5},{5,4},{6,7},{7,6},{8,9},{9,8},{10,11... | collective-permute-start | bytes 1769480 | tf_op jit(solution)/shard_map/ppermute | solution.py:32
  130.4 4.7 %collective-permute-start.29 = (bf16[17,256]{1,0:T(8,128)(2,1)S(1)}, bf16[17,256]{1,0:T(8,128)(2,1)S(1)}, u32[]{:S(2)}, u32[]{:S(2)}) collective-permute-start(bf16[17,256]{1,0:T(8,128)(2,1)S(1)} %fusion.23), channel_id=1, source_target_pairs={{0,8},{1,9},{2,10},{3,11},{4,12},{5,13},{6,14},{7,15},{8,0},{9,1},... | collective-permute-start | bytes 26120 | tf_op jit(solution)/shard_map/ppermute | solution.py:32
  130.9 7.2 %collective-permute-start.20 = (bf16[2,2,2,2,72,256]{5,4,0,2,1,3:T(8,128)(2,1)S(1)}, bf16[2,2,2,2,72,256]{5,4,0,2,1,3:T(8,128)(2,1)S(1)}, u32[]{:S(2)}, u32[]{:S(2)}) collective-permute-start(bf16[2,2,2,2,72,256]{5,4,0,2,1,3:T(8,128)(2,1)S(1)} %fusion.1), channel_id=1, source_target_pairs={{0,1},{1,0},{2,3},{3,2},{4,5},{5,4},{6,7},{7,6},{8,9},{9,8},{10,11... | collective-permute-start | bytes 1769480 | tf_op jit(solution)/shard_map/ppermute | solution.py:32
  136.5 7.4 %collective-permute-start.16 = (bf16[2,2,2,72,256]{4,3,2,1,0:T(8,128)(2,1)S(1)}, bf16[2,2,2,72,256]{4,3,2,1,0:T(8,128)(2,1)S(1)}, u32[]{:S(2)}, u32[]{:S(2)}) collective-permute-start(bf16[2,2,2,72,256]{4,3,2,1,0:T(8,128)(2,1)S(1)} %fusion.7), channel_id=1, source_target_pairs={{0,2},{1,17},{2,0},{3,19},{4,6},{5,21},{6,4},{7,23},{8,10},{9,25},... | collective-permute-start | bytes 884744 | tf_op jit(solution)/shard_map/ppermute | solution.py:36
  138.3 11.3 %collective-permute-start.21 = (bf16[2,2,2,72,256]{4,3,2,1,0:T(8,128)(2,1)S(1)}, bf16[2,2,2,72,256]{4,3,2,1,0:T(8,128)(2,1)S(1)}, u32[]{:S(2)}, u32[]{:S(2)}) collective-permute-start(bf16[2,2,2,72,256]{4,3,2,1,0:T(8,128)(2,1)S(1)} %fusion.8), channel_id=1, source_target_pairs={{0,2},{1,17},{2,0},{3,19},{4,6},{5,21},{6,4},{7,23},{8,10},{9,25},... | collective-permute-start | bytes 884744 | tf_op jit(solution)/shard_map/ppermute | solution.py:36
  144.1 7.2 %collective-permute-start.17 = (bf16[2,2,72,256]{3,2,1,0:T(8,128)(2,1)S(1)}, bf16[2,2,72,256]{3,2,1,0:T(8,128)(2,1)S(1)}, u32[]{:S(2)}, u32[]{:S(2)}) collective-permute-start(bf16[2,2,72,256]{3,2,1,0:T(8,128)(2,1)S(1)} %fusion.10), channel_id=1, source_target_pairs={{0,16},{1,3},{2,18},{3,1},{4,20},{5,7},{6,22},{7,5},{8,24},{9,11},... | collective-permute-start | bytes 442376 | tf_op jit(solution)/shard_map/ppermute | solution.py:36
  149.7 5.2 %collective-permute-start.22 = (bf16[2,2,72,256]{3,2,1,0:T(8,128)(2,1)S(1)}, bf16[2,2,72,256]{3,2,1,0:T(8,128)(2,1)S(1)}, u32[]{:S(2)}, u32[]{:S(2)}) collective-permute-start(bf16[2,2,72,256]{3,2,1,0:T(8,128)(2,1)S(1)} %fusion.11), channel_id=1, source_target_pairs={{0,16},{1,3},{2,18},{3,1},{4,20},{5,7},{6,22},{7,5},{8,24},{9,11},... | collective-permute-start | bytes 442376 | tf_op jit(solution)/shard_map/ppermute | solution.py:36
  151.3 4.9 %collective-permute-start.18 = (bf16[2,72,256]{2,1,0:T(8,128)(2,1)S(1)}, bf16[2,72,256]{2,1,0:T(8,128)(2,1)S(1)}, u32[]{:S(2)}, u32[]{:S(2)}) collective-permute-start(bf16[2,72,256]{2,1,0:T(8,128)(2,1)S(1)} %fusion.13), channel_id=1, source_target_pairs={{0,4},{1,5},{2,6},{3,7},{4,0},{5,1},{6,2},{7,3},{8,12},{9,13},{10,... | collective-permute-start | bytes 221192 | tf_op jit(solution)/shard_map/ppermute | solution.py:32
  155.0 4.4 %collective-permute-start.23 = (bf16[2,72,256]{2,1,0:T(8,128)(2,1)S(1)}, bf16[2,72,256]{2,1,0:T(8,128)(2,1)S(1)}, u32[]{:S(2)}, u32[]{:S(2)}) collective-permute-start(bf16[2,72,256]{2,1,0:T(8,128)(2,1)S(1)} %fusion.14), channel_id=1, source_target_pairs={{0,4},{1,5},{2,6},{3,7},{4,0},{5,1},{6,2},{7,3},{8,12},{9,13},{10,... | collective-permute-start | bytes 221192 | tf_op jit(solution)/shard_map/ppermute | solution.py:32
  156.3 4.9 %collective-permute-start.19 = (bf16[72,256]{1,0:T(8,128)(2,1)S(1)}, bf16[72,256]{1,0:T(8,128)(2,1)S(1)}, u32[]{:S(2)}, u32[]{:S(2)}) collective-permute-start(bf16[72,256]{1,0:T(8,128)(2,1)S(1)} %fusion.18), channel_id=1, source_target_pairs={{0,8},{1,9},{2,10},{3,11},{4,12},{5,13},{6,14},{7,15},{8,0},{9,1},... | collective-permute-start | bytes 110600 | tf_op jit(solution)/shard_map/ppermute | solution.py:32
  159.5 4.9 %collective-permute-start.24 = (bf16[72,256]{1,0:T(8,128)(2,1)S(1)}, bf16[72,256]{1,0:T(8,128)(2,1)S(1)}, u32[]{:S(2)}, u32[]{:S(2)}) collective-permute-start(bf16[72,256]{1,0:T(8,128)(2,1)S(1)} %fusion.19), channel_id=1, source_target_pairs={{0,8},{1,9},{2,10},{3,11},{4,12},{5,13},{6,14},{7,15},{8,0},{9,1},... | collective-permute-start | bytes 110600 | tf_op jit(solution)/shard_map/ppermute | solution.py:32
  (25 other events, 123.6 us)
where the time goes:
time: 166 us; the launch traced here: 165 us
  Pallas kernels  66 us (40%)
  waiting for transfers between devices  41.3 us (25%)
  starting transfers between devices  31.5 us (19%)
  local copies, waits for them, and re-layouts  17.1 us (10%)
  other arithmetic  6.99 us (4%)
    pallas_call x6, Pallas kernels, call(): pl.pallas_call(body, out_shape=[jax.ShapeDtypeStruct(shape, dtype) for sh...  66 us
    ppermute x12, waiting for transfers between devices, swap_cross(): lax.ppermute(value, AXES, [(i, i ^ 1 << (odd if i & 1 else even)) for i i...  23.7 us
    ppermute x18, waiting for transfers between devices, swap(): return lax.ppermute(value, AXES, [(i, i ^ 1 << b) for i in range(self.n)])  17.6 us
    ppermute x18, starting transfers between devices, swap(): return lax.ppermute(value, AXES, [(i, i ^ 1 << b) for i in range(self.n)])  16.2 us
    ppermute x12, starting transfers between devices, swap_cross(): lax.ppermute(value, AXES, [(i, i ^ 1 << (odd if i & 1 else even)) for i i...  15.3 us
    unnamed x42, local copies, waits for them, and re-layouts  11.5 us
  transfers between devices with their start and end apart: 30, of which 20 were waited for; matrix products, arithmetic and copies ran while one was open for 6% of the time, Pallas kernels for 8%

commit v1 on v0

v1 whole, which is shorter than its diff:
```python
import functools
import math

import jax
import jax.numpy as jnp
from jax import lax
from jax.experimental import pallas as pl
from jax.experimental.pallas import tpu as pltpu
from jax.sharding import PartitionSpec as P

GROUPS = 32
EPS = 1e-05
AXES = ("dp", "fsdp")
LANES = 128
VEC_ROWS = 16


class Wires:
    def __init__(self, n_dp, n_fsdp):
        self.n_fsdp = n_fsdp
        self.n = n_dp * n_fsdp
        self.bits = int(math.log2(self.n))
        fsdp_bits = int(math.log2(n_fsdp))
        assert 1 << self.bits == self.n and 1 << fsdp_bits == n_fsdp and fsdp_bits >= 2 and n_dp >= 2
        a, b = 1, fsdp_bits
        far = [bit for bit in range(self.bits - 1, 0, -1) if bit not in (a, b)]
        self.order = {0: [*far, a, b], 1: [*far, b, a]}
        self.stages = self.bits - 1
        self.slots = 1 << self.stages

    def swap(self, value, stage):
        bit = (lambda i: 0) if stage == self.stages else (lambda i: self.order[i & 1][stage])
        return lax.ppermute(value, AXES, [(i, i ^ (1 << bit(i))) for i in range(self.n)])

    def mask(self, slot, core):
        return sum(1 << self.order[core][i] for i in range(self.stages) if slot >> i & 1)

    def me(self):
        return lax.axis_index("dp") * self.n_fsdp + lax.axis_index("fsdp")

    def owner(self, slot, other, me):
        core = me & 1
        if other:
            me, core = me ^ 1, 1 - core
        return me ^ jnp.where(core == 0, self.mask(slot, 0), self.mask(slot, 1))


ROWS = 16
F32 = jnp.float32
BF16 = jnp.bfloat16
VMEM_BYTES = 14 * 1024 * 1024


def group_sum(totals):
    channels = totals.shape[1]
    lane = lax.broadcasted_iota(jnp.int32, totals.shape, 1)
    span = 1
    while span < channels // GROUPS:
        up = pltpu.roll(totals, channels - span, 1)
        down = pltpu.roll(totals, span, 1)
        totals = totals + jnp.where((lane & span) == 0, up, down)
        span *= 2
    return totals


def fold(values):
    channels = values.shape[-1]
    return jnp.sum(values.reshape(-1, 8, channels), 0)


def total(partial):
    return jnp.sum(partial, 0, keepdims=True)


def sigmoid(v):
    return 0.5 * jnp.tanh(0.5 * v) + 0.5


def clear_edges(three):
    height = three.shape[1] - 2
    zero = jnp.zeros((3, 1) + three.shape[2:], three.dtype)
    three[:, 0:1] = zero
    three[:, height + 1 : height + 2] = zero


def store_three(three, row, value):
    width = value.shape[0]
    column = lax.broadcasted_iota(jnp.int32, value.shape, 0)
    left = jnp.where(column == 0, 0.0, pltpu.roll(value, 1, 0))
    right = jnp.where(column == width - 1, 0.0, pltpu.roll(value, width - 1, 0))
    three[0, row + 1] = left.astype(three.dtype)
    three[1, row + 1] = value.astype(three.dtype)
    three[2, row + 1] = right.astype(three.dtype)


def conv_rows(three, kernel, start, back):
    width, channels = three.shape[2:]
    acc = None
    for tap in range(9):
        lhs = three[tap % 3, pl.ds(start + tap // 3, ROWS)].reshape(ROWS * width, channels)
        at = (8 - tap if back else tap) * channels
        rhs = kernel[at : at + channels, :]
        part = lax.dot_general(
            lhs, rhs, (((1,), (1 if back else 0,)), ((), ())), preferred_element_type=F32
        )
        acc = part if acc is None else acc + part
    return acc


def store_flat(flat, start, value):
    rows = value.shape[0]
    flat[pl.ds(start, rows, stride=2), :] = value[:, :LANES]
    flat[pl.ds(start + 1, rows, stride=2), :] = value[:, LANES:]


def load_flat(flat, start, rows):
    left = flat[pl.ds(start, rows, stride=2), :]
    right = flat[pl.ds(start + 1, rows, stride=2), :]
    return jnp.concatenate([left, right], axis=1)


def kernel_grad(acts, three, flat):
    height, width, channels = acts.shape

    def step(tap, _):
        row = tap // 3
        col = tap - 3 * row
        lhs = acts[...].reshape(height * width, channels)
        rhs = three[2 - col, pl.ds(2 - row, height)].reshape(height * width, channels)
        out = lax.dot_general(lhs, rhs, (((0,), (0,)), ((), ())), preferred_element_type=F32)
        store_flat(flat, pl.multiple_of(tap * 2 * channels, 2 * channels), out)
        return 0

    lax.fori_loop(0, 9, step, 0)


def prepare_kernel(x, g, stats, three, g_sum):
    height, width, channels = x.shape
    count = height * width * (channels // GROUPS)
    zero = jnp.zeros((8, channels), F32)
    clear_edges(three)

    def first(i, carry):
        s, gs = carry
        row = i * 4
        s = s + fold(x[pl.ds(row, 4)].astype(F32))
        rows = g[pl.ds(row, 4)].astype(F32)
        for j in range(4):
            store_three(three, row + j, rows[j])
        return s, gs + fold(rows)

    s, gs = lax.fori_loop(0, height // 4, first, (zero, zero))
    g_sum[...] = total(gs)
    mean = group_sum(total(s)) / count

    def second(i, v):
        d = x[pl.ds(i * 4, 4)].astype(F32) - mean
        return v + fold(d * d)

    v = lax.fori_loop(0, height // 4, second, zero)
    inv = lax.rsqrt(group_sum(total(v)) / count + EPS)
    stats[0:1, :] = mean
    stats[1:2, :] = inv


def first_kernel(x, stats, vec, q, kernel, act, centred, stats_out, three):
    height, width, channels = x.shape
    count = height * width * (channels // GROUPS)
    mean, scale, shift = stats[0:1, :], stats[1:2, :] * vec[0:1, :], vec[1:2, :]
    time = jnp.dot(q[...], kernel[9 * channels :, :], preferred_element_type=F32)
    offset = vec[2:3, :] + time
    zero = jnp.zeros((8, channels), F32)
    clear_edges(three)

    def activate(i, _):
        row = i * 4
        h = (x[pl.ds(row, 4)].astype(F32) - mean) * scale + shift
        a = h * sigmoid(h)
        act[pl.ds(row, 4)] = a.astype(BF16)
        for j in range(4):
            store_three(three, row + j, a[j])
        return 0

    lax.fori_loop(0, height // 4, activate, 0)

    def conv(i, s):
        row = pl.multiple_of(i * ROWS, ROWS)
        acc = conv_rows(three, kernel, row, False)
        centred[pl.ds(row * width, ROWS * width), :] = acc
        return s + fold(acc)

    s = lax.fori_loop(0, height // ROWS, conv, zero)
    mean_two = group_sum(total(s) / (height * width) + offset) / (channels // GROUPS)
    move = offset - mean_two

    def centre(i, v):
        at = pl.ds(i * 256, 256)
        d = centred[at, :] + move
        centred[at, :] = d
        return v + fold(d * d)

    v = lax.fori_loop(0, height * width // 256, centre, zero)
    stats_out[...] = lax.rsqrt(group_sum(total(v)) / count + EPS)


def second_kernel(three, centred, inv, vec, kernel, dh, act, sums, grad):
    height, width, channels = act.shape
    scale, shift = inv[...] * vec[3:4, :], vec[4:5, :]
    zero = jnp.zeros((8, channels), F32)

    def conv(i, carry):
        s, sc = carry
        row = pl.multiple_of(i * ROWS, ROWS)
        at = pl.ds(row * width, ROWS * width)
        acc = conv_rows(three, kernel, row, True)
        c = centred[at, :]
        h = c * scale + shift
        sig = sigmoid(h)
        a = h * sig
        act[pl.ds(row, ROWS)] = a.astype(BF16).reshape(ROWS, width, channels)
        d = acc * (sig + a * (1.0 - sig))
        dh[at, :] = d
        return s + fold(d), sc + fold(d * c)

    s, sc = lax.fori_loop(0, height // ROWS, conv, (zero, zero))
    sums[0:1, :] = total(sc) * inv[...]
    sums[1:2, :] = total(s)
    kernel_grad(act, three, grad)


def middle_kernel(dh_two, centred, inv_two, sums_two, x, stats, vec, kernel, three, dc_sum, dq, dh, sums):
    height, width, channels = x.shape
    count = height * width * (channels // GROUPS)
    gain = vec[3:4, :]
    inv = inv_two[...]
    scale = inv * gain
    base = inv * (group_sum(sums_two[1:2, :] * gain) / count)
    slope = inv * inv * (group_sum(sums_two[0:1, :] * gain) / count)
    zero = jnp.zeros((8, channels), F32)
    clear_edges(three)

    def back(i, s):
        row = i * 4
        at = pl.ds(row * width, 4 * width)
        d = dh_two[at, :] * scale - base - centred[at, :] * slope
        rows = d.reshape(4, width, channels)
        for j in range(4):
            store_three(three, row + j, rows[j])
        return s + fold(d)

    dc = total(lax.fori_loop(0, height // 4, back, zero))
    dc_sum[...] = dc
    dq[...] = lax.dot_general(
        dc,
        kernel[9 * channels :, :].astype(F32),
        (((1,), (1,)), ((), ())),
        precision=lax.Precision.HIGHEST,
        preferred_element_type=F32,
    )
    mean, scale, shift = stats[0:1, :], stats[1:2, :] * vec[0:1, :], vec[1:2, :]

    def conv(i, carry):
        s, sn = carry
        row = pl.multiple_of(i * ROWS, ROWS)
        acc = conv_rows(three, kernel, row, True)
        c = x[pl.ds(row, ROWS)].astype(F32).reshape(ROWS * width, channels) - mean
        h = c * scale + shift
        sig = sigmoid(h)
        d = acc * (sig + h * sig * (1.0 - sig))
        dh[pl.ds(row * width, ROWS * width), :] = d
        return s + fold(d), sn + fold(d * c)

    s, sn = lax.fori_loop(0, height // ROWS, conv, (zero, zero))
    sums[0:1, :] = total(sn) * stats[1:2, :]
    sums[1:2, :] = total(s)


def input_kernel(dh, x, g, stats, sums, vec, result, done):
    height, width, channels = x.shape
    count = height * width * (channels // GROUPS)
    mean, inv, gain = stats[0:1, :], stats[1:2, :], vec[0:1, :]
    scale = inv * gain
    base = inv * (group_sum(sums[1:2, :] * gain) / count)
    slope = inv * inv * (group_sum(sums[0:1, :] * gain) / count)

    def back(i, _):
        row = i * 4
        d = dh[pl.ds(row * width, 4 * width), :].reshape(4, width, channels)
        c = x[pl.ds(row, 4)].astype(F32) - mean
        result[pl.ds(row, 4)] = g[pl.ds(row, 4)].astype(F32) + (d * scale - base - c * slope)
        return 0

    lax.fori_loop(0, height // 4, back, 0)
    done[...] = base


def last_kernel(act, x, vec, kernel, result, done, three):
    height, width, channels = x.shape
    bias = vec[5:6, :]
    clear_edges(three)

    def spread(i, _):
        rows = act[pl.ds(i * 4, 4)].astype(F32)
        for j in range(4):
            store_three(three, i * 4 + j, rows[j])
        return 0

    lax.fori_loop(0, height // 4, spread, 0)

    def conv(i, _):
        row = pl.multiple_of(i * ROWS, ROWS)
        acc = conv_rows(three, kernel, row, False).reshape(ROWS, width, channels)
        result[pl.ds(row, ROWS)] = (x[pl.ds(row, ROWS)].astype(F32) + acc + bias).astype(BF16)
        return 0

    lax.fori_loop(0, height // ROWS, conv, 0)
    done[...] = bias


def join_kernel(mine, got, out):
    rows = mine.shape[0] - VEC_ROWS
    out[0:rows, :] = mine[0:rows, :]
    out[rows : 2 * rows, :] = got[0:rows, :]
    out[2 * rows : 2 * rows + VEC_ROWS, :] = mine[rows : rows + VEC_ROWS, :] + got[rows : rows + VEC_ROWS, :]


def halve_kernel(keep, got, send_next, keep_next):
    rows = (keep.shape[0] - VEC_ROWS) // 2
    keep_next[0:rows, :] = keep[0:rows, :] + got[0:rows, :].astype(F32)
    send_next[0:rows, :] = (keep[rows : 2 * rows, :] + got[rows : 2 * rows, :].astype(F32)).astype(BF16)
    vec = keep[2 * rows : 2 * rows + VEC_ROWS, :] + got[2 * rows : 2 * rows + VEC_ROWS, :].astype(F32)
    keep_next[rows : rows + VEC_ROWS, :] = vec
    send_next[rows : rows + VEC_ROWS, :] = vec.astype(BF16)


def arrange_kernel(wires, cuts, mine, got, first, kernel_two, vec, flat_one, flat_two, flat_project, flat_vec):
    me = wires.me()
    block = sum(cuts)
    flats = (flat_one, flat_two, flat_project)
    for slot in range(wires.slots):
        for other, source in ((False, mine), (True, got)):
            owner = wires.owner(slot, other, me)
            values = source[slot * block : (slot + 1) * block, :].astype(F32)
            at = 0
            for flat, rows in zip(flats, cuts):
                flat[pl.ds(pl.multiple_of(owner * rows, rows), rows), :] = values[at : at + rows]
                at += rows
    rows_one = flat_one.shape[0] // 2
    for flat, out, base in ((flat_one, first, 0), (flat_two, kernel_two, 0), (flat_project, first, rows_one)):
        for start in range(0, flat.shape[0] // 2, 256):
            out[base + start : base + start + 256, :] = load_flat(flat, 2 * start, 256).astype(BF16)
    at = wires.slots * block
    flat_vec[...] = mine[at : at + VEC_ROWS, :].astype(F32) + got[at : at + VEC_ROWS, :].astype(F32)
    vec[...] = load_flat(flat_vec, 0, VEC_ROWS // 2)


def pack_kernel(wires, cuts, act, three, flat_two, q, dc_sum, sums_one, sums_two, g_sum, send, keep, flat_one, flat_project):
    me = wires.me()
    block = sum(cuts)
    kernel_grad(act, three, flat_one)
    for start in range(0, q.shape[0], 256):
        store_flat(flat_project, 2 * start, q[start : start + 256, :] * dc_sum[...])
    for slot in range(wires.slots):
        for other in (True, False):
            owner = wires.owner(slot, other, me)
            at = slot * block
            for flat, rows in zip((flat_one, flat_two, flat_project), cuts):
                values = flat[pl.ds(pl.multiple_of(owner * rows, rows), rows), :]
                if other:
                    send[at : at + rows, :] = values.astype(BF16)
                else:
                    keep[at : at + rows, :] = values
                at += rows
    at = wires.slots * block
    vectors = [sums_one[0:1, :], sums_one[1:2, :], dc_sum[...], sums_two[0:1, :], sums_two[1:2, :], g_sum[...]]
    halves = [row[:, i * LANES : (i + 1) * LANES] for row in vectors for i in range(2)]
    values = jnp.concatenate(halves + [jnp.zeros((VEC_ROWS - len(halves), LANES), F32)], axis=0)
    keep[at : at + VEC_ROWS, :] = values
    send[at : at + VEC_ROWS, :] = values.astype(BF16)


def finish_kernel(wires, cuts, n_vec, keep, got, one, two, project, vec):
    at = 0
    for out, rows in zip((one, two, project), cuts):
        out[...] = keep[at : at + rows, :] + got[at : at + rows, :].astype(F32)
        at += rows
    vectors = keep[at : at + VEC_ROWS, :] + got[at : at + VEC_ROWS, :].astype(F32)
    start = wires.me() * n_vec
    row, lane = start // LANES, start % LANES
    place = lax.broadcasted_iota(jnp.int32, vectors.shape, 0)
    own = jnp.sum(jnp.where(place == row, vectors, 0.0), 0, keepdims=True)
    following = jnp.sum(jnp.where(place == row + 1, vectors, 0.0), 0, keepdims=True)
    column = lax.broadcasted_iota(jnp.int32, own.shape, 1)
    shifted = pltpu.roll(jnp.where(column >= lane, own, following), (LANES - lane) % LANES, 1)
    vec[...] = shifted[:, :n_vec]


def call(body, outs, *args, scratch=(), flops=0, size=4 << 20, after=()):
    held, n_in = len(after), len(args)

    def run(*refs):
        body(*refs[:n_in], *refs[n_in + held :])

    return pl.pallas_call(
        run,
        out_shape=[jax.ShapeDtypeStruct(shape, dtype) for shape, dtype in outs],
        in_specs=[pl.BlockSpec(memory_space=pltpu.VMEM)] * n_in + [pl.BlockSpec(memory_space=pl.ANY)] * held,
        scratch_shapes=[pltpu.VMEM(shape, dtype) for shape, dtype in scratch],
        compiler_params=pltpu.CompilerParams(vmem_limit_bytes=VMEM_BYTES),
        cost_estimate=pl.CostEstimate(flops=flops, bytes_accessed=size, transcendentals=0),
    )(*args, *after)


def gather(wires, cuts, parts, vectors, beside):
    block = sum(cuts)
    n_vec = vectors.shape[0]
    me = wires.me()
    wide = VEC_ROWS * LANES
    placed = lax.dynamic_slice(jnp.pad(vectors, (wide, wide - n_vec)), (wide - me * n_vec,), (wide,))
    held = jnp.concatenate([v.reshape(-1, LANES) for v in (*parts, placed)], axis=0)
    for stage in range(wires.stages):
        got = wires.swap(held, stage)
        shape = (2 * (held.shape[0] - VEC_ROWS) + VEC_ROWS, LANES)
        after = beside.get(stage, ())
        held, = call(join_kernel, [(shape, BF16)], held, got, size=4 * LANES * shape[0], after=after)
    got = wires.swap(held, wires.stages)
    channels = 2 * LANES
    totals = [wires.n * rows for rows in cuts]
    outs = [((rows // 2, channels), BF16) for rows in (totals[0] + totals[2], totals[1])]
    if all(rows % 8 == 0 for rows in cuts):
        return call(
            functools.partial(arrange_kernel, wires, cuts),
            [*outs, ((VEC_ROWS // 2, channels), F32)],
            held,
            got,
            scratch=[((rows, LANES), F32) for rows in (*totals, VEC_ROWS)],
        )
    rows = wires.slots * block
    both = jnp.concatenate([held[:rows], got[:rows]]).reshape(wires.n, block, LANES)
    owners = jnp.stack([wires.owner(j, other, me) for other in (False, True) for j in range(wires.slots)])
    both = jnp.zeros_like(both).at[owners].set(both)
    at, whole = 0, []
    for cut in cuts:
        whole.append(both[:, at : at + cut].reshape(-1, channels))
        at += cut
    vec = (held[rows:].astype(F32) + got[rows:].astype(F32)).reshape(VEC_ROWS // 2, channels)
    return jnp.concatenate([whole[0], whole[2]]), whole[1], vec


def pack(wires, cuts, act, three, flat_two, q, dc_sum, sums_one, sums_two, g_sum):
    block = sum(cuts)
    shape = (wires.slots * block + VEC_ROWS, LANES)
    totals = [wires.n * rows for rows in cuts]
    if all(rows % 8 == 0 for rows in cuts):
        return call(
            functools.partial(pack_kernel, wires, cuts),
            [(shape, BF16), (shape, F32)],
            act,
            three,
            flat_two,
            q,
            dc_sum,
            sums_one,
            sums_two,
            g_sum,
            scratch=[((totals[0], LANES), F32), ((totals[2], LANES), F32)],
            flops=2 * 9 * act.size * act.shape[-1],
        )
    flat_one, = call(kernel_grad, [((totals[0], LANES), F32)], act, three, flops=2 * 9 * act.size * act.shape[-1])
    flats = (flat_one, flat_two, (q * dc_sum).reshape(-1, LANES))
    blocks = jnp.concatenate([f.reshape(wires.n, rows, LANES) for f, rows in zip(flats, cuts)], axis=1)
    me = wires.me()
    vec = jnp.concatenate([sums_one, dc_sum, sums_two, g_sum]).reshape(-1, LANES)
    vec = jnp.pad(vec, ((0, VEC_ROWS - vec.shape[0]), (0, 0)))
    halves = []
    for other in (True, False):
        owners = jnp.stack([wires.owner(j, other, me) for j in range(wires.slots)])
        halves.append(jnp.concatenate([blocks[owners].reshape(-1, LANES), vec]))
    return halves[0].astype(BF16), halves[1]


def reduce_scatter(wires, cuts, n_vec, send, keep, beside):
    for stage in range(wires.stages, 0, -1):
        got = wires.swap(send, stage)
        shape = ((keep.shape[0] - VEC_ROWS) // 2 + VEC_ROWS, LANES)
        send, keep = call(halve_kernel, [(shape, BF16), (shape, F32)], keep, got, size=12 * LANES * shape[0], after=beside.get(stage, ()))
    got = wires.swap(send, 0)
    return call(
        functools.partial(finish_kernel, wires, cuts, n_vec),
        [*[((rows, LANES), F32) for rows in cuts], ((1, n_vec), F32)],
        keep,
        got,
        size=12 * LANES * keep.shape[0],
    )


def swish_slope(values):
    sigma = jax.nn.sigmoid(values)
    return sigma * (1.0 + values * (1.0 - sigma))


def local(sizes, images, embedding, conv_first, conv_second, projection, vectors, cotangent):
    count, height, width, channels = images.shape
    emb_width = embedding.shape[-1]
    wires = Wires(*sizes)
    n_vec = vectors.shape[0]
    assert count == 1 and channels == 2 * LANES and n_vec <= LANES
    cuts = [v.shape[0] // LANES for v in (conv_first, conv_second, projection)]
    pixels = height * width
    three = ((3, height + 2, width, channels), BF16)
    maps = ((height, width, channels), BF16)
    flat = ((pixels, channels), F32)
    line = ((1, channels), F32)
    pair = ((2, channels), F32)
    taps = ((18 * channels, LANES), F32)
    conv_flops = 2 * 9 * pixels * channels * channels

    x, g = images[0], cotangent[0]
    stats, g_three, g_sum = call(prepare_kernel, [pair, three, line], x, g)
    first, kernel_two, vec = gather(
        wires, cuts, (conv_first, conv_second, projection), vectors, {wires.stages - 1: (g_sum,)}
    )

    emb_float = embedding.astype(F32)
    emb_act = jax.nn.silu(emb_float).astype(BF16)
    q = emb_act.astype(F32).reshape(emb_width, 1)
    act_one, centred, inv_two = call(
        first_kernel, [maps, flat, line], x, stats, vec, emb_act, first, scratch=[three], flops=conv_flops
    )
    dh_two, act_two, sums_two, grad_two = call(
        second_kernel,
        [flat, maps, pair, taps],
        g_three,
        centred,
        inv_two,
        vec,
        kernel_two,
        flops=2 * conv_flops,
    )
    e_three, dc_sum, dq, dh_one, sums_one = call(
        middle_kernel,
        [three, line, ((1, emb_width), F32), flat, pair],
        dh_two,
        centred,
        inv_two,
        sums_two,
        x,
        stats,
        vec,
        first,
        flops=conv_flops,
    )
    send, keep = pack(wires, cuts, act_one, e_three, grad_two, q, dc_sum, sums_one, sums_two, g_sum)
    input_grad, input_done = call(input_kernel, [(maps[0], F32), line], dh_one, x, g, stats, sums_one, vec)
    output, output_done = call(last_kernel, [maps, line], act_two, x, vec, kernel_two, scratch=[three], flops=conv_flops)
    beside = {wires.stages - 1: (output_done,), wires.stages - 2: (input_done,)}
    summed = reduce_scatter(wires, cuts, n_vec, send, keep, beside)
    embedding_grad = dq * swish_slope(emb_float)
    return (output[None], input_grad[None], embedding_grad, *[v.reshape(-1) for v in summed])


def solution(mesh):
    sizes = (mesh.shape["dp"], mesh.shape["fsdp"])
    split = P(AXES)
    maps = P(AXES, None, None, None)
    in_specs = (maps, P(AXES, None), split, split, split, split, maps)
    out_specs = (maps, maps, P(AXES, None), split, split, split, split)

    def body(*args):
        return local(sizes, *args)

    return jax.shard_map(body, mesh=mesh, in_specs=in_specs, out_specs=out_specs, check_vma=False)
```

time: 166 us -> 112 us (0.67)
  starting transfers between devices: 31.5 us -> 16.9 us
  local copies, waits for them, and re-layouts: 17.1 us -> 6.1 us
  waiting for transfers between devices: 41.3 us -> 30.3 us
  Pallas kernels: 66 us -> 56.3 us
  other arithmetic: 6.99 us -> 1.41 us
    ppermute x30 -> x10, starting transfers between devices: 31.5 us -> 16.9 us  [swap(): lax.ppermute(value, AXES, [(i, i ^ 1 << bit(i)) for i in range(self.n)])]
    ppermute x30 -> x10, waiting for transfers between devices: 41.3 us -> 30.3 us  [swap(): lax.ppermute(value, AXES, [(i, i ^ 1 << bit(i)) for i in range(self.n)])]
    pallas_call x6 -> x17, Pallas kernels: 66 us -> 56.3 us  [call(): pl.pallas_call(run, out_shape=[jax.ShapeDtypeStruct(shape, dtype) for sha...]
    unnamed x42 -> x16, local copies, waits for them, and re-layouts: 11.5 us -> 4.35 us
    select_n x15 -> x0, other arithmetic: 3.79 us -> none  [the longest x10 2.82 us: merge(): return jnp.where(place == bit, mine, other)]
    broadcast_in_dim x6 -> x0, local copies, waits for them, and re-layouts: 2.31 us -> none  [merge(): return jnp.where(place == bit, mine, other)]
  transfers between devices with their start and end apart: 30 -> 10, of which waited for: 20 -> 10; matrix products, arithmetic and copies ran while one was open for 6% -> 1% of each run, Pallas kernels for 8% -> 12%
where the time goes in v1:
time: 112 us
  Pallas kernels  56.3 us (50%)
  waiting for transfers between devices  30.3 us (27%)
  starting transfers between devices  16.9 us (15%)
  local copies, waits for them, and re-layouts  6.1 us (5%)
  other arithmetic  1.41 us (1%)
    pallas_call x17, Pallas kernels, call(): pl.pallas_call(run, out_shape=[jax.ShapeDtypeStruct(shape, dtype) for sha...  56.3 us
    ppermute x10, waiting for transfers between devices, swap(): lax.ppermute(value, AXES, [(i, i ^ 1 << bit(i)) for i in range(self.n)])  30.3 us
    ppermute x10, starting transfers between devices, swap(): lax.ppermute(value, AXES, [(i, i ^ 1 << bit(i)) for i in range(self.n)])  16.9 us
    unnamed x16, local copies, waits for them, and re-layouts  4.35 us
  transfers between devices with their start and end apart: 10, of which 10 were waited for; matrix products, arithmetic and copies ran while one was open for 1% of the time, Pallas kernels for 12%

profile of v1, /device:TPU:0, one launch (start us, length us, event | category | flops | bytes accessed | tf_op | source)
XLA Modules:
  0.0 111.8 jit_solution(11644192887237442359)
XLA Ops:
  2.3 4.0 %collective-permute-start = (bf16[336,128]{1,0:T(8,128)(2,1)S(1)}, bf16[336,128]{1,0:T(8,128)(2,1)S(1)}, u32[]{:S(2)}, u32[]{:S(2)}) collective-permute-start(bf16[336,128]{1,0:T(8,128)(2,1)S(1)} %pad_maximum_fusion.refs_0_), channel_id=1, source_target_pairs={{0,8},{1,9},{2,10},{3,11},{4,12},{5,13},{6,14},{7,15},{8,0},{9,1},... | collective-permute-start | bytes 258056 | tf_op jit(solution)/shard_map/ppermute | solution.py:33
  6.4 4.4 %collective-permute-done.refs_1_ = bf16[336,128]{1,0:T(8,128)(2,1)S(1)} collective-permute-done((bf16[336,128]{1,0:T(8,128)(2,1)S(1)}, bf16[336,128]{1,0:T(8,128)(2,1)S(1)}, u32[]{:S(2)}, u32[]{:S(2)}) %collective-permute-start) | collective-permute-done | bytes 86048 | tf_op jit(solution)/shard_map/ppermute | solution.py:33
  11.6 4.6 %collective-permute-done.1.refs_1_ = bf16[656,128]{1,0:T(8,128)(2,1)S(1)} collective-permute-done((bf16[656,128]{1,0:T(8,128)(2,1)S(1)}, bf16[656,128]{1,0:T(8,128)(2,1)S(1)}, u32[]{:S(2)}, u32[]{:S(2)}) %collective-permute-start.1) | collective-permute-done | bytes 167968 | tf_op jit(solution)/shard_map/ppermute | solution.py:33
  16.2 1.7 %collective-permute-start.2 = (bf16[1296,128]{1,0:T(8,128)(2,1)S(1)}, bf16[1296,128]{1,0:T(8,128)(2,1)S(1)}, u32[]{:S(2)}, u32[]{:S(2)}) collective-permute-start(bf16[1296,128]{1,0:T(8,128)(2,1)S(1)} %shard_map.128.refs_0_), channel_id=1, source_target_pairs={{0,2},{1,17},{2,0},{3,19},{4,6},{5,21},{6,4},{7,23},{8,10},{9,25},... | collective-permute-start | bytes 995336 | tf_op jit(solution)/shard_map/ppermute | solution.py:33
  17.9 5.5 %collective-permute-done.2.refs_1_ = bf16[1296,128]{1,0:T(8,128)(2,1)S(1)} collective-permute-done((bf16[1296,128]{1,0:T(8,128)(2,1)S(1)}, bf16[1296,128]{1,0:T(8,128)(2,1)S(1)}, u32[]{:S(2)}, u32[]{:S(2)}) %collective-permute-start.2) | collective-permute-done | bytes 331808 | tf_op jit(solution)/shard_map/ppermute | solution.py:33
  23.5 1.9 %collective-permute-start.3 = (bf16[2576,128]{1,0:T(8,128)(2,1)S(1)}, bf16[2576,128]{1,0:T(8,128)(2,1)S(1)}, u32[]{:S(2)}, u32[]{:S(2)}) collective-permute-start(bf16[2576,128]{1,0:T(8,128)(2,1)S(1)} %shard_map.129.refs_0_), channel_id=1, source_target_pairs={{0,16},{1,3},{2,18},{3,1},{4,20},{5,7},{6,22},{7,5},{8,24},{9,11},... | collective-permute-start | bytes 1978376 | tf_op jit(solution)/shard_map/ppermute | solution.py:33
  27.0 2.6 %shard_map.126 = (f32[2,256]{1,0:T(2,128)S(1)}, bf16[3,66,64,256]{3,2,1,0:T(8,128)(2,1)S(1)}, f32[1,256]{1,0:T(1,128)S(1)}) custom-call(bf16[64,64,256]{2,1,0:T(8,128)(2,1)S(1)} %bitcast.16, bf16[64,64,256]{2,1,0:T(8,128)(2,1)S(1)} %bitcast.21), custom_call_target="tpu_custom_call" | custom-call | bytes 4194304 | tf_op jit(solution)/shard_map/pallas_call | solution.py:404
  29.6 2.7 %copy-done.4 = bf16[3,66,64,256]{3,2,1,0:T(8,128)(2,1)} copy-done((bf16[3,66,64,256]{3,2,1,0:T(8,128)(2,1)}, bf16[3,66,64,256]{3,2,1,0:T(8,128)(2,1)S(1)}, u32[]{:S(2)}) %copy-start.4) | copy-done | bytes 6488088
  32.4 1.9 %collective-permute-done.3.refs_1_ = bf16[2576,128]{1,0:T(8,128)(2,1)S(1)} collective-permute-done((bf16[2576,128]{1,0:T(8,128)(2,1)S(1)}, bf16[2576,128]{1,0:T(8,128)(2,1)S(1)}, u32[]{:S(2)}, u32[]{:S(2)}) %collective-permute-start.3) | collective-permute-done | bytes 659488 | tf_op jit(solution)/shard_map/ppermute | solution.py:33
  35.3 2.3 %collective-permute-done.4.refs_1_ = bf16[5136,128]{1,0:T(8,128)(2,1)} collective-permute-done((bf16[5136,128]{1,0:T(8,128)(2,1)S(1)}, bf16[5136,128]{1,0:T(8,128)(2,1)}, u32[]{:S(2)}, u32[]{:S(2)}) %collective-permute-start.4) | collective-permute-done | bytes 1314848 | tf_op jit(solution)/shard_map/ppermute | solution.py:33
  37.5 2.1 %shard_map.131 = (bf16[2816,256]{1,0:T(8,128)(2,1)S(1)}, bf16[2304,256]{1,0:T(8,128)(2,1)S(1)}, f32[8,256]{1,0:T(8,128)S(1)}) custom-call(bf16[5136,128]{1,0:T(8,128)(2,1)S(1)} %shard_map.130.refs_0_, bf16[5136,128]{1,0:T(8,128)(2,1)} %collective-permute-done.4.refs_1_), custom_call_target="tpu_custom_call" | custom-call | bytes 4194304 | tf_op jit(solution)/shard_map/pallas_call | solution.py:404
  39.7 8.9 %shard_map.132 = (bf16[64,64,256]{2,1,0:T(8,128)(2,1)S(1)}, f32[4096,256]{1,0:T(8,128)S(1)}, f32[1,256]{1,0:T(1,128)S(1)}) custom-call(bf16[64,64,256]{2,1,0:T(8,128)(2,1)S(1)} %bitcast.17, f32[2,256]{1,0:T(2,128)S(1)} %get-tuple-element.44.refs_1_.refs_5_.refs_3_, f32[8,256]{1,0:T(8,128)S(1)} %get-tuple-element.46.refs_2_.refs_3_.refs_6_.refs_5_, ...), custom_call_target="tpu_custom_call" | custom-call | flops 4831838208 | bytes 4194304 | tf_op jit(solution)/shard_map/pallas_call | solution.py:404
  48.6 13.4 %shard_map.133 = (f32[4096,256]{1,0:T(8,128)S(1)}, bf16[64,64,256]{2,1,0:T(8,128)(2,1)S(1)}, f32[2,256]{1,0:T(2,128)S(1)}, f32[4608,128]{1,0:T(8,128)S(1)}) custom-call(bf16[3,66,64,256]{3,2,1,0:T(8,128)(2,1)S(1)} %bitcast.24, f32[4096,256]{1,0:T(8,128)S(1)} %get-tuple-element.48.refs_1_, f32[1,256]{1,0:T(1,128)S(1)} %get-tuple-element.49.refs_2_, ...), custom_call_target="tpu_custom_call" | custom-call | flops 9663676416 | bytes 4194304 | tf_op jit(solution)/shard_map/pallas_call | solution.py:404
  62.0 9.1 %shard_map.135 = (bf16[3,66,64,256]{3,2,1,0:T(8,128)(2,1)S(1)}, f32[1,256]{1,0:T(1,128)S(1)}, f32[1,512]{1,0:T(1,128)S(1)}, f32[4096,256]{1,0:T(8,128)S(1)}, f32[2,256]{1,0:T(2,128)S(1)}) custom-call(f32[4096,256]{1,0:T(8,128)S(1)} %get-tuple-element.53.refs_0_, f32[4096,256]{1,0:T(8,128)S(1)} %get-tuple-element.48.refs_1_, ...), custom_call_target="tpu_custom_call" | custom-call | flops 4831838208 | bytes 4194304 | tf_op jit(solution)/shard_map/pallas_call | solution.py:404
  71.1 7.4 %shard_map.137 = (bf16[5136,128]{1,0:T(8,128)(2,1)S(1)}, f32[5136,128]{1,0:T(8,128)S(1)}) custom-call(bf16[64,64,256]{2,1,0:T(8,128)(2,1)S(1)} %get-tuple-element.59.refs_0_, bf16[3,66,64,256]{3,2,1,0:T(8,128)(2,1)S(1)} %get-tuple-element.60.refs_1_, f32[4608,128]{1,0:T(8,128)S(1)} %get-tuple-element.61.refs_2_, f32[512,1]{1,0:T(8,128)S(1)} %copy-done.3, ...), custom_call_target="tpu_custom_call" | custom-call | flops 4831838208 | bytes 4194304 | tf_op jit(solution)/shard_map/pallas_call | solution.py:404
  78.7 2.9 %collective-permute-done.5.refs_1_ = bf16[5136,128]{1,0:T(8,128)(2,1)S(1)} collective-permute-done((bf16[5136,128]{1,0:T(8,128)(2,1)S(1)}, bf16[5136,128]{1,0:T(8,128)(2,1)S(1)}, u32[]{:S(2)}, u32[]{:S(2)}) %collective-permute-start.5) | collective-permute-done | bytes 1314848 | tf_op jit(solution)/shard_map/ppermute | solution.py:33
  82.0 1.9 %collective-permute-start.6 = (bf16[2576,128]{1,0:T(8,128)(2,1)S(1)}, bf16[2576,128]{1,0:T(8,128)(2,1)S(1)}, u32[]{:S(2)}, u32[]{:S(2)}) collective-permute-start(bf16[2576,128]{1,0:T(8,128)(2,1)S(1)} %get-tuple-element.66), channel_id=1, source_target_pairs={{0,16},{1,3},{2,18},{3,1},{4,20},{5,7},{6,22},{7,5},{8,24},{9,11},... | collective-permute-start | bytes 1978376 | tf_op jit(solution)/shard_map/ppermute | solution.py:33
  83.8 7.8 %shard_map.134 = (bf16[64,64,256]{2,1,0:T(8,128)(2,1)}, f32[1,256]{1,0:T(1,128)S(1)}) custom-call(bf16[64,64,256]{2,1,0:T(8,128)(2,1)S(1)} %get-tuple-element.51.refs_0_, bf16[64,64,256]{2,1,0:T(8,128)(2,1)S(1)} %bitcast.19, f32[8,256]{1,0:T(8,128)S(1)} %get-tuple-element.46.refs_2_.refs_3_.refs_6_.refs_5_, ...), custom_call_target="tpu_custom_call" | custom-call | flops 4831838208 | bytes 4194304 | tf_op jit(solution)/shard_map/pallas_call | solution.py:404
  92.8 1.8 %collective-permute-start.7 = (bf16[1296,128]{1,0:T(8,128)(2,1)S(1)}, bf16[1296,128]{1,0:T(8,128)(2,1)S(1)}, u32[]{:S(2)}, u32[]{:S(2)}) collective-permute-start(bf16[1296,128]{1,0:T(8,128)(2,1)S(1)} %get-tuple-element.69), channel_id=1, source_target_pairs={{0,2},{1,17},{2,0},{3,19},{4,6},{5,21},{6,4},{7,23},{8,10},{9,25},... | collective-permute-start | bytes 995336 | tf_op jit(solution)/shard_map/ppermute | solution.py:33
  94.7 3.5 %shard_map.136 = (f32[64,64,256]{2,1,0:T(8,128)}, f32[1,256]{1,0:T(1,128)S(1)}) custom-call(f32[4096,256]{1,0:T(8,128)S(1)} %get-tuple-element.55.refs_0_, bf16[64,64,256]{2,1,0:T(8,128)(2,1)S(1)} %bitcast.20, bf16[64,64,256]{2,1,0:T(8,128)(2,1)S(1)} %bitcast.22, f32[2,256]{1,0:T(2,128)S(1)} %get-tuple-element.44.refs_1_.refs_5_.refs_3_, ...), custom_call_target="tpu_custom_call" | custom-call | bytes 4194304 | tf_op jit(solution)/shard_map/pallas_call | solution.py:404
  98.2 1.8 %collective-permute-done.7.refs_1_ = bf16[1296,128]{1,0:T(8,128)(2,1)S(1)} collective-permute-done((bf16[1296,128]{1,0:T(8,128)(2,1)S(1)}, bf16[1296,128]{1,0:T(8,128)(2,1)S(1)}, u32[]{:S(2)}, u32[]{:S(2)}) %collective-permute-start.7) | collective-permute-done | bytes 331808 | tf_op jit(solution)/shard_map/ppermute | solution.py:33
  101.5 4.0 %collective-permute-done.8.refs_1_ = bf16[656,128]{1,0:T(8,128)(2,1)S(1)} collective-permute-done((bf16[656,128]{1,0:T(8,128)(2,1)S(1)}, bf16[656,128]{1,0:T(8,128)(2,1)S(1)}, u32[]{:S(2)}, u32[]{:S(2)}) %collective-permute-start.8) | collective-permute-done | bytes 167968 | tf_op jit(solution)/shard_map/ppermute | solution.py:33
  105.5 3.1 %collective-permute-start.9 = (bf16[336,128]{1,0:T(8,128)(2,1)S(1)}, bf16[336,128]{1,0:T(8,128)(2,1)S(1)}, u32[]{:S(2)}, u32[]{:S(2)}) collective-permute-start(bf16[336,128]{1,0:T(8,128)(2,1)S(1)} %get-tuple-element.74), channel_id=1, source_target_pairs={{0,8},{1,9},{2,10},{3,11},{4,12},{5,13},{6,14},{7,15},{8,0},{9,1},... | collective-permute-start | bytes 258056 | tf_op jit(solution)/shard_map/ppermute | solution.py:33
  109.2 1.9 %collective-permute-done.9.refs_1_ = bf16[336,128]{1,0:T(8,128)(2,1)S(1)} collective-permute-done((bf16[336,128]{1,0:T(8,128)(2,1)S(1)}, bf16[336,128]{1,0:T(8,128)(2,1)S(1)}, u32[]{:S(2)}, u32[]{:S(2)}) %collective-permute-start.9) | collective-permute-done | bytes 86048 | tf_op jit(solution)/shard_map/ppermute | solution.py:33
  (35 shorter events, 9.7 us)
Async XLA Ops:
  0.6 24.8 %copy-start = (bf16[1,64,64,256]{3,2,1,0:T(8,128)(2,1)S(1)}, bf16[1,64,64,256]{3,2,1,0:T(8,128)(2,1)}, u32[]{:S(2)}) copy-start(bf16[1,64,64,256]{3,2,1,0:T(8,128)(2,1)} %param.7) | copy-start | bytes 6291460
  2.3 8.4 %collective-permute-start = (bf16[336,128]{1,0:T(8,128)(2,1)S(1)}, bf16[336,128]{1,0:T(8,128)(2,1)S(1)}, u32[]{:S(2)}, u32[]{:S(2)}) collective-permute-start(bf16[336,128]{1,0:T(8,128)(2,1)S(1)} %pad_maximum_fusion.refs_0_), channel_id=1, source_target_pairs={{0,8},{1,9},{2,10},{3,11},{4,12},{5,13},{6,14},{7,15},{8,0},{9,1},... | collective-permute-start | bytes 258056 | tf_op jit(solution)/shard_map/ppermute | solution.py:33
  10.8 5.4 %collective-permute-start.1 = (bf16[656,128]{1,0:T(8,128)(2,1)S(1)}, bf16[656,128]{1,0:T(8,128)(2,1)S(1)}, u32[]{:S(2)}, u32[]{:S(2)}) collective-permute-start(bf16[656,128]{1,0:T(8,128)(2,1)S(1)} %shard_map.127.refs_0_), channel_id=1, source_target_pairs={{0,4},{1,5},{2,6},{3,7},{4,0},{5,1},{6,2},{7,3},{8,12},{9,13},{10,... | collective-permute-start | bytes 503816 | tf_op jit(solution)/shard_map/ppermute | solution.py:33
  16.2 7.2 %collective-permute-start.2 = (bf16[1296,128]{1,0:T(8,128)(2,1)S(1)}, bf16[1296,128]{1,0:T(8,128)(2,1)S(1)}, u32[]{:S(2)}, u32[]{:S(2)}) collective-permute-start(bf16[1296,128]{1,0:T(8,128)(2,1)S(1)} %shard_map.128.refs_0_), channel_id=1, source_target_pairs={{0,2},{1,17},{2,0},{3,19},{4,6},{5,21},{6,4},{7,23},{8,10},{9,25},... | collective-permute-start | bytes 995336 | tf_op jit(solution)/shard_map/ppermute | solution.py:33
  23.5 10.7 %collective-permute-start.3 = (bf16[2576,128]{1,0:T(8,128)(2,1)S(1)}, bf16[2576,128]{1,0:T(8,128)(2,1)S(1)}, u32[]{:S(2)}, u32[]{:S(2)}) collective-permute-start(bf16[2576,128]{1,0:T(8,128)(2,1)S(1)} %shard_map.129.refs_0_), channel_id=1, source_target_pairs={{0,16},{1,3},{2,18},{3,1},{4,20},{5,7},{6,22},{7,5},{8,24},{9,11},... | collective-permute-start | bytes 1978376 | tf_op jit(solution)/shard_map/ppermute | solution.py:33
  25.4 1.6 %copy-start.1 = (bf16[1,64,64,256]{3,2,1,0:T(8,128)(2,1)S(1)}, bf16[1,64,64,256]{3,2,1,0:T(8,128)(2,1)}, u32[]{:S(2)}) copy-start(bf16[1,64,64,256]{3,2,1,0:T(8,128)(2,1)} %param.13) | copy-start | bytes 6291460
  29.6 2.7 %copy-start.4 = (bf16[3,66,64,256]{3,2,1,0:T(8,128)(2,1)}, bf16[3,66,64,256]{3,2,1,0:T(8,128)(2,1)S(1)}, u32[]{:S(2)}) copy-start(bf16[3,66,64,256]{3,2,1,0:T(8,128)(2,1)S(1)} %get-tuple-element.43.refs_0_) | copy-start | bytes 19464196
  32.4 2.0 %copy-start.5 = (bf16[1,512]{1,0:T(2,128)(2,1)S(1)}, bf16[1,512]{1,0:T(2,128)(2,1)}, u32[]{:S(2)}) copy-start(bf16[1,512]{1,0:T(2,128)(2,1)} %param.8) | copy-start | bytes 3076
  34.3 3.2 %collective-permute-start.4 = (bf16[5136,128]{1,0:T(8,128)(2,1)S(1)}, bf16[5136,128]{1,0:T(8,128)(2,1)}, u32[]{:S(2)}, u32[]{:S(2)}) collective-permute-start(bf16[5136,128]{1,0:T(8,128)(2,1)S(1)} %shard_map.130.refs_0_), channel_id=1, source_target_pairs={{0,1},{1,0},{2,3},{3,2},{4,5},{5,4},{6,7},{7,6},{8,9},{9,8},{10,11... | collective-permute-start | bytes 3944456 | tf_op jit(solution)/shard_map/ppermute | solution.py:33
  37.5 11.0 %slice-start = ((s8[6488064]{0:T(1024)(128)(4,1)}), s8[4194304]{0:T(1024)(128)(4,1)S(1)}, s32[]{:S(2)}) async-start(s8[6488064]{0:T(1024)(128)(4,1)} %bitcast.23), calls=%async_computation | async-start | bytes 8388608
  39.7 8.9 %slice-start.1 = ((s8[6488064]{0:T(1024)(128)(4,1)}), s8[2293760]{0:T(1024)(128)(4,1)S(1)}, s32[]{:S(2)}) async-start(s8[6488064]{0:T(1024)(128)(4,1)} %bitcast.23), calls=%async_computation.1 | async-start | bytes 4587520
  62.0 9.1 %copy-start.3 = (f32[512,1]{1,0:T(8,128)S(1)}, f32[512,1]{1,0:T(8,128)}, u32[]{:S(2)}) copy-start(f32[512,1]{1,0:T(8,128)} %copy.14.refs_3_) | copy-start | bytes 6148
  78.5 3.1 %collective-permute-start.5 = (bf16[5136,128]{1,0:T(8,128)(2,1)S(1)}, bf16[5136,128]{1,0:T(8,128)(2,1)S(1)}, u32[]{:S(2)}, u32[]{:S(2)}) collective-permute-start(bf16[5136,128]{1,0:T(8,128)(2,1)S(1)} %get-tuple-element.64), channel_id=1, source_target_pairs={{0,1},{1,0},{2,3},{3,2},{4,5},{5,4},{6,7},{7,6},{8,9},{9,8},{10,11... | collective-permute-start | bytes 3944456 | tf_op jit(solution)/shard_map/ppermute | solution.py:33
  82.0 10.7 %collective-permute-start.6 = (bf16[2576,128]{1,0:T(8,128)(2,1)S(1)}, bf16[2576,128]{1,0:T(8,128)(2,1)S(1)}, u32[]{:S(2)}, u32[]{:S(2)}) collective-permute-start(bf16[2576,128]{1,0:T(8,128)(2,1)S(1)} %get-tuple-element.66), channel_id=1, source_target_pairs={{0,16},{1,3},{2,18},{3,1},{4,20},{5,7},{6,22},{7,5},{8,24},{9,11},... | collective-permute-start | bytes 1978376 | tf_op jit(solution)/shard_map/ppermute | solution.py:33
  83.8 10.8 %copy-start.2 = (bf16[1,64,64,256]{3,2,1,0:T(8,128)(2,1)S(1)}, bf16[1,64,64,256]{3,2,1,0:T(8,128)(2,1)}, u32[]{:S(2)}) copy-start(bf16[1,64,64,256]{3,2,1,0:T(8,128)(2,1)} %param.13) | copy-start | bytes 6291460
  92.8 7.2 %collective-permute-start.7 = (bf16[1296,128]{1,0:T(8,128)(2,1)S(1)}, bf16[1296,128]{1,0:T(8,128)(2,1)S(1)}, u32[]{:S(2)}, u32[]{:S(2)}) collective-permute-start(bf16[1296,128]{1,0:T(8,128)(2,1)S(1)} %get-tuple-element.69), channel_id=1, source_target_pairs={{0,2},{1,17},{2,0},{3,19},{4,6},{5,21},{6,4},{7,23},{8,10},{9,25},... | collective-permute-start | bytes 995336 | tf_op jit(solution)/shard_map/ppermute | solution.py:33
  100.1 5.4 %collective-permute-start.8 = (bf16[656,128]{1,0:T(8,128)(2,1)S(1)}, bf16[656,128]{1,0:T(8,128)(2,1)S(1)}, u32[]{:S(2)}, u32[]{:S(2)}) collective-permute-start(bf16[656,128]{1,0:T(8,128)(2,1)S(1)} %get-tuple-element.72), channel_id=1, source_target_pairs={{0,4},{1,5},{2,6},{3,7},{4,0},{5,1},{6,2},{7,3},{8,12},{9,13},{10,... | collective-permute-start | bytes 503816 | tf_op jit(solution)/shard_map/ppermute | solution.py:33
  105.5 5.6 %collective-permute-start.9 = (bf16[336,128]{1,0:T(8,128)(2,1)S(1)}, bf16[336,128]{1,0:T(8,128)(2,1)S(1)}, u32[]{:S(2)}, u32[]{:S(2)}) collective-permute-start(bf16[336,128]{1,0:T(8,128)(2,1)S(1)} %get-tuple-element.74), channel_id=1, source_target_pairs={{0,8},{1,9},{2,10},{3,11},{4,12},{5,13},{6,14},{7,15},{8,0},{9,1},... | collective-permute-start | bytes 258056 | tf_op jit(solution)/shard_map/ppermute | solution.py:33

commit v2 on v1

--- a/solution.py
+++ b/solution.py
@@ -45,7 +45,9 @@
         return me ^ jnp.where(core == 0, self.mask(slot, 0), self.mask(slot, 1))
 
 
-ROWS = 16
+ROWS = 4
+UNITS = 2
+PIECE = 64
 F32 = jnp.float32
 BF16 = jnp.bfloat16
 VMEM_BYTES = 14 * 1024 * 1024
@@ -93,18 +95,144 @@
     three[2, row + 1] = right.astype(three.dtype)
 
 
-def conv_rows(three, kernel, start, back):
+def accumulators(body, *refs):
+    groups = 4
+
+    def run(*accs):
+        accs = iter(accs)
+        body(*refs, [[[next(accs) for _ in range(ROWS)] for _ in range(groups)] for _ in range(UNITS)])
+
+    pl.run_scoped(run, *[pltpu.ACC(unit)((PIECE, 2 * LANES), F32) for unit in range(UNITS) for _ in range(groups * ROWS)])
+
+
+def interleave(pieces, slots):
+    return [pieces * (i + 1) // slots - pieces * i // slots for i in range(slots)]
+
+
+def times(value, size):
+    return value * size if isinstance(value, int) else pl.multiple_of(value * size, size)
+
+
+def conv_step(accs, three, kernel, step, parity, back, others=()):
+    others = list(others)
+    for tap, share in enumerate(interleave(len(others), 9)):
+        at = (8 - tap if back else tap) * three.shape[3]
+        stage = (parity + tap) % 2
+        for unit in range(UNITS):
+            pltpu.matmul_push_rhs(kernel[at : at + three.shape[3], :], stage, unit, transpose=back)
+        for piece in range(ROWS):
+            for unit in range(UNITS):
+                row = (UNITS * step + unit) * ROWS + piece + tap // 3
+                pltpu.matmul_acc_lhs(
+                    accs[unit][parity][piece], three[tap % 3, row], load_staged_rhs=stage if piece == 0 else None
+                )
+        for _ in range(share):
+            others.pop(0)()
+
+
+def conv_rows(accs, step, parity, use):
+    def one(unit, piece):
+        use((UNITS * step + unit) * ROWS + piece, pltpu.matmul_pop(accs[unit][parity][piece]))
+
+    return [functools.partial(one, unit, piece) for unit in range(UNITS) for piece in range(ROWS)]
+
+
+def conv_all(accs, three, kernel, back, use):
+    steps = (three.shape[1] - 2) // (UNITS * ROWS)
+    for step in range(steps):
+        others = conv_rows(accs, step - 1, (step - 1) % 2, use) if step else ()
+        conv_step(accs, three, kernel, step, step % 2, back, others)
+    for other in conv_rows(accs, steps - 1, (steps - 1) % 2, use):
+        other()
+
+
+class Sums:
+    def __init__(self, channels, count):
+        self.values = [jnp.zeros((8, channels), F32)] * count
+
+    def add(self, *values):
+        self.values = [s + fold(v) for s, v in zip(self.values, values)]
+
+    def totals(self):
+        return [total(s) for s in self.values]
+
+
+def store_turned(turned, padded, row):
+    width, channels = padded.shape[1:]
+    size = ROWS * width
+    lanes = pl.ds(times(row // ROWS, size), size)
+    turned[0, :, lanes] = padded[pl.ds(row + 1, ROWS)].reshape(size, channels).T
+    turned[1, :, lanes] = padded[pl.ds(row, ROWS)].reshape(size, channels).T
+
+
+def turn_end(turned, padded):
+    height = padded.shape[0] - 2
+    width, channels = padded.shape[1:]
+    at = height * width
+    turned[1, :, at : at + 2 * width] = padded[height : height + 2].reshape(2 * width, channels).T
+
+
+def grad_step(accs, turned, three, work, stage, others=()):
+    others = list(others)
     width, channels = three.shape[2:]
-    acc = None
-    for tap in range(9):
-        lhs = three[tap % 3, pl.ds(start + tap // 3, ROWS)].reshape(ROWS * width, channels)
-        at = (8 - tap if back else tap) * channels
-        rhs = kernel[at : at + channels, :]
-        part = lax.dot_general(
-            lhs, rhs, (((1,), (1 if back else 0,)), ((), ())), preferred_element_type=F32
-        )
-        acc = part if acc is None else acc + part
-    return acc
+    size = ROWS * width
+    for unit, column, chunk, _ in work:
+        rhs = three[column, pl.ds(1 + times(chunk, ROWS), ROWS)].reshape(size, channels)
+        pltpu.matmul_push_rhs(rhs, stage, unit)
+    shares = iter(interleave(len(others), 3 * ROWS))
+    for row in range(3):
+        for piece in range(ROWS):
+            for unit, _, chunk, groups in work:
+                source, at = (0, times(chunk, size)) if row == 1 else (1, times(chunk, size) + row * width)
+                lhs = turned[source, piece * PIECE : (piece + 1) * PIECE, pl.ds(at, size)]
+                first = row == 0 and piece == 0
+                pltpu.matmul_acc_lhs(accs[unit][groups[row]][piece], lhs, load_staged_rhs=stage if first else None)
+            for _ in range(next(shares)):
+                others.pop(0)()
+
+
+def kernel_grad(accs, turned, three, flat, beside, carry):
+    height, channels = three.shape[1] - 2, three.shape[3]
+    chunks = height // ROWS
+
+    def outer(i, carry):
+        kept = [carry]
+
+        def other(row):
+            kept[0] = beside(row, kept[0])
+
+        for k in range(4):
+            chunk = 4 * i + k
+            work = [(0, 0, chunk, (0, 1, 2)), (1, 2, chunk, (0, 1, 2))]
+            others = [functools.partial(other, ROWS * chunk + j) for j in range(ROWS)] if beside else ()
+            grad_step(accs, turned, three, work, k % 2, others)
+        return kept[0]
+
+    if beside:
+        carry = lax.fori_loop(0, chunks // 4, outer, carry)
+    else:
+        for i in range(chunks // 4):
+            outer(i, carry)
+
+    def store(tap, piece, value):
+        store_flat(flat, (tap * channels + piece * PIECE) * 2, value)
+
+    def side(unit, column, row, piece):
+        store(3 * row + 2 - column, piece, pltpu.matmul_pop(accs[unit][row][piece]))
+
+    for row in range(2):
+        for unit, column in ((0, 0), (1, 2)):
+            for piece in range(ROWS):
+                side(unit, column, row, piece)
+    half = chunks // UNITS
+    for chunk in range(half):
+        work = [(unit, 1, unit * half + chunk, (3, 0, 1)) for unit in range(UNITS)]
+        others = [functools.partial(side, unit, 2 * unit, 2, piece) for unit in range(UNITS) for piece in range(ROWS)]
+        grad_step(accs, turned, three, work, chunk % 2, others if chunk == 0 else ())
+    for row, group in enumerate((3, 0, 1)):
+        for piece in range(ROWS):
+            store(3 * row + 1, piece, pltpu.matmul_pop(accs[0][group][piece]) + pltpu.matmul_pop(accs[1][group][piece]))
+    return carry
 
 
 def store_flat(flat, start, value):
@@ -117,21 +245,6 @@
     left = flat[pl.ds(start, rows, stride=2), :]
     right = flat[pl.ds(start + 1, rows, stride=2), :]
     return jnp.concatenate([left, right], axis=1)
-
-
-def kernel_grad(acts, three, flat):
-    height, width, channels = acts.shape
-
-    def step(tap, _):
-        row = tap // 3
-        col = tap - 3 * row
-        lhs = acts[...].reshape(height * width, channels)
-        rhs = three[2 - col, pl.ds(2 - row, height)].reshape(height * width, channels)
-        out = lax.dot_general(lhs, rhs, (((0,), (0,)), ((), ())), preferred_element_type=F32)
-        store_flat(flat, pl.multiple_of(tap * 2 * channels, 2 * channels), out)
-        return 0
-
-    lax.fori_loop(0, 9, step, 0)
 
 
 def prepare_kernel(x, g, stats, three, g_sum):
@@ -163,119 +276,124 @@
     stats[1:2, :] = inv
 
 
-def first_kernel(x, stats, vec, q, kernel, act, centred, stats_out, three):
+def first_kernel(x, stats, vec, time, kernel, turned, raw, stats_out, three):
+    accumulators(first_body, x, stats, vec, time, kernel, turned, raw, stats_out, three)
+
+
+def first_body(x, stats, vec, time, kernel, turned, raw, stats_out, three, accs):
     height, width, channels = x.shape
+    pixels = height * width
+    per_group = channels // GROUPS
+    mean, scale, shift = stats[0:1, :], stats[1:2, :] * vec[0:1, :], vec[1:2, :]
+    offset = vec[2:3, :] + time[...]
+    sums = Sums(channels, 2)
+    pivot = []
+    clear_edges(three)
+
+    def activate(row):
+        h = (x[row].astype(F32) - mean) * scale + shift
+        store_three(three, row, h * sigmoid(h))
+        if row % ROWS == ROWS - 1:
+            store_turned(turned, three.at[1], row + 1 - ROWS)
+
+    def use(row, v):
+        if row == 0:
+            pivot.append(total(fold(v)) / width)
+        raw[row * width : (row + 1) * width, :] = v
+        d = v - pivot[0]
+        sums.add(d, d * d)
+
+    per_step = UNITS * ROWS
+    steps = height // per_step
+    for row in range(per_step + 1):
+        activate(row)
+    for step in range(steps):
+        ahead = range((step + 1) * per_step + 1, min((step + 2) * per_step + 1, height))
+        others = [functools.partial(activate, row) for row in ahead]
+        done = conv_rows(accs, step - 1, (step - 1) % 2, use) if step else []
+        mixed = [f for i in range(per_step) for f in (*others[i : i + 1], *done[i : i + 1])]
+        conv_step(accs, three, kernel, step, step % 2, False, mixed)
+    turn_end(turned, three.at[1])
+    for other in conv_rows(accs, steps - 1, (steps - 1) % 2, use):
+        other()
+    part, square = [v / pixels for v in sums.totals()]
+    spread = square - part * part
+    middle = pivot[0] + part + offset
+    mean_two = group_sum(middle) / per_group
+    away = middle - mean_two
+    stats_out[0:1, :] = offset - mean_two
+    stats_out[1:2, :] = lax.rsqrt(group_sum(spread + away * away) / per_group + EPS)
+
+
+def second_kernel(g_three, raw, stats, vec, kernel, act, sums, flat, three, dc_sum, dh, turned):
+    accumulators(second_body, g_three, raw, stats, vec, kernel, act, sums, flat, three, dc_sum, dh, turned)
+
+
+def second_body(g_three, raw, stats, vec, kernel, act, sums, flat, three, dc_sum, dh, turned, accs):
+    height, width, channels = act.shape[0] - 2, act.shape[1], act.shape[2]
     count = height * width * (channels // GROUPS)
-    mean, scale, shift = stats[0:1, :], stats[1:2, :] * vec[0:1, :], vec[1:2, :]
-    time = jnp.dot(q[...], kernel[9 * channels :, :], preferred_element_type=F32)
-    offset = vec[2:3, :] + time
-    zero = jnp.zeros((8, channels), F32)
+    move, inv, gain, shift = stats[0:1, :], stats[1:2, :], vec[3:4, :], vec[4:5, :]
+    scale = inv * gain
+    both = Sums(channels, 2)
+    act[0:1] = jnp.zeros((1, width, channels), BF16)
+    act[height + 1 : height + 2] = jnp.zeros((1, width, channels), BF16)
     clear_edges(three)
 
-    def activate(i, _):
-        row = i * 4
-        h = (x[pl.ds(row, 4)].astype(F32) - mean) * scale + shift
-        a = h * sigmoid(h)
-        act[pl.ds(row, 4)] = a.astype(BF16)
-        for j in range(4):
-            store_three(three, row + j, a[j])
-        return 0
-
-    lax.fori_loop(0, height // 4, activate, 0)
-
-    def conv(i, s):
-        row = pl.multiple_of(i * ROWS, ROWS)
-        acc = conv_rows(three, kernel, row, False)
-        centred[pl.ds(row * width, ROWS * width), :] = acc
-        return s + fold(acc)
-
-    s = lax.fori_loop(0, height // ROWS, conv, zero)
-    mean_two = group_sum(total(s) / (height * width) + offset) / (channels // GROUPS)
-    move = offset - mean_two
-
-    def centre(i, v):
-        at = pl.ds(i * 256, 256)
-        d = centred[at, :] + move
-        centred[at, :] = d
-        return v + fold(d * d)
-
-    v = lax.fori_loop(0, height * width // 256, centre, zero)
-    stats_out[...] = lax.rsqrt(group_sum(total(v)) / count + EPS)
-
-
-def second_kernel(three, centred, inv, vec, kernel, dh, act, sums, grad):
-    height, width, channels = act.shape
-    scale, shift = inv[...] * vec[3:4, :], vec[4:5, :]
-    zero = jnp.zeros((8, channels), F32)
-
-    def conv(i, carry):
-        s, sc = carry
-        row = pl.multiple_of(i * ROWS, ROWS)
-        at = pl.ds(row * width, ROWS * width)
-        acc = conv_rows(three, kernel, row, True)
-        c = centred[at, :]
+    def use(row, v):
+        at = slice(row * width, (row + 1) * width)
+        c = raw[at, :] + move
         h = c * scale + shift
         sig = sigmoid(h)
         a = h * sig
-        act[pl.ds(row, ROWS)] = a.astype(BF16).reshape(ROWS, width, channels)
-        d = acc * (sig + a * (1.0 - sig))
+        act[row + 1] = a.astype(BF16)
+        d = v * (sig + a * (1.0 - sig))
         dh[at, :] = d
-        return s + fold(d), sc + fold(d * c)
-
-    s, sc = lax.fori_loop(0, height // ROWS, conv, (zero, zero))
-    sums[0:1, :] = total(sc) * inv[...]
-    sums[1:2, :] = total(s)
-    kernel_grad(act, three, grad)
-
-
-def middle_kernel(dh_two, centred, inv_two, sums_two, x, stats, vec, kernel, three, dc_sum, dq, dh, sums):
+        both.add(d, d * c)
+        if row % ROWS == ROWS - 1:
+            store_turned(turned, act, row + 1 - ROWS)
+
+    conv_all(accs, g_three, kernel, True, use)
+    turn_end(turned, act)
+    s, sc = both.totals()
+    sn = sc * inv
+    sums[0:1, :] = sn
+    sums[1:2, :] = s
+    base = inv * (group_sum(s * gain) / count)
+    slope = inv * inv * (group_sum(sn * gain) / count)
+
+    def back(row, dc):
+        at = pl.ds(times(row, width), width)
+        d = dh[at, :] * scale - base - (raw[at, :] + move) * slope
+        store_three(three, row, d)
+        return dc + fold(d)
+
+    dc_sum[...] = total(kernel_grad(accs, turned, g_three, flat, back, jnp.zeros((8, channels), F32)))
+
+
+def third_kernel(three, x, stats, vec, kernel, dh, sums):
+    accumulators(third_body, three, x, stats, vec, kernel, dh, sums)
+
+
+def third_body(three, x, stats, vec, kernel, dh, sums, accs):
     height, width, channels = x.shape
-    count = height * width * (channels // GROUPS)
-    gain = vec[3:4, :]
-    inv = inv_two[...]
-    scale = inv * gain
-    base = inv * (group_sum(sums_two[1:2, :] * gain) / count)
-    slope = inv * inv * (group_sum(sums_two[0:1, :] * gain) / count)
-    zero = jnp.zeros((8, channels), F32)
-    clear_edges(three)
-
-    def back(i, s):
-        row = i * 4
-        at = pl.ds(row * width, 4 * width)
-        d = dh_two[at, :] * scale - base - centred[at, :] * slope
-        rows = d.reshape(4, width, channels)
-        for j in range(4):
-            store_three(three, row + j, rows[j])
-        return s + fold(d)
-
-    dc = total(lax.fori_loop(0, height // 4, back, zero))
-    dc_sum[...] = dc
-    dq[...] = lax.dot_general(
-        dc,
-        kernel[9 * channels :, :].astype(F32),
-        (((1,), (1,)), ((), ())),
-        precision=lax.Precision.HIGHEST,
-        preferred_element_type=F32,
-    )
     mean, scale, shift = stats[0:1, :], stats[1:2, :] * vec[0:1, :], vec[1:2, :]
-
-    def conv(i, carry):
-        s, sn = carry
-        row = pl.multiple_of(i * ROWS, ROWS)
-        acc = conv_rows(three, kernel, row, True)
-        c = x[pl.ds(row, ROWS)].astype(F32).reshape(ROWS * width, channels) - mean
+    both = Sums(channels, 2)
+
+    def use(row, v):
+        c = x[row].astype(F32) - mean
         h = c * scale + shift
         sig = sigmoid(h)
-        d = acc * (sig + h * sig * (1.0 - sig))
-        dh[pl.ds(row * width, ROWS * width), :] = d
-        return s + fold(d), sn + fold(d * c)
-
-    s, sn = lax.fori_loop(0, height // ROWS, conv, (zero, zero))
-    sums[0:1, :] = total(sn) * stats[1:2, :]
-    sums[1:2, :] = total(s)
-
-
-def input_kernel(dh, x, g, stats, sums, vec, result, done):
+        d = v * (sig + h * sig * (1.0 - sig))
+        dh[row * width : (row + 1) * width, :] = d
+        both.add(d, d * c)
+
+    conv_all(accs, three, kernel, True, use)
+    s, sn = both.totals()
+    sums[0:1, :] = sn * stats[1:2, :]
+    sums[1:2, :] = s
+
+
+def input_kernel(dh, x, g, stats, sums, vec, dc_sum, kernel, result, dq, done):
     height, width, channels = x.shape
     count = height * width * (channels // GROUPS)
     mean, inv, gain = stats[0:1, :], stats[1:2, :], vec[0:1, :]
@@ -291,29 +409,43 @@
         return 0
 
     lax.fori_loop(0, height // 4, back, 0)
+    dq[...] = lax.dot_general(
+        dc_sum[...],
+        kernel[9 * channels :, :].astype(F32),
+        (((1,), (1,)), ((), ())),
+        precision=lax.Precision.HIGHEST,
+        preferred_element_type=F32,
+    )
     done[...] = base
 
 
 def last_kernel(act, x, vec, kernel, result, done, three):
-    height, width, channels = x.shape
+    accumulators(last_body, act, x, vec, kernel, result, done, three)
+
+
+def last_body(act, x, vec, kernel, result, done, three, accs):
+    height = x.shape[0]
     bias = vec[5:6, :]
     clear_edges(three)
 
-    def spread(i, _):
-        rows = act[pl.ds(i * 4, 4)].astype(F32)
-        for j in range(4):
-            store_three(three, i * 4 + j, rows[j])
-        return 0
-
-    lax.fori_loop(0, height // 4, spread, 0)
-
-    def conv(i, _):
-        row = pl.multiple_of(i * ROWS, ROWS)
-        acc = conv_rows(three, kernel, row, False).reshape(ROWS, width, channels)
-        result[pl.ds(row, ROWS)] = (x[pl.ds(row, ROWS)].astype(F32) + acc + bias).astype(BF16)
-        return 0
-
-    lax.fori_loop(0, height // ROWS, conv, 0)
+    def spread(row):
+        store_three(three, row, act[row + 1].astype(F32))
+
+    def use(row, v):
+        result[row] = (x[row].astype(F32) + v + bias).astype(BF16)
+
+    per_step = UNITS * ROWS
+    steps = height // per_step
+    for row in range(per_step + 1):
+        spread(row)
+    for step in range(steps):
+        ahead = range((step + 1) * per_step + 1, min((step + 2) * per_step + 1, height))
+        others = [functools.partial(spread, row) for row in ahead]
+        done_rows = conv_rows(accs, step - 1, (step - 1) % 2, use) if step else []
+        mixed = [f for i in range(per_step) for f in (*others[i : i + 1], *done_rows[i : i + 1])]
+        conv_step(accs, three, kernel, step, step % 2, False, mixed)
+    for other in conv_rows(accs, steps - 1, (steps - 1) % 2, use):
+        other()
     done[...] = bias
 
 
@@ -333,7 +465,7 @@
     send_next[rows : rows + VEC_ROWS, :] = vec.astype(BF16)
 
 
-def arrange_kernel(wires, cuts, mine, got, first, kernel_two, vec, flat_one, flat_two, flat_project, flat_vec):
+def arrange_kernel(wires, cuts, mine, got, q, first, kernel_two, vec, time, flat_one, flat_two, flat_project, flat_vec):
     me = wires.me()
     block = sum(cuts)
     flats = (flat_one, flat_two, flat_project)
@@ -352,12 +484,17 @@
     at = wires.slots * block
     flat_vec[...] = mine[at : at + VEC_ROWS, :].astype(F32) + got[at : at + VEC_ROWS, :].astype(F32)
     vec[...] = load_flat(flat_vec, 0, VEC_ROWS // 2)
-
-
-def pack_kernel(wires, cuts, act, three, flat_two, q, dc_sum, sums_one, sums_two, g_sum, send, keep, flat_one, flat_project):
+    time[...] = jnp.dot(q[...], first[rows_one:, :], preferred_element_type=F32)
+
+
+def grad_kernel(turned, three, flat):
+    accumulators(lambda *refs: kernel_grad(refs[-1], *refs[:-1], None, 0), turned, three, flat)
+
+
+def pack_kernel(wires, cuts, turned, three, flat_two, q, dc_sum, sums_one, sums_two, g_sum, send, keep, flat_one, flat_project):
     me = wires.me()
     block = sum(cuts)
-    kernel_grad(act, three, flat_one)
+    grad_kernel(turned, three, flat_one)
     for start in range(0, q.shape[0], 256):
         store_flat(flat_project, 2 * start, q[start : start + 256, :] * dc_sum[...])
     for slot in range(wires.slots):
@@ -405,13 +542,14 @@
         run,
         out_shape=[jax.ShapeDtypeStruct(shape, dtype) for shape, dtype in outs],
         in_specs=[pl.BlockSpec(memory_space=pltpu.VMEM)] * n_in + [pl.BlockSpec(memory_space=pl.ANY)] * held,
+        out_specs=[pl.BlockSpec(memory_space=pltpu.VMEM)] * len(outs),
         scratch_shapes=[pltpu.VMEM(shape, dtype) for shape, dtype in scratch],
         compiler_params=pltpu.CompilerParams(vmem_limit_bytes=VMEM_BYTES),
         cost_estimate=pl.CostEstimate(flops=flops, bytes_accessed=size, transcendentals=0),
     )(*args, *after)
 
 
-def gather(wires, cuts, parts, vectors, beside):
+def gather(wires, cuts, parts, vectors, q, beside):
     block = sum(cuts)
     n_vec = vectors.shape[0]
     me = wires.me()
@@ -430,9 +568,10 @@
     if all(rows % 8 == 0 for rows in cuts):
         return call(
             functools.partial(arrange_kernel, wires, cuts),
-            [*outs, ((VEC_ROWS // 2, channels), F32)],
+            [*outs, ((VEC_ROWS // 2, channels), F32), ((1, channels), F32)],
             held,
             got,
+            q,
             scratch=[((rows, LANES), F32) for rows in (*totals, VEC_ROWS)],
         )
     rows = wires.slots * block
@@ -444,10 +583,11 @@
         whole.append(both[:, at : at + cut].reshape(-1, channels))
         at += cut
     vec = (held[rows:].astype(F32) + got[rows:].astype(F32)).reshape(VEC_ROWS // 2, channels)
-    return jnp.concatenate([whole[0], whole[2]]), whole[1], vec
-
-
-def pack(wires, cuts, act, three, flat_two, q, dc_sum, sums_one, sums_two, g_sum):
+    time = jnp.dot(q, whole[2], preferred_element_type=F32)
+    return jnp.concatenate([whole[0], whole[2]]), whole[1], vec, time
+
+
+def pack(wires, cuts, turned, three, flat_two, q, dc_sum, sums_one, sums_two, g_sum):
     block = sum(cuts)
     shape = (wires.slots * block + VEC_ROWS, LANES)
     totals = [wires.n * rows for rows in cuts]
@@ -455,7 +595,7 @@
         return call(
             functools.partial(pack_kernel, wires, cuts),
             [(shape, BF16), (shape, F32)],
-            act,
+            turned,
             three,
             flat_two,
             q,
@@ -464,9 +604,9 @@
             sums_two,
             g_sum,
             scratch=[((totals[0], LANES), F32), ((totals[2], LANES), F32)],
-            flops=2 * 9 * act.size * act.shape[-1],
+            flops=9 * three.size * three.shape[-1] // 2,
         )
-    flat_one, = call(kernel_grad, [((totals[0], LANES), F32)], act, three, flops=2 * 9 * act.size * act.shape[-1])
+    flat_one, = call(grad_kernel, [((totals[0], LANES), F32)], turned, three)
     flats = (flat_one, flat_two, (q * dc_sum).reshape(-1, LANES))
     blocks = jnp.concatenate([f.reshape(wires.n, rows, LANES) for f, rows in zip(flats, cuts)], axis=1)
     me = wires.me()
@@ -513,46 +653,40 @@
     line = ((1, channels), F32)
     pair = ((2, channels), F32)
     taps = ((18 * channels, LANES), F32)
+    padded = ((height + 2, width, channels), BF16)
+    turned = ((2, channels, pixels + 2 * width), BF16)
     conv_flops = 2 * 9 * pixels * channels * channels
 
     x, g = images[0], cotangent[0]
     stats, g_three, g_sum = call(prepare_kernel, [pair, three, line], x, g)
-    first, kernel_two, vec = gather(
-        wires, cuts, (conv_first, conv_second, projection), vectors, {wires.stages - 1: (g_sum,)}
-    )
-
     emb_float = embedding.astype(F32)
     emb_act = jax.nn.silu(emb_float).astype(BF16)
     q = emb_act.astype(F32).reshape(emb_width, 1)
-    act_one, centred, inv_two = call(
-        first_kernel, [maps, flat, line], x, stats, vec, emb_act, first, scratch=[three], flops=conv_flops
+    parts = (conv_first, conv_second, projection)
+    first, kernel_two, vec, time = gather(wires, cuts, parts, vectors, emb_act, {wires.stages - 1: (g_sum,)})
+
+    turned_one, raw, stats_two = call(
+        first_kernel, [turned, flat, pair], x, stats, vec, time, first, scratch=[three], flops=conv_flops
     )
-    dh_two, act_two, sums_two, grad_two = call(
+    act_two, sums_two, grad_two, e_three, dc_sum = call(
         second_kernel,
-        [flat, maps, pair, taps],
+        [padded, pair, taps, three, line],
         g_three,
-        centred,
-        inv_two,
+        raw,
+        stats_two,
         vec,
         kernel_two,
+        scratch=[flat, turned],
         flops=2 * conv_flops,
     )
-    e_three, dc_sum, dq, dh_one, sums_one = call(
-        middle_kernel,
-        [three, line, ((1, emb_width), F32), flat, pair],
-        dh_two,
-        centred,
-        inv_two,
-        sums_two,
-        x,
-        stats,
-        vec,
-        first,
-        flops=conv_flops,
+    dh_one, sums_one = call(third_kernel, [flat, pair], e_three, x, stats, vec, first, flops=conv_flops)
+    send, keep = pack(wires, cuts, turned_one, e_three, grad_two, q, dc_sum, sums_one, sums_two, g_sum)
+    input_grad, dq, input_done = call(
+        input_kernel, [(maps[0], F32), ((1, emb_width), F32), line], dh_one, x, g, stats, sums_one, vec, dc_sum, first
     )
-    send, keep = pack(wires, cuts, act_one, e_three, grad_two, q, dc_sum, sums_one, sums_two, g_sum)
-    input_grad, input_done = call(input_kernel, [(maps[0], F32), line], dh_one, x, g, stats, sums_one, vec)
-    output, output_done = call(last_kernel, [maps, line], act_two, x, vec, kernel_two, scratch=[three], flops=conv_flops)
+    output, output_done = call(
+        last_kernel, [maps, line], act_two, x, vec, kernel_two, scratch=[three], flops=conv_flops
+    )
     beside = {wires.stages - 1: (output_done,), wires.stages - 2: (input_done,)}
     summed = reduce_scatter(wires, cuts, n_vec, send, keep, beside)
     embedding_grad = dq * swish_slope(emb_float)

time: 112 us -> 103 us (0.920)
  Pallas kernels: 56.3 us -> 46.6 us
    pallas_call x17, Pallas kernels: 56.3 us -> 46.6 us  [call(): pl.pallas_call(run, out_shape=[jax.ShapeDtypeStruct(shape, dtype) for sha...]
  transfers between devices with their start and end apart: 10 -> 10, of which waited for: 10 -> 10; matrix products, arithmetic and copies ran while one was open for 1% -> 1% of each run, Pallas kernels for 12% -> 13%
where the time goes in v2:
time: 103 us
  Pallas kernels  46.6 us (45%)
  waiting for transfers between devices  31.2 us (30%)
  starting transfers between devices  16.9 us (16%)
  local copies, waits for them, and re-layouts  6.1 us (6%)
  other arithmetic  1.41 us (1%)
    pallas_call x17, Pallas kernels, call(): pl.pallas_call(run, out_shape=[jax.ShapeDtypeStruct(shape, dtype) for sha...  46.6 us
    ppermute x10, waiting for transfers between devices, swap(): lax.ppermute(value, AXES, [(i, i ^ 1 << bit(i)) for i in range(self.n)])  31.2 us
    ppermute x10, starting transfers between devices, swap(): lax.ppermute(value, AXES, [(i, i ^ 1 << bit(i)) for i in range(self.n)])  16.9 us
    unnamed x16, local copies, waits for them, and re-layouts  4.35 us
  transfers between devices with their start and end apart: 10, of which 10 were waited for; matrix products, arithmetic and copies ran while one was open for 1% of the time, Pallas kernels for 13%

profile of v2, /device:TPU:0, one launch (start us, length us, event | category | flops | bytes accessed | tf_op | source)
XLA Modules:
  0.0 103.1 jit_solution(16399330744977728513)
XLA Ops:
  2.3 4.0 %collective-permute-start = (bf16[336,128]{1,0:T(8,128)(2,1)S(1)}, bf16[336,128]{1,0:T(8,128)(2,1)S(1)}, u32[]{:S(2)}, u32[]{:S(2)}) collective-permute-start(bf16[336,128]{1,0:T(8,128)(2,1)S(1)} %pad_maximum_fusion.refs_0_), channel_id=1, source_target_pairs={{0,8},{1,9},{2,10},{3,11},{4,12},{5,13},{6,14},{7,15},{8,0},{9,1},... | collective-permute-start | bytes 258056 | tf_op jit(solution)/shard_map/ppermute | solution.py:33
  6.4 4.4 %collective-permute-done.refs_1_ = bf16[336,128]{1,0:T(8,128)(2,1)S(1)} collective-permute-done((bf16[336,128]{1,0:T(8,128)(2,1)S(1)}, bf16[336,128]{1,0:T(8,128)(2,1)S(1)}, u32[]{:S(2)}, u32[]{:S(2)}) %collective-permute-start) | collective-permute-done | bytes 86048 | tf_op jit(solution)/shard_map/ppermute | solution.py:33
  11.6 4.6 %collective-permute-done.1.refs_1_ = bf16[656,128]{1,0:T(8,128)(2,1)S(1)} collective-permute-done((bf16[656,128]{1,0:T(8,128)(2,1)S(1)}, bf16[656,128]{1,0:T(8,128)(2,1)S(1)}, u32[]{:S(2)}, u32[]{:S(2)}) %collective-permute-start.1) | collective-permute-done | bytes 167968 | tf_op jit(solution)/shard_map/ppermute | solution.py:33
  17.9 5.5 %collective-permute-done.2.refs_1_ = bf16[1296,128]{1,0:T(8,128)(2,1)S(1)} collective-permute-done((bf16[1296,128]{1,0:T(8,128)(2,1)S(1)}, bf16[1296,128]{1,0:T(8,128)(2,1)S(1)}, u32[]{:S(2)}, u32[]{:S(2)}) %collective-permute-start.2) | collective-permute-done | bytes 331808 | tf_op jit(solution)/shard_map/ppermute | solution.py:33
  23.5 1.9 %collective-permute-start.3 = (bf16[2576,128]{1,0:T(8,128)(2,1)S(1)}, bf16[2576,128]{1,0:T(8,128)(2,1)S(1)}, u32[]{:S(2)}, u32[]{:S(2)}) collective-permute-start(bf16[2576,128]{1,0:T(8,128)(2,1)S(1)} %shard_map.129.refs_0_), channel_id=1, source_target_pairs={{0,16},{1,3},{2,18},{3,1},{4,20},{5,7},{6,22},{7,5},{8,24},{9,11},... | collective-permute-start | bytes 1978376 | tf_op jit(solution)/shard_map/ppermute | solution.py:33
  27.0 2.6 %shard_map.126 = (f32[2,256]{1,0:T(2,128)S(1)}, bf16[3,66,64,256]{3,2,1,0:T(8,128)(2,1)S(1)}, f32[1,256]{1,0:T(1,128)S(1)}) custom-call(bf16[64,64,256]{2,1,0:T(8,128)(2,1)S(1)} %bitcast.16, bf16[64,64,256]{2,1,0:T(8,128)(2,1)S(1)} %bitcast.21), custom_call_target="tpu_custom_call" | custom-call | bytes 4194304 | tf_op jit(solution)/shard_map/pallas_call | solution.py:541
  29.6 2.7 %copy-done.4 = bf16[3,66,64,256]{3,2,1,0:T(8,128)(2,1)} copy-done((bf16[3,66,64,256]{3,2,1,0:T(8,128)(2,1)}, bf16[3,66,64,256]{3,2,1,0:T(8,128)(2,1)S(1)}, u32[]{:S(2)}) %copy-start.4) | copy-done | bytes 6488088
  32.4 1.9 %collective-permute-done.3.refs_1_ = bf16[2576,128]{1,0:T(8,128)(2,1)S(1)} collective-permute-done((bf16[2576,128]{1,0:T(8,128)(2,1)S(1)}, bf16[2576,128]{1,0:T(8,128)(2,1)S(1)}, u32[]{:S(2)}, u32[]{:S(2)}) %collective-permute-start.3) | collective-permute-done | bytes 659488 | tf_op jit(solution)/shard_map/ppermute | solution.py:33
  35.3 2.3 %collective-permute-done.4.refs_1_ = bf16[5136,128]{1,0:T(8,128)(2,1)} collective-permute-done((bf16[5136,128]{1,0:T(8,128)(2,1)S(1)}, bf16[5136,128]{1,0:T(8,128)(2,1)}, u32[]{:S(2)}, u32[]{:S(2)}) %collective-permute-start.4) | collective-permute-done | bytes 1314848 | tf_op jit(solution)/shard_map/ppermute | solution.py:33
  37.5 2.2 %shard_map.131 = (bf16[2816,256]{1,0:T(8,128)(2,1)S(1)}, bf16[2304,256]{1,0:T(8,128)(2,1)S(1)}, f32[8,256]{1,0:T(8,128)S(1)}, f32[1,256]{1,0:T(1,128)S(1)}) custom-call(bf16[5136,128]{1,0:T(8,128)(2,1)S(1)} %shard_map.130.refs_0_, bf16[5136,128]{1,0:T(8,128)(2,1)} %collective-permute-done.4.refs_1_, bf16[1,512]{1,0:T(2,128)(2,1)S(1)} %get-tuple-element.80.refs_2_), custom_call_target="tpu_custom_call" | custom-call | bytes 4194304 | tf_op jit(solution)/shard_map/pallas_call | solution.py:541
  39.8 6.4 %shard_map.132 = (bf16[2,256,4224]{2,1,0:T(8,128)(2,1)S(1)}, f32[4096,256]{1,0:T(8,128)S(1)}, f32[2,256]{1,0:T(2,128)S(1)}) custom-call(bf16[64,64,256]{2,1,0:T(8,128)(2,1)S(1)} %bitcast.17, f32[2,256]{1,0:T(2,128)S(1)} %get-tuple-element.44.refs_1_.refs_2_.refs_3_, f32[8,256]{1,0:T(8,128)S(1)} %get-tuple-element.46.refs_2_.refs_3_.refs_5_, ...), custom_call_target="tpu_custom_call" | custom-call | flops 4831838208 | bytes 4194304 | tf_op jit(solution)/shard_map/pallas_call | solution.py:541
  46.2 12.1 %shard_map.133 = (bf16[66,64,256]{2,1,0:T(8,128)(2,1)S(1)}, f32[2,256]{1,0:T(2,128)S(1)}, f32[4608,128]{1,0:T(8,128)S(1)}, bf16[3,66,64,256]{3,2,1,0:T(8,128)(2,1)S(1)}, f32[1,256]{1,0:T(1,128)S(1)}) custom-call(bf16[3,66,64,256]{3,2,1,0:T(8,128)(2,1)S(1)} %bitcast.24, f32[4096,256]{1,0:T(8,128)S(1)} %get-tuple-element.49.refs_1_, ...), custom_call_target="tpu_custom_call" | custom-call | flops 9663676416 | bytes 4194304 | tf_op jit(solution)/shard_map/pallas_call | solution.py:541
  58.3 6.2 %shard_map.135 = (f32[4096,256]{1,0:T(8,128)S(1)}, f32[2,256]{1,0:T(2,128)S(1)}) custom-call(bf16[3,66,64,256]{3,2,1,0:T(8,128)(2,1)S(1)} %get-tuple-element.54.refs_0_.refs_1_, bf16[64,64,256]{2,1,0:T(8,128)(2,1)S(1)} %bitcast.18, f32[2,256]{1,0:T(2,128)S(1)} %get-tuple-element.44.refs_1_.refs_2_.refs_3_, ...), custom_call_target="tpu_custom_call" | custom-call | flops 4831838208 | bytes 4194304 | tf_op jit(solution)/shard_map/pallas_call | solution.py:541
  64.6 5.3 %shard_map.137 = (bf16[5136,128]{1,0:T(8,128)(2,1)S(1)}, f32[5136,128]{1,0:T(8,128)S(1)}) custom-call(bf16[2,256,4224]{2,1,0:T(8,128)(2,1)S(1)} %get-tuple-element.60.refs_0_, bf16[3,66,64,256]{3,2,1,0:T(8,128)(2,1)S(1)} %get-tuple-element.54.refs_0_.refs_1_, f32[4608,128]{1,0:T(8,128)S(1)} %get-tuple-element.61.refs_2_, f32[512,1]{1,0:T(8,128)S(1)} %copy-done.3, ...), custom_call_target="tpu_custom_call" | custom-call | flops 3737124864 | bytes 4194304 | tf_op jit(solution)/shard_map/pallas_call | solution.py:541
  70.0 2.9 %collective-permute-done.5.refs_1_ = bf16[5136,128]{1,0:T(8,128)(2,1)S(1)} collective-permute-done((bf16[5136,128]{1,0:T(8,128)(2,1)S(1)}, bf16[5136,128]{1,0:T(8,128)(2,1)S(1)}, u32[]{:S(2)}, u32[]{:S(2)}) %collective-permute-start.5) | collective-permute-done | bytes 1314848 | tf_op jit(solution)/shard_map/ppermute | solution.py:33
  73.3 1.9 %collective-permute-start.6 = (bf16[2576,128]{1,0:T(8,128)(2,1)S(1)}, bf16[2576,128]{1,0:T(8,128)(2,1)S(1)}, u32[]{:S(2)}, u32[]{:S(2)}) collective-permute-start(bf16[2576,128]{1,0:T(8,128)(2,1)S(1)} %get-tuple-element.66), channel_id=1, source_target_pairs={{0,16},{1,3},{2,18},{3,1},{4,20},{5,7},{6,22},{7,5},{8,24},{9,11},... | collective-permute-start | bytes 1978376 | tf_op jit(solution)/shard_map/ppermute | solution.py:33
  75.1 6.8 %shard_map.134 = (bf16[64,64,256]{2,1,0:T(8,128)(2,1)}, f32[1,256]{1,0:T(1,128)S(1)}) custom-call(bf16[66,64,256]{2,1,0:T(8,128)(2,1)S(1)} %get-tuple-element.52.refs_0_, bf16[64,64,256]{2,1,0:T(8,128)(2,1)S(1)} %bitcast.19, f32[8,256]{1,0:T(8,128)S(1)} %get-tuple-element.46.refs_2_.refs_3_.refs_5_, bf16[2304,256]{1,0:T(8,128)(2,1)S(1)} %get-tuple-element.51.refs_4_.refs_3_), custom_call_target="tpu_custom_call" | custom-call | flops 4831838208 | bytes 4194304 | tf_op jit(solution)/shard_map/pallas_call | solution.py:541
  82.0 2.0 %collective-permute-done.6.refs_1_ = bf16[2576,128]{1,0:T(8,128)(2,1)S(1)} collective-permute-done((bf16[2576,128]{1,0:T(8,128)(2,1)S(1)}, bf16[2576,128]{1,0:T(8,128)(2,1)S(1)}, u32[]{:S(2)}, u32[]{:S(2)}) %collective-permute-start.6) | collective-permute-done | bytes 659488 | tf_op jit(solution)/shard_map/ppermute | solution.py:33
  84.1 1.8 %collective-permute-start.7 = (bf16[1296,128]{1,0:T(8,128)(2,1)S(1)}, bf16[1296,128]{1,0:T(8,128)(2,1)S(1)}, u32[]{:S(2)}, u32[]{:S(2)}) collective-permute-start(bf16[1296,128]{1,0:T(8,128)(2,1)S(1)} %get-tuple-element.69), channel_id=1, source_target_pairs={{0,2},{1,17},{2,0},{3,19},{4,6},{5,21},{6,4},{7,23},{8,10},{9,25},... | collective-permute-start | bytes 995336 | tf_op jit(solution)/shard_map/ppermute | solution.py:33
  86.0 3.5 %shard_map.136 = (f32[64,64,256]{2,1,0:T(8,128)}, f32[1,512]{1,0:T(1,128)S(1)}, f32[1,256]{1,0:T(1,128)S(1)}) custom-call(f32[4096,256]{1,0:T(8,128)S(1)} %get-tuple-element.55.refs_0_, bf16[64,64,256]{2,1,0:T(8,128)(2,1)S(1)} %bitcast.20, bf16[64,64,256]{2,1,0:T(8,128)(2,1)S(1)} %bitcast.22, f32[2,256]{1,0:T(2,128)S(1)} %get-tuple-element.44.refs_1_.refs_2_.refs_3_, ...), custom_call_target="tpu_custom_call" | custom-call | bytes 4194304 | tf_op jit(solution)/shard_map/pallas_call | solution.py:541
  89.5 1.8 %collective-permute-done.7.refs_1_ = bf16[1296,128]{1,0:T(8,128)(2,1)S(1)} collective-permute-done((bf16[1296,128]{1,0:T(8,128)(2,1)S(1)}, bf16[1296,128]{1,0:T(8,128)(2,1)S(1)}, u32[]{:S(2)}, u32[]{:S(2)}) %collective-permute-start.7) | collective-permute-done | bytes 331808 | tf_op jit(solution)/shard_map/ppermute | solution.py:33
  92.8 4.0 %collective-permute-done.8.refs_1_ = bf16[656,128]{1,0:T(8,128)(2,1)S(1)} collective-permute-done((bf16[656,128]{1,0:T(8,128)(2,1)S(1)}, bf16[656,128]{1,0:T(8,128)(2,1)S(1)}, u32[]{:S(2)}, u32[]{:S(2)}) %collective-permute-start.8) | collective-permute-done | bytes 167968 | tf_op jit(solution)/shard_map/ppermute | solution.py:33
  96.9 3.1 %collective-permute-start.9 = (bf16[336,128]{1,0:T(8,128)(2,1)S(1)}, bf16[336,128]{1,0:T(8,128)(2,1)S(1)}, u32[]{:S(2)}, u32[]{:S(2)}) collective-permute-start(bf16[336,128]{1,0:T(8,128)(2,1)S(1)} %get-tuple-element.74), channel_id=1, source_target_pairs={{0,8},{1,9},{2,10},{3,11},{4,12},{5,13},{6,14},{7,15},{8,0},{9,1},... | collective-permute-start | bytes 258056 | tf_op jit(solution)/shard_map/ppermute | solution.py:33
  100.5 1.9 %collective-permute-done.9.refs_1_ = bf16[336,128]{1,0:T(8,128)(2,1)S(1)} collective-permute-done((bf16[336,128]{1,0:T(8,128)(2,1)S(1)}, bf16[336,128]{1,0:T(8,128)(2,1)S(1)}, u32[]{:S(2)}, u32[]{:S(2)}) %collective-permute-start.9) | collective-permute-done | bytes 86048 | tf_op jit(solution)/shard_map/ppermute | solution.py:33
  (35 shorter events, 10.4 us)
Async XLA Ops:
  0.6 24.8 %copy-start = (bf16[1,64,64,256]{3,2,1,0:T(8,128)(2,1)S(1)}, bf16[1,64,64,256]{3,2,1,0:T(8,128)(2,1)}, u32[]{:S(2)}) copy-start(bf16[1,64,64,256]{3,2,1,0:T(8,128)(2,1)} %param.7) | copy-start | bytes 6291460
  2.3 8.4 %collective-permute-start = (bf16[336,128]{1,0:T(8,128)(2,1)S(1)}, bf16[336,128]{1,0:T(8,128)(2,1)S(1)}, u32[]{:S(2)}, u32[]{:S(2)}) collective-permute-start(bf16[336,128]{1,0:T(8,128)(2,1)S(1)} %pad_maximum_fusion.refs_0_), channel_id=1, source_target_pairs={{0,8},{1,9},{2,10},{3,11},{4,12},{5,13},{6,14},{7,15},{8,0},{9,1},... | collective-permute-start | bytes 258056 | tf_op jit(solution)/shard_map/ppermute | solution.py:33
  10.8 5.4 %collective-permute-start.1 = (bf16[656,128]{1,0:T(8,128)(2,1)S(1)}, bf16[656,128]{1,0:T(8,128)(2,1)S(1)}, u32[]{:S(2)}, u32[]{:S(2)}) collective-permute-start(bf16[656,128]{1,0:T(8,128)(2,1)S(1)} %shard_map.127.refs_0_), channel_id=1, source_target_pairs={{0,4},{1,5},{2,6},{3,7},{4,0},{5,1},{6,2},{7,3},{8,12},{9,13},{10,... | collective-permute-start | bytes 503816 | tf_op jit(solution)/shard_map/ppermute | solution.py:33
  16.2 7.2 %collective-permute-start.2 = (bf16[1296,128]{1,0:T(8,128)(2,1)S(1)}, bf16[1296,128]{1,0:T(8,128)(2,1)S(1)}, u32[]{:S(2)}, u32[]{:S(2)}) collective-permute-start(bf16[1296,128]{1,0:T(8,128)(2,1)S(1)} %shard_map.128.refs_0_), channel_id=1, source_target_pairs={{0,2},{1,17},{2,0},{3,19},{4,6},{5,21},{6,4},{7,23},{8,10},{9,25},... | collective-permute-start | bytes 995336 | tf_op jit(solution)/shard_map/ppermute | solution.py:33
  23.5 10.7 %collective-permute-start.3 = (bf16[2576,128]{1,0:T(8,128)(2,1)S(1)}, bf16[2576,128]{1,0:T(8,128)(2,1)S(1)}, u32[]{:S(2)}, u32[]{:S(2)}) collective-permute-start(bf16[2576,128]{1,0:T(8,128)(2,1)S(1)} %shard_map.129.refs_0_), channel_id=1, source_target_pairs={{0,16},{1,3},{2,18},{3,1},{4,20},{5,7},{6,22},{7,5},{8,24},{9,11},... | collective-permute-start | bytes 1978376 | tf_op jit(solution)/shard_map/ppermute | solution.py:33
  25.4 1.6 %copy-start.1 = (bf16[1,64,64,256]{3,2,1,0:T(8,128)(2,1)S(1)}, bf16[1,64,64,256]{3,2,1,0:T(8,128)(2,1)}, u32[]{:S(2)}) copy-start(bf16[1,64,64,256]{3,2,1,0:T(8,128)(2,1)} %param.13) | copy-start | bytes 6291460
  29.6 2.7 %copy-start.4 = (bf16[3,66,64,256]{3,2,1,0:T(8,128)(2,1)}, bf16[3,66,64,256]{3,2,1,0:T(8,128)(2,1)S(1)}, u32[]{:S(2)}) copy-start(bf16[3,66,64,256]{3,2,1,0:T(8,128)(2,1)S(1)} %get-tuple-element.43.refs_0_) | copy-start | bytes 19464196
  32.4 2.0 %copy-start.5 = (bf16[1,512]{1,0:T(2,128)(2,1)S(1)}, bf16[1,512]{1,0:T(2,128)(2,1)}, u32[]{:S(2)}) copy-start(bf16[1,512]{1,0:T(2,128)(2,1)} %param.8) | copy-start | bytes 3076
  34.3 3.2 %collective-permute-start.4 = (bf16[5136,128]{1,0:T(8,128)(2,1)S(1)}, bf16[5136,128]{1,0:T(8,128)(2,1)}, u32[]{:S(2)}, u32[]{:S(2)}) collective-permute-start(bf16[5136,128]{1,0:T(8,128)(2,1)S(1)} %shard_map.130.refs_0_), channel_id=1, source_target_pairs={{0,1},{1,0},{2,3},{3,2},{4,5},{5,4},{6,7},{7,6},{8,9},{9,8},{10,11... | collective-permute-start | bytes 3944456 | tf_op jit(solution)/shard_map/ppermute | solution.py:33
  37.5 8.6 %slice-start = ((s8[6488064]{0:T(1024)(128)(4,1)}), s8[4194304]{0:T(1024)(128)(4,1)S(1)}, s32[]{:S(2)}) async-start(s8[6488064]{0:T(1024)(128)(4,1)} %bitcast.23), calls=%async_computation | async-start | bytes 8388608
  39.8 6.4 %slice-start.1 = ((s8[6488064]{0:T(1024)(128)(4,1)}), s8[2293760]{0:T(1024)(128)(4,1)S(1)}, s32[]{:S(2)}) async-start(s8[6488064]{0:T(1024)(128)(4,1)} %bitcast.23), calls=%async_computation.1 | async-start | bytes 4587520
  58.3 6.2 %copy-start.3 = (f32[512,1]{1,0:T(8,128)S(1)}, f32[512,1]{1,0:T(8,128)}, u32[]{:S(2)}) copy-start(f32[512,1]{1,0:T(8,128)} %copy.14.refs_3_) | copy-start | bytes 6148
  69.9 3.1 %collective-permute-start.5 = (bf16[5136,128]{1,0:T(8,128)(2,1)S(1)}, bf16[5136,128]{1,0:T(8,128)(2,1)S(1)}, u32[]{:S(2)}, u32[]{:S(2)}) collective-permute-start(bf16[5136,128]{1,0:T(8,128)(2,1)S(1)} %get-tuple-element.64), channel_id=1, source_target_pairs={{0,1},{1,0},{2,3},{3,2},{4,5},{5,4},{6,7},{7,6},{8,9},{9,8},{10,11... | collective-permute-start | bytes 3944456 | tf_op jit(solution)/shard_map/ppermute | solution.py:33
  73.3 10.7 %collective-permute-start.6 = (bf16[2576,128]{1,0:T(8,128)(2,1)S(1)}, bf16[2576,128]{1,0:T(8,128)(2,1)S(1)}, u32[]{:S(2)}, u32[]{:S(2)}) collective-permute-start(bf16[2576,128]{1,0:T(8,128)(2,1)S(1)} %get-tuple-element.66), channel_id=1, source_target_pairs={{0,16},{1,3},{2,18},{3,1},{4,20},{5,7},{6,22},{7,5},{8,24},{9,11},... | collective-permute-start | bytes 1978376 | tf_op jit(solution)/shard_map/ppermute | solution.py:33
  75.1 10.8 %copy-start.2 = (bf16[1,64,64,256]{3,2,1,0:T(8,128)(2,1)S(1)}, bf16[1,64,64,256]{3,2,1,0:T(8,128)(2,1)}, u32[]{:S(2)}) copy-start(bf16[1,64,64,256]{3,2,1,0:T(8,128)(2,1)} %param.13) | copy-start | bytes 6291460
  84.1 7.2 %collective-permute-start.7 = (bf16[1296,128]{1,0:T(8,128)(2,1)S(1)}, bf16[1296,128]{1,0:T(8,128)(2,1)S(1)}, u32[]{:S(2)}, u32[]{:S(2)}) collective-permute-start(bf16[1296,128]{1,0:T(8,128)(2,1)S(1)} %get-tuple-element.69), channel_id=1, source_target_pairs={{0,2},{1,17},{2,0},{3,19},{4,6},{5,21},{6,4},{7,23},{8,10},{9,25},... | collective-permute-start | bytes 995336 | tf_op jit(solution)/shard_map/ppermute | solution.py:33
  91.4 5.4 %collective-permute-start.8 = (bf16[656,128]{1,0:T(8,128)(2,1)S(1)}, bf16[656,128]{1,0:T(8,128)(2,1)S(1)}, u32[]{:S(2)}, u32[]{:S(2)}) collective-permute-start(bf16[656,128]{1,0:T(8,128)(2,1)S(1)} %get-tuple-element.72), channel_id=1, source_target_pairs={{0,4},{1,5},{2,6},{3,7},{4,0},{5,1},{6,2},{7,3},{8,12},{9,13},{10,... | collective-permute-start | bytes 503816 | tf_op jit(solution)/shard_map/ppermute | solution.py:33
  96.9 5.6 %collective-permute-start.9 = (bf16[336,128]{1,0:T(8,128)(2,1)S(1)}, bf16[336,128]{1,0:T(8,128)(2,1)S(1)}, u32[]{:S(2)}, u32[]{:S(2)}) collective-permute-start(bf16[336,128]{1,0:T(8,128)(2,1)S(1)} %get-tuple-element.74), channel_id=1, source_target_pairs={{0,8},{1,9},{2,10},{3,11},{4,12},{5,13},{6,14},{7,15},{8,0},{9,1},... | collective-permute-start | bytes 258056 | tf_op jit(solution)/shard_map/ppermute | solution.py:33

commit v3 on v2

--- a/solution.py
+++ b/solution.py
@@ -21,24 +21,37 @@
         self.n = n_dp * n_fsdp
         self.bits = int(math.log2(self.n))
         fsdp_bits = int(math.log2(n_fsdp))
-        assert 1 << self.bits == self.n and 1 << fsdp_bits == n_fsdp and fsdp_bits >= 2 and n_dp >= 2
+        assert 1 << self.bits == self.n and 1 << fsdp_bits == n_fsdp and fsdp_bits >= 3 and n_dp >= 2
         a, b = 1, fsdp_bits
         far = [bit for bit in range(self.bits - 1, 0, -1) if bit not in (a, b)]
-        self.order = {0: [*far, a, b], 1: [*far, b, a]}
+        self.far = len(far)
+        self.order = {0: [*far, a, b], 1: [*far[::-1], b, a]}
         self.stages = self.bits - 1
         self.slots = 1 << self.stages
 
-    def swap(self, value, stage):
-        bit = (lambda i: 0) if stage == self.stages else (lambda i: self.order[i & 1][stage])
-        return lax.ppermute(value, AXES, [(i, i ^ (1 << bit(i))) for i in range(self.n)])
-
-    def mask(self, slot, core):
-        return sum(1 << self.order[core][i] for i in range(self.stages) if slot >> i & 1)
+    def swap(self, value, stage, turned=0):
+        def bit(core):
+            return 0 if stage == self.stages else self.bit_of(stage, core, turned)
+
+        return lax.ppermute(value, AXES, [(i, i ^ (1 << bit(i & 1))) for i in range(self.n)])
+
+    def bit_of(self, stage, core, turned):
+        return self.order[core ^ turned if stage >= self.far else core][stage]
+
+    def mask(self, slot, core, turned):
+        return sum(1 << self.bit_of(i, core, turned) for i in range(self.stages) if slot >> i & 1)
 
     def me(self):
         return lax.axis_index("dp") * self.n_fsdp + lax.axis_index("fsdp")
 
-    def owner(self, slot, other, me):
+    def owner(self, slot, other, me, turned=0):
+        core = me & 1
+        if other:
+            me, core = me ^ 1, 1 - core
+        return me ^ jnp.where(core == 0, self.mask(slot, 0, turned), self.mask(slot, 1, turned))
+
+
+def owner(self, slot, other, me):
         core = me & 1
         if other:
             me, core = me ^ 1, 1 - core
@@ -247,23 +260,22 @@
     return jnp.concatenate([left, right], axis=1)
 
 
-def prepare_kernel(x, g, stats, three, g_sum):
+def stats_kernel(x_hbm, stats, x, arrived):
     height, width, channels = x.shape
     count = height * width * (channels // GROUPS)
     zero = jnp.zeros((8, channels), F32)
-    clear_edges(three)
-
-    def first(i, carry):
-        s, gs = carry
-        row = i * 4
-        s = s + fold(x[pl.ds(row, 4)].astype(F32))
-        rows = g[pl.ds(row, 4)].astype(F32)
-        for j in range(4):
-            store_three(three, row + j, rows[j])
-        return s, gs + fold(rows)
-
-    s, gs = lax.fori_loop(0, height // 4, first, (zero, zero))
-    g_sum[...] = total(gs)
+    parts = arrived.shape[0]
+    rows = height // parts
+    copies = [
+        pltpu.make_async_copy(x_hbm.at[pl.ds(k * rows, rows)], x.at[pl.ds(k * rows, rows)], arrived.at[k])
+        for k in range(parts)
+    ]
+    for copy in copies:
+        copy.start()
+    s = zero
+    for k, copy in enumerate(copies):
+        copy.wait()
+        s = lax.fori_loop(0, rows // 4, lambda i, s, k=k: s + fold(x[pl.ds(k * rows + i * 4, 4)].astype(F32)), s)
     mean = group_sum(total(s)) / count
 
     def second(i, v):
@@ -274,6 +286,40 @@
     inv = lax.rsqrt(group_sum(total(v)) / count + EPS)
     stats[0:1, :] = mean
     stats[1:2, :] = inv
+
+
+def spread_kernel(g_hbm, three_hbm, g_sum, g, three, arrived, left):
+    height, width, channels = g.shape
+    parts = arrived.shape[0]
+    rows = height // parts
+    copies = [
+        pltpu.make_async_copy(g_hbm.at[pl.ds(k * rows, rows)], g.at[pl.ds(k * rows, rows)], arrived.at[k])
+        for k in range(parts)
+    ]
+    for copy in copies:
+        copy.start()
+    clear_edges(three)
+    s = jnp.zeros((8, channels), F32)
+    out = []
+    for k, copy in enumerate(copies):
+        copy.wait()
+
+        def step(i, s, k=k):
+            row = k * rows + i * 4
+            values = g[pl.ds(row, 4)].astype(F32)
+            for j in range(4):
+                store_three(three, row + j, values[j])
+            return s + fold(values)
+
+        s = lax.fori_loop(0, rows // 4, step, s)
+        start = k * rows + (1 if k else 0)
+        size = rows + (1 if k == 0 else 0) + (1 if k == parts - 1 else 0)
+        away = pltpu.make_async_copy(three.at[:, pl.ds(start, size)], three_hbm.at[:, pl.ds(start, size)], left.at[k])
+        away.start()
+        out.append(away)
+    g_sum[...] = total(s)
+    for away in out:
+        away.wait()
 
 
 def first_kernel(x, stats, vec, time, kernel, turned, raw, stats_out, three):
@@ -393,7 +439,7 @@
     sums[1:2, :] = s
 
 
-def input_kernel(dh, x, g, stats, sums, vec, dc_sum, kernel, result, dq, done):
+def input_kernel(dh, x, g, stats, sums, vec, dc_sum, kernel, embedding, result, emb_grad, done):
     height, width, channels = x.shape
     count = height * width * (channels // GROUPS)
     mean, inv, gain = stats[0:1, :], stats[1:2, :], vec[0:1, :]
@@ -409,116 +455,202 @@
         return 0
 
     lax.fori_loop(0, height // 4, back, 0)
-    dq[...] = lax.dot_general(
+    dq = lax.dot_general(
         dc_sum[...],
         kernel[9 * channels :, :].astype(F32),
         (((1,), (1,)), ((), ())),
         precision=lax.Precision.HIGHEST,
         preferred_element_type=F32,
     )
+    emb = embedding[...].astype(F32)
+    sig = sigmoid(emb)
+    emb_grad[...] = dq * (sig * (1.0 + emb * (1.0 - sig)))
     done[...] = base
 
 
-def last_kernel(act, x, vec, kernel, result, done, three):
-    accumulators(last_body, act, x, vec, kernel, result, done, three)
-
-
-def last_body(act, x, vec, kernel, result, done, three, accs):
+def last_kernel(part, parts, *refs):
+    accumulators(functools.partial(last_body, part, parts), *refs)
+
+
+def last_body(part, parts, act, x, vec, kernel, *refs):
+    out, done, three, result, left, accs = refs[-6:]
     height = x.shape[0]
+    rows = height // parts
+    base = part * rows
     bias = vec[5:6, :]
-    clear_edges(three)
 
     def spread(row):
-        store_three(three, row, act[row + 1].astype(F32))
+        if 0 <= base + row < height:
+            store_three(three, row, act[base + row + 1].astype(F32))
+        else:
+            three[:, row + 1 : row + 2] = jnp.zeros((3, 1) + three.shape[2:], BF16)
 
     def use(row, v):
-        result[row] = (x[row].astype(F32) + v + bias).astype(BF16)
+        result[row] = (x[base + row].astype(F32) + v + bias).astype(BF16)
 
     per_step = UNITS * ROWS
-    steps = height // per_step
-    for row in range(per_step + 1):
+    steps = rows // per_step
+    copies = []
+
+    def send(step):
+        here = pl.ds(step * per_step, per_step)
+        copies.append(pltpu.make_async_copy(result.at[here], out.at[pl.ds(base + step * per_step, per_step)], left.at[step]))
+        copies[-1].start()
+
+    for row in range(-1, per_step + 1):
         spread(row)
     for step in range(steps):
-        ahead = range((step + 1) * per_step + 1, min((step + 2) * per_step + 1, height))
+        ahead = range((step + 1) * per_step + 1, min((step + 2) * per_step, rows) + 1)
         others = [functools.partial(spread, row) for row in ahead]
         done_rows = conv_rows(accs, step - 1, (step - 1) % 2, use) if step else []
         mixed = [f for i in range(per_step) for f in (*others[i : i + 1], *done_rows[i : i + 1])]
         conv_step(accs, three, kernel, step, step % 2, False, mixed)
+        if step:
+            send(step - 1)
     for other in conv_rows(accs, steps - 1, (steps - 1) % 2, use):
         other()
+    send(steps - 1)
     done[...] = bias
-
-
-def join_kernel(mine, got, out):
-    rows = mine.shape[0] - VEC_ROWS
+    for copy in copies:
+        copy.wait()
+
+
+def join_kernel(mine, got, out, tail=VEC_ROWS):
+    rows = mine.shape[0] - tail
     out[0:rows, :] = mine[0:rows, :]
     out[rows : 2 * rows, :] = got[0:rows, :]
-    out[2 * rows : 2 * rows + VEC_ROWS, :] = mine[rows : rows + VEC_ROWS, :] + got[rows : rows + VEC_ROWS, :]
-
-
-def halve_kernel(keep, got, send_next, keep_next):
-    rows = (keep.shape[0] - VEC_ROWS) // 2
+    if tail:
+        out[2 * rows :, :] = mine[rows:, :] + got[rows:, :]
+
+
+def join_both_kernel(first, first_got, second, second_got, first_out, second_out):
+    join_kernel(first, first_got, first_out)
+    join_kernel(second, second_got, second_out, 0)
+
+
+def part_kernel(cuts, mine, got, first, second):
+    block, cut = sum(cuts), sum(cuts[:-1])
+    slots = (mine.shape[0] - VEC_ROWS) // block
+    for half, source in enumerate((mine, got)):
+        for slot in range(slots):
+            at, to = slot * block, half * slots + slot
+            first[to * cut : (to + 1) * cut, :] = source[at : at + cut, :]
+            second[to * cuts[-1] : (to + 1) * cuts[-1], :] = source[at + cut : at + block, :]
+    first[2 * slots * cut :, :] = mine[slots * block :, :] + got[slots * block :, :]
+
+
+def halve_kernel(keep, got, send_next, keep_next, tail=VEC_ROWS):
+    rows = (keep.shape[0] - tail) // 2
     keep_next[0:rows, :] = keep[0:rows, :] + got[0:rows, :].astype(F32)
     send_next[0:rows, :] = (keep[rows : 2 * rows, :] + got[rows : 2 * rows, :].astype(F32)).astype(BF16)
-    vec = keep[2 * rows : 2 * rows + VEC_ROWS, :] + got[2 * rows : 2 * rows + VEC_ROWS, :].astype(F32)
-    keep_next[rows : rows + VEC_ROWS, :] = vec
-    send_next[rows : rows + VEC_ROWS, :] = vec.astype(BF16)
-
-
-def arrange_kernel(wires, cuts, mine, got, q, first, kernel_two, vec, time, flat_one, flat_two, flat_project, flat_vec):
+    if tail:
+        vec = keep[2 * rows :, :] + got[2 * rows :, :].astype(F32)
+        keep_next[rows:, :] = vec
+        send_next[rows:, :] = vec.astype(BF16)
+
+
+def halve_second_kernel(keep, got, send_next, keep_next):
+    halve_kernel(keep, got, send_next, keep_next, 0)
+
+
+def merge_kernel(wide, narrow, one, one_got, two_send, two, send, keep):
+    slots = two.shape[0] // narrow
+    for slot in range(slots):
+        to = slot * (wide + narrow)
+        at, up = slot * wide, (slots + slot) * wide
+        keep[to : to + wide, :] = one[at : at + wide, :] + one_got[at : at + wide, :].astype(F32)
+        send[to : to + wide, :] = (one[up : up + wide, :] + one_got[up : up + wide, :].astype(F32)).astype(BF16)
+        at, to, up = slot * narrow, to + wide, to + wide + narrow
+        keep[to:up, :] = two[at : at + narrow, :]
+        send[to:up, :] = two_send[at : at + narrow, :]
+    at, to = 2 * slots * wide, slots * (wide + narrow)
+    values = one[at:, :] + one_got[at:, :].astype(F32)
+    keep[to:, :] = values
+    send[to:, :] = values.astype(BF16)
+
+
+def place_blocks(wires, cuts, mine, got, flats, turned=0):
     me = wires.me()
     block = sum(cuts)
-    flats = (flat_one, flat_two, flat_project)
     for slot in range(wires.slots):
         for other, source in ((False, mine), (True, got)):
-            owner = wires.owner(slot, other, me)
+            owner = wires.owner(slot, other, me, turned)
             values = source[slot * block : (slot + 1) * block, :].astype(F32)
             at = 0
             for flat, rows in zip(flats, cuts):
                 flat[pl.ds(pl.multiple_of(owner * rows, rows), rows), :] = values[at : at + rows]
                 at += rows
+
+
+def unflatten(flat, out, base):
+    for start in range(0, flat.shape[0] // 2, 256):
+        out[base + start : base + start + 256, :] = load_flat(flat, 2 * start, 256).astype(BF16)
+
+
+def arrange_first_kernel(wires, cuts, mine, got, embedding, first, vec, time, flat_one, flat_project, flat_vec):
+    place_blocks(wires, cuts, mine, got, (flat_one, flat_project))
     rows_one = flat_one.shape[0] // 2
-    for flat, out, base in ((flat_one, first, 0), (flat_two, kernel_two, 0), (flat_project, first, rows_one)):
-        for start in range(0, flat.shape[0] // 2, 256):
-            out[base + start : base + start + 256, :] = load_flat(flat, 2 * start, 256).astype(BF16)
-    at = wires.slots * block
+    unflatten(flat_project, first, rows_one)
+    emb = embedding[...].astype(F32)
+    act = (emb * sigmoid(emb)).astype(BF16)
+    time[...] = jnp.dot(act, first[rows_one:, :], preferred_element_type=F32)
+    unflatten(flat_one, first, 0)
+    at = wires.slots * sum(cuts)
     flat_vec[...] = mine[at : at + VEC_ROWS, :].astype(F32) + got[at : at + VEC_ROWS, :].astype(F32)
     vec[...] = load_flat(flat_vec, 0, VEC_ROWS // 2)
-    time[...] = jnp.dot(q[...], first[rows_one:, :], preferred_element_type=F32)
+
+
+def arrange_second_kernel(wires, cuts, mine, got, second, flat_two):
+    place_blocks(wires, cuts, mine, got, (flat_two,), 1)
+    unflatten(flat_two, second, 0)
 
 
 def grad_kernel(turned, three, flat):
     accumulators(lambda *refs: kernel_grad(refs[-1], *refs[:-1], None, 0), turned, three, flat)
 
 
-def pack_kernel(wires, cuts, turned, three, flat_two, q, dc_sum, sums_one, sums_two, g_sum, send, keep, flat_one, flat_project):
+def take_blocks(wires, cuts, flats, send, keep):
     me = wires.me()
     block = sum(cuts)
-    grad_kernel(turned, three, flat_one)
-    for start in range(0, q.shape[0], 256):
-        store_flat(flat_project, 2 * start, q[start : start + 256, :] * dc_sum[...])
     for slot in range(wires.slots):
         for other in (True, False):
             owner = wires.owner(slot, other, me)
             at = slot * block
-            for flat, rows in zip((flat_one, flat_two, flat_project), cuts):
+            for flat, rows in zip(flats, cuts):
                 values = flat[pl.ds(pl.multiple_of(owner * rows, rows), rows), :]
                 if other:
                     send[at : at + rows, :] = values.astype(BF16)
                 else:
                     keep[at : at + rows, :] = values
                 at += rows
-    at = wires.slots * block
-    vectors = [sums_one[0:1, :], sums_one[1:2, :], dc_sum[...], sums_two[0:1, :], sums_two[1:2, :], g_sum[...]]
+
+
+def pack_first_kernel(
+    wires, cuts, flat_one, embedding, dc_sum, sums_one, sums_two, g_sum, two, two_got,
+    send, keep, two_send, two_keep, flat_project,
+):
+    halve_kernel(two, two_got, two_send, two_keep, 0)
+    emb = embedding[...].astype(F32)
+    q = (emb * sigmoid(emb)).astype(BF16).astype(F32)
+    q = jnp.broadcast_to(q, (LANES, q.shape[1])).T
+    dc = dc_sum[...]
+    store_flat(flat_project, 0, jnp.concatenate([q * dc[:, :LANES], q * dc[:, LANES:]], axis=1))
+    take_blocks(wires, cuts, (flat_one, flat_project), send, keep)
+    at = wires.slots * sum(cuts)
+    vectors = [sums_one[0:1, :], sums_one[1:2, :], dc, sums_two[0:1, :], sums_two[1:2, :], g_sum[...]]
     halves = [row[:, i * LANES : (i + 1) * LANES] for row in vectors for i in range(2)]
     values = jnp.concatenate(halves + [jnp.zeros((VEC_ROWS - len(halves), LANES), F32)], axis=0)
     keep[at : at + VEC_ROWS, :] = values
     send[at : at + VEC_ROWS, :] = values.astype(BF16)
 
 
-def finish_kernel(wires, cuts, n_vec, keep, got, one, two, project, vec):
+def pack_second_kernel(wires, cuts, flat, send, keep):
+    take_blocks(wires, cuts, (flat,), send, keep)
+
+
+def finish_kernel(wires, cuts, n_vec, keep, got, one, project, two, vec):
     at = 0
-    for out, rows in zip((one, two, project), cuts):
+    for out, rows in zip((one, project, two), cuts):
         out[...] = keep[at : at + rows, :] + got[at : at + rows, :].astype(F32)
         at += rows
     vectors = keep[at : at + VEC_ROWS, :] + got[at : at + VEC_ROWS, :].astype(F32)
@@ -532,111 +664,135 @@
     vec[...] = shifted[:, :n_vec]
 
 
-def call(body, outs, *args, scratch=(), flops=0, size=4 << 20, after=()):
+def call(body, outs, *args, scratch=(), flops=0, size=4 << 20, after=(), far=(), far_outs=(), semaphores=(), same=None):
     held, n_in = len(after), len(args)
 
     def run(*refs):
         body(*refs[:n_in], *refs[n_in + held :])
 
+    args = [pltpu.with_memory_space_constraint(v, pltpu.HBM) if i in far else v for i, v in enumerate(args)]
+
+    def spec(is_far):
+        return pl.BlockSpec(memory_space=pltpu.HBM if is_far else pltpu.VMEM)
+
     return pl.pallas_call(
         run,
-        out_shape=[jax.ShapeDtypeStruct(shape, dtype) for shape, dtype in outs],
-        in_specs=[pl.BlockSpec(memory_space=pltpu.VMEM)] * n_in + [pl.BlockSpec(memory_space=pl.ANY)] * held,
-        out_specs=[pl.BlockSpec(memory_space=pltpu.VMEM)] * len(outs),
-        scratch_shapes=[pltpu.VMEM(shape, dtype) for shape, dtype in scratch],
+        out_shape=[
+            pltpu.HBM(shape, dtype) if i in far_outs else jax.ShapeDtypeStruct(shape, dtype)
+            for i, (shape, dtype) in enumerate(outs)
+        ],
+        in_specs=[spec(i in far) for i in range(n_in)] + [pl.BlockSpec(memory_space=pl.ANY)] * held,
+        out_specs=[spec(i in far_outs) for i in range(len(outs))],
+        scratch_shapes=[pltpu.VMEM(shape, dtype) for shape, dtype in scratch]
+        + [pltpu.SemaphoreType.DMA((n,)) for n in semaphores],
+        input_output_aliases=same or {},
         compiler_params=pltpu.CompilerParams(vmem_limit_bytes=VMEM_BYTES),
         cost_estimate=pl.CostEstimate(flops=flops, bytes_accessed=size, transcendentals=0),
     )(*args, *after)
 
 
-def gather(wires, cuts, parts, vectors, q, beside):
+def joined(held, tail=VEC_ROWS):
+    return ((2 * (held.shape[0] - tail) + tail, LANES), BF16)
+
+
+def gather_start(wires, cuts, held, beside):
+    part = wires.far - 1
+    for stage in range(part):
+        after = beside.get(stage, ())
+        held, = call(join_kernel, [joined(held)], held, wires.swap(held, stage), after=after)
+    got = wires.swap(held, part)
+    slots = 2 << part
+    shapes = [(slots * sum(cuts[:-1]) + VEC_ROWS, LANES), (slots * cuts[-1], LANES)]
+    outs = [(shape, BF16) for shape in shapes]
+    first, second = call(functools.partial(part_kernel, cuts), outs, held, got, after=beside.get(part, ()))
+    for stage in range(wires.far, wires.stages):
+        first_got, second_got = wires.swap(first, stage), wires.swap(second, stage, 1)
+        outs = [joined(first), joined(second, 0)]
+        after = beside.get(stage, ())
+        first, second = call(join_both_kernel, outs, first, first_got, second, second_got, after=after)
+    return first, wires.swap(first, wires.stages), second, wires.swap(second, wires.stages)
+
+
+def in_order(wires, cuts, mine, got, turned=0):
     block = sum(cuts)
-    n_vec = vectors.shape[0]
+    rows = wires.slots * block
+    both = jnp.concatenate([mine[:rows], got[:rows]]).reshape(wires.n, block, LANES)
     me = wires.me()
-    wide = VEC_ROWS * LANES
-    placed = lax.dynamic_slice(jnp.pad(vectors, (wide, wide - n_vec)), (wide - me * n_vec,), (wide,))
-    held = jnp.concatenate([v.reshape(-1, LANES) for v in (*parts, placed)], axis=0)
-    for stage in range(wires.stages):
-        got = wires.swap(held, stage)
-        shape = (2 * (held.shape[0] - VEC_ROWS) + VEC_ROWS, LANES)
-        after = beside.get(stage, ())
-        held, = call(join_kernel, [(shape, BF16)], held, got, size=4 * LANES * shape[0], after=after)
-    got = wires.swap(held, wires.stages)
+    owners = jnp.stack([wires.owner(j, other, me, turned) for other in (False, True) for j in range(wires.slots)])
+    both = jnp.zeros_like(both).at[owners].set(both)
+    ends = [sum(cuts[:i]) for i in range(len(cuts) + 1)]
+    return [both[:, a:b].reshape(-1, 2 * LANES) for a, b in zip(ends, ends[1:])]
+
+
+def arrange_first(wires, cuts, mine, got, embedding):
     channels = 2 * LANES
-    totals = [wires.n * rows for rows in cuts]
-    outs = [((rows // 2, channels), BF16) for rows in (totals[0] + totals[2], totals[1])]
-    if all(rows % 8 == 0 for rows in cuts):
-        return call(
-            functools.partial(arrange_kernel, wires, cuts),
-            [*outs, ((VEC_ROWS // 2, channels), F32), ((1, channels), F32)],
-            held,
-            got,
-            q,
-            scratch=[((rows, LANES), F32) for rows in (*totals, VEC_ROWS)],
-        )
-    rows = wires.slots * block
-    both = jnp.concatenate([held[:rows], got[:rows]]).reshape(wires.n, block, LANES)
-    owners = jnp.stack([wires.owner(j, other, me) for other in (False, True) for j in range(wires.slots)])
-    both = jnp.zeros_like(both).at[owners].set(both)
-    at, whole = 0, []
-    for cut in cuts:
-        whole.append(both[:, at : at + cut].reshape(-1, channels))
-        at += cut
-    vec = (held[rows:].astype(F32) + got[rows:].astype(F32)).reshape(VEC_ROWS // 2, channels)
-    time = jnp.dot(q, whole[2], preferred_element_type=F32)
-    return jnp.concatenate([whole[0], whole[2]]), whole[1], vec, time
-
-
-def pack(wires, cuts, turned, three, flat_two, q, dc_sum, sums_one, sums_two, g_sum):
-    block = sum(cuts)
-    shape = (wires.slots * block + VEC_ROWS, LANES)
     totals = [wires.n * rows for rows in cuts]
     if all(rows % 8 == 0 for rows in cuts):
         return call(
-            functools.partial(pack_kernel, wires, cuts),
-            [(shape, BF16), (shape, F32)],
-            turned,
-            three,
-            flat_two,
-            q,
+            functools.partial(arrange_first_kernel, wires, cuts),
+            [((sum(totals) // 2, channels), BF16), ((VEC_ROWS // 2, channels), F32), ((1, channels), F32)],
+            mine,
+            got,
+            embedding,
+            scratch=[((rows, LANES), F32) for rows in (*totals, VEC_ROWS)],
+        )
+    one, project = in_order(wires, cuts, mine, got)
+    vec = (mine[-VEC_ROWS:].astype(F32) + got[-VEC_ROWS:].astype(F32)).reshape(VEC_ROWS // 2, channels)
+    act = jax.nn.silu(embedding.astype(F32)).astype(BF16)
+    return jnp.concatenate([one, project]), vec, jnp.dot(act, project, preferred_element_type=F32)
+
+
+def arrange_second(wires, cuts, mine, got, after):
+    rows = wires.n * cuts[0]
+    if cuts[0] % 8 == 0:
+        body = functools.partial(arrange_second_kernel, wires, cuts)
+        return call(body, [((rows // 2, 2 * LANES), BF16)], mine, got, scratch=[((rows, LANES), F32)], after=after)[0]
+    return in_order(wires, cuts, mine, got, 1)[0]
+
+
+def out_of_order(wires, cuts, parts, tail):
+    me = wires.me()
+    blocks = jnp.concatenate([v.reshape(wires.n, rows, LANES) for v, rows in zip(parts, cuts)], axis=1)
+    halves = []
+    for other in (True, False):
+        owners = jnp.stack([wires.owner(j, other, me) for j in range(wires.slots)])
+        halves.append(jnp.concatenate([blocks[owners].reshape(-1, LANES), tail]))
+    return halves[0].astype(BF16), halves[1]
+
+
+def pack_first(wires, cuts, flat_one, embedding, dc_sum, sums_one, sums_two, g_sum, two, two_got):
+    shape = (wires.slots * sum(cuts) + VEC_ROWS, LANES)
+    if all(rows % 8 == 0 for rows in cuts):
+        return call(
+            functools.partial(pack_first_kernel, wires, cuts),
+            [(shape, BF16), (shape, F32), *halved(two, 0)],
+            flat_one,
+            embedding,
             dc_sum,
             sums_one,
             sums_two,
             g_sum,
-            scratch=[((totals[0], LANES), F32), ((totals[2], LANES), F32)],
-            flops=9 * three.size * three.shape[-1] // 2,
+            two,
+            two_got,
+            scratch=[((wires.n * cuts[1], LANES), F32)],
         )
-    flat_one, = call(grad_kernel, [((totals[0], LANES), F32)], turned, three)
-    flats = (flat_one, flat_two, (q * dc_sum).reshape(-1, LANES))
-    blocks = jnp.concatenate([f.reshape(wires.n, rows, LANES) for f, rows in zip(flats, cuts)], axis=1)
-    me = wires.me()
+    q = jax.nn.silu(embedding.astype(F32)).astype(BF16).astype(F32).reshape(-1, 1)
     vec = jnp.concatenate([sums_one, dc_sum, sums_two, g_sum]).reshape(-1, LANES)
     vec = jnp.pad(vec, ((0, VEC_ROWS - vec.shape[0]), (0, 0)))
-    halves = []
-    for other in (True, False):
-        owners = jnp.stack([wires.owner(j, other, me) for j in range(wires.slots)])
-        halves.append(jnp.concatenate([blocks[owners].reshape(-1, LANES), vec]))
-    return halves[0].astype(BF16), halves[1]
-
-
-def reduce_scatter(wires, cuts, n_vec, send, keep, beside):
-    for stage in range(wires.stages, 0, -1):
-        got = wires.swap(send, stage)
-        shape = ((keep.shape[0] - VEC_ROWS) // 2 + VEC_ROWS, LANES)
-        send, keep = call(halve_kernel, [(shape, BF16), (shape, F32)], keep, got, size=12 * LANES * shape[0], after=beside.get(stage, ()))
-    got = wires.swap(send, 0)
-    return call(
-        functools.partial(finish_kernel, wires, cuts, n_vec),
-        [*[((rows, LANES), F32) for rows in cuts], ((1, n_vec), F32)],
-        keep,
-        got,
-        size=12 * LANES * keep.shape[0],
-    )
-
-
-def swish_slope(values):
-    sigma = jax.nn.sigmoid(values)
-    return sigma * (1.0 + values * (1.0 - sigma))
+    send, keep = out_of_order(wires, cuts, (flat_one, (q * dc_sum).reshape(-1, LANES)), vec)
+    return send, keep, *call(halve_second_kernel, halved(two, 0), two, two_got)
+
+
+def pack_second(wires, cuts, flat):
+    if cuts[0] % 8 == 0:
+        shape = (wires.slots * cuts[0], LANES)
+        return call(functools.partial(pack_second_kernel, wires, cuts), [(shape, BF16), (shape, F32)], flat)
+    return out_of_order(wires, cuts, (flat,), jnp.zeros((0, LANES), F32))
+
+
+def halved(keep, tail=VEC_ROWS):
+    shape = ((keep.shape[0] - tail) // 2 + tail, LANES)
+    return [(shape, BF16), (shape, F32)]
 
 
 def local(sizes, images, embedding, conv_first, conv_second, projection, vectors, cotangent):
@@ -658,16 +814,21 @@
     conv_flops = 2 * 9 * pixels * channels * channels
 
     x, g = images[0], cotangent[0]
-    stats, g_three, g_sum = call(prepare_kernel, [pair, three, line], x, g)
-    emb_float = embedding.astype(F32)
-    emb_act = jax.nn.silu(emb_float).astype(BF16)
-    q = emb_act.astype(F32).reshape(emb_width, 1)
-    parts = (conv_first, conv_second, projection)
-    first, kernel_two, vec, time = gather(wires, cuts, parts, vectors, emb_act, {wires.stages - 1: (g_sum,)})
+    stats, x_near = call(stats_kernel, [pair, maps], x, far=(0,), semaphores=(4,))
+    g_three, g_sum = call(
+        spread_kernel, [three, line], g, scratch=[maps, three], far=(0,), far_outs=(0,), semaphores=(4, 4)
+    )
+    wide = VEC_ROWS * LANES
+    placed = lax.dynamic_slice(jnp.pad(vectors, (wide, wide - n_vec)), (wide - wires.me() * n_vec,), (wide,))
+    start = jnp.concatenate([v.reshape(-1, LANES) for v in (conv_first, projection, conv_second, placed)])
+    beside = {wires.stages - 2: (g_sum,), wires.stages - 1: (stats,)}
+    one, one_got, two, two_got = gather_start(wires, (cuts[0], cuts[2], cuts[1]), start, beside)
+    first, vec, time = arrange_first(wires, (cuts[0], cuts[2]), one, one_got, embedding)
 
     turned_one, raw, stats_two = call(
-        first_kernel, [turned, flat, pair], x, stats, vec, time, first, scratch=[three], flops=conv_flops
+        first_kernel, [turned, flat, pair], x_near, stats, vec, time, first, scratch=[three], flops=conv_flops
     )
+    kernel_two = arrange_second(wires, cuts[1:2], two, two_got, (stats_two,))
     act_two, sums_two, grad_two, e_three, dc_sum = call(
         second_kernel,
         [padded, pair, taps, three, line],
@@ -679,18 +840,76 @@
         scratch=[flat, turned],
         flops=2 * conv_flops,
     )
-    dh_one, sums_one = call(third_kernel, [flat, pair], e_three, x, stats, vec, first, flops=conv_flops)
-    send, keep = pack(wires, cuts, turned_one, e_three, grad_two, q, dc_sum, sums_one, sums_two, g_sum)
-    input_grad, dq, input_done = call(
-        input_kernel, [(maps[0], F32), ((1, emb_width), F32), line], dh_one, x, g, stats, sums_one, vec, dc_sum, first
+    last = wires.stages
+    two_send, two = pack_second(wires, cuts[1:2], grad_two)
+    two_got = wires.swap(two_send, last)
+    dh_one, sums_one = call(third_kernel, [flat, pair], e_three, x_near, stats, vec, first, flops=conv_flops)
+    two_send, two = call(halve_second_kernel, halved(two, 0), two, two_got, after=(sums_one,))
+    two_got = wires.swap(two_send, last - 1)
+    grad_one, = call(grad_kernel, [taps], turned_one, e_three, flops=conv_flops)
+    one_cuts = (cuts[0], cuts[2])
+    one_send, one, two_send, two = pack_first(
+        wires, one_cuts, grad_one, embedding, dc_sum, sums_one, sums_two, g_sum, two, two_got
     )
-    output, output_done = call(
-        last_kernel, [maps, line], act_two, x, vec, kernel_two, scratch=[three], flops=conv_flops
+    input_grad, embedding_grad, input_done = call(
+        input_kernel,
+        [(maps[0], F32), ((1, emb_width), F32), line],
+        dh_one,
+        x,
+        g,
+        stats,
+        sums_one,
+        vec,
+        dc_sum,
+        first,
+        embedding,
     )
-    beside = {wires.stages - 1: (output_done,), wires.stages - 2: (input_done,)}
-    summed = reduce_scatter(wires, cuts, n_vec, send, keep, beside)
-    embedding_grad = dq * swish_slope(emb_float)
-    return (output[None], input_grad[None], embedding_grad, *[v.reshape(-1) for v in summed])
+    parts = 2
+    rows = height // parts
+    output, output_done = (), []
+    for part in range(parts):
+        *output, done = call(
+            functools.partial(last_kernel, part, parts),
+            [maps, line],
+            act_two,
+            x_near,
+            vec,
+            kernel_two,
+            *output,
+            scratch=[((3, rows + 2, width, channels), BF16), ((rows, width, channels), BF16)],
+            far=(4,),
+            far_outs=(0,),
+            semaphores=(rows // (UNITS * ROWS),),
+            same={4: 0} if output else None,
+            flops=conv_flops // parts,
+        )
+        output_done.append(done)
+    one_got = wires.swap(one_send, last)
+    one_send, one = call(halve_kernel, halved(one), one, one_got, after=(input_done,))
+    one_got = wires.swap(one_send, last - 1)
+    wide, narrow = sum(one_cuts), cuts[1]
+    shape = (wires.slots // 4 * (wide + narrow) + VEC_ROWS, LANES)
+    send, keep = call(
+        functools.partial(merge_kernel, wide, narrow),
+        [(shape, BF16), (shape, F32)],
+        one,
+        one_got,
+        two_send,
+        two,
+        after=(output_done[0],),
+    )
+    for stage in range(last - 2, 0, -1):
+        after = (output_done[1],) if stage == last - 2 else ()
+        send, keep = call(halve_kernel, halved(keep), keep, wires.swap(send, stage), after=after)
+    all_cuts = (*one_cuts, cuts[1])
+    first_sum, project_sum, second_sum, vec_sum = call(
+        functools.partial(finish_kernel, wires, all_cuts, n_vec),
+        [*[((rows, LANES), F32) for rows in all_cuts], ((1, n_vec), F32)],
+        keep,
+        wires.swap(send, 0),
+    )
+    summed = (first_sum, second_sum, project_sum, vec_sum)
+    return (output[0][None], input_grad[None], embedding_grad, *[v.reshape(-1) for v in summed])
 
 
 def solution(mesh):

time: 103 us -> 98.4 us (0.955)
  local copies, waits for them, and re-layouts: 6.1 us -> 0.77 us
  waiting for transfers between devices: 31.2 us -> 28 us
  Pallas kernels: 46.6 us -> 49.8 us
    unnamed x16 -> x10, local copies, waits for them, and re-layouts: 4.35 us -> 0.02 us
    ppermute x10 -> x15, waiting for transfers between devices: 31.2 us -> 28 us  [swap(): lax.ppermute(value, AXES, [(i, i ^ 1 << bit(i & 1)) for i in range(self.n)])]
    pallas_call x17 -> x23, Pallas kernels: 46.6 us -> 49.8 us  [call(): pl.pallas_call(run, out_shape=[pltpu.HBM(shape, dtype) if i in far_outs e...]
    ppermute x10 -> x15, starting transfers between devices: 16.9 us -> 17.9 us  [swap(): lax.ppermute(value, AXES, [(i, i ^ 1 << bit(i & 1)) for i in range(self.n)])]
  transfers between devices with their start and end apart: 10 -> 15, of which waited for: 10 -> 10; matrix products, arithmetic and copies ran while one was open for 1% -> 0% of each run, Pallas kernels for 13% -> 36%
where the time goes in v3:
time: 98.4 us; the launch traced here: 98.2 us
  Pallas kernels  49.8 us (51%)
  waiting for transfers between devices  28 us (28%)
  starting transfers between devices  17.9 us (18%)
    pallas_call x23, Pallas kernels, call(): pl.pallas_call(run, out_shape=[pltpu.HBM(shape, dtype) if i in far_outs e...  49.8 us
    ppermute x15, waiting for transfers between devices, swap(): lax.ppermute(value, AXES, [(i, i ^ 1 << bit(i & 1)) for i in range(self.n)])  28 us
    ppermute x15, starting transfers between devices, swap(): lax.ppermute(value, AXES, [(i, i ^ 1 << bit(i & 1)) for i in range(self.n)])  17.9 us
  transfers between devices with their start and end apart: 15, of which 10 were waited for; matrix products, arithmetic and copies ran while one was open for 0% of the time, Pallas kernels for 36%

profile of v3, /device:TPU:0, one launch (start us, length us, event | category | flops | bytes accessed | tf_op | source)
XLA Modules:
  0.0 98.2 jit_solution(589338819970893527)
XLA Ops:
  2.2 4.0 %collective-permute-start = (bf16[336,128]{1,0:T(8,128)(2,1)S(1)}, bf16[336,128]{1,0:T(8,128)(2,1)S(1)}, u32[]{:S(2)}, u32[]{:S(2)}) collective-permute-start(bf16[336,128]{1,0:T(8,128)(2,1)S(1)} %pad_maximum_fusion.refs_0_), channel_id=1, source_target_pairs={{0,8},{1,5},{2,10},{3,7},{4,12},{5,1},{6,14},{7,3},{8,0},{9,13},{1... | collective-permute-start | bytes 258056 | tf_op jit(solution)/shard_map/ppermute | solution.py:36
  6.2 2.5 %collective-permute-done.refs_1_ = bf16[336,128]{1,0:T(8,128)(2,1)S(1)} collective-permute-done((bf16[336,128]{1,0:T(8,128)(2,1)S(1)}, bf16[336,128]{1,0:T(8,128)(2,1)S(1)}, u32[]{:S(2)}, u32[]{:S(2)}) %collective-permute-start) | collective-permute-done | bytes 86048 | tf_op jit(solution)/shard_map/ppermute | solution.py:36
  8.7 2.0 %collective-permute-start.1 = (bf16[656,128]{1,0:T(8,128)(2,1)S(1)}, bf16[656,128]{1,0:T(8,128)(2,1)S(1)}, u32[]{:S(2)}, u32[]{:S(2)}) collective-permute-start(bf16[656,128]{1,0:T(8,128)(2,1)S(1)} %shard_map.128.refs_0_), channel_id=1, source_target_pairs={{0,4},{1,9},{2,6},{3,11},{4,0},{5,13},{6,2},{7,15},{8,12},{9,1},{1... | collective-permute-start | bytes 503816 | tf_op jit(solution)/shard_map/ppermute | solution.py:36
  10.7 4.1 %collective-permute-done.1.refs_1_ = bf16[656,128]{1,0:T(8,128)(2,1)S(1)} collective-permute-done((bf16[656,128]{1,0:T(8,128)(2,1)S(1)}, bf16[656,128]{1,0:T(8,128)(2,1)S(1)}, u32[]{:S(2)}, u32[]{:S(2)}) %collective-permute-start.1) | collective-permute-done | bytes 167968 | tf_op jit(solution)/shard_map/ppermute | solution.py:36
  14.8 1.9 %collective-permute-start.2 = (bf16[720,128]{1,0:T(8,128)(2,1)S(1)}, bf16[720,128]{1,0:T(8,128)(2,1)S(1)}, u32[]{:S(2)}, u32[]{:S(2)}) collective-permute-start(bf16[720,128]{1,0:T(8,128)(2,1)S(1)} %get-tuple-element.60.refs_0_), channel_id=1, source_target_pairs={{0,2},{1,17},{2,0},{3,19},{4,6},{5,21},{6,4},{7,23},{8,10},{9,25},... | collective-permute-start | bytes 552968 | tf_op jit(solution)/shard_map/ppermute | solution.py:36
  16.7 1.5 %collective-permute-start.3 = (bf16[576,128]{1,0:T(8,128)(2,1)S(1)}, bf16[576,128]{1,0:T(8,128)(2,1)S(1)}, u32[]{:S(2)}, u32[]{:S(2)}) collective-permute-start(bf16[576,128]{1,0:T(8,128)(2,1)S(1)} %get-tuple-element.61.refs_2_), channel_id=1, source_target_pairs={{0,16},{1,3},{2,18},{3,1},{4,20},{5,7},{6,22},{7,5},{8,24},{9,11},... | collective-permute-start | bytes 442376 | tf_op jit(solution)/shard_map/ppermute | solution.py:36
  18.3 4.0 %shard_map.126 = (bf16[3,66,64,256]{3,2,1,0:T(8,128)(2,1)}, f32[1,256]{1,0:T(1,128)S(1)}) custom-call(bf16[64,64,256]{2,1,0:T(8,128)(2,1)} %bitcast.13), custom_call_target="tpu_custom_call" | custom-call | bytes 4194304 | tf_op jit(solution)/shard_map/pallas_call | solution.py:678
  24.1 2.8 %shard_map.127 = (f32[2,256]{1,0:T(2,128)S(1)}, bf16[64,64,256]{2,1,0:T(8,128)(2,1)S(1)}) custom-call(bf16[64,64,256]{2,1,0:T(8,128)(2,1)} %bitcast.15), custom_call_target="tpu_custom_call" | custom-call | bytes 4194304 | tf_op jit(solution)/shard_map/pallas_call | solution.py:678
  26.9 3.5 %collective-permute-done.5.refs_3_ = bf16[1152,128]{1,0:T(8,128)(2,1)S(1)} collective-permute-done((bf16[1152,128]{1,0:T(8,128)(2,1)S(1)}, bf16[1152,128]{1,0:T(8,128)(2,1)S(1)}, u32[]{:S(2)}, u32[]{:S(2)}) %collective-permute-start.5) | collective-permute-done | bytes 294944 | tf_op jit(solution)/shard_map/ppermute | solution.py:36
  31.8 1.7 %collective-permute-done.6.refs_1_ = bf16[2832,128]{1,0:T(8,128)(2,1)S(1)} collective-permute-done((bf16[2832,128]{1,0:T(8,128)(2,1)S(1)}, bf16[2832,128]{1,0:T(8,128)(2,1)S(1)}, u32[]{:S(2)}, u32[]{:S(2)}) %collective-permute-start.6) | collective-permute-done | bytes 725024 | tf_op jit(solution)/shard_map/ppermute | solution.py:36
  34.0 6.4 %shard_map.133 = (bf16[2,256,4224]{2,1,0:T(8,128)(2,1)S(1)}, f32[4096,256]{1,0:T(8,128)S(1)}, f32[2,256]{1,0:T(2,128)S(1)}) custom-call(bf16[64,64,256]{2,1,0:T(8,128)(2,1)S(1)} %get-tuple-element.58.refs_0_.refs_1_, f32[2,256]{1,0:T(2,128)S(1)} %get-tuple-element.59.refs_4_.refs_1_.refs_2_.refs_3_, f32[8,256]{1,0:T(8,128)S(1)} %get-tuple-element.66.refs_2_.refs_3_.refs_5_, ...), custom_call_target="tpu_custom_call" | custom-call | flops 4831838208 | bytes 4194304 | tf_op jit(solution)/shard_map/pallas_call | solution.py:678
  40.7 12.2 %shard_map.135 = (bf16[66,64,256]{2,1,0:T(8,128)(2,1)S(1)}, f32[2,256]{1,0:T(2,128)S(1)}, f32[4608,128]{1,0:T(8,128)S(1)}, bf16[3,66,64,256]{3,2,1,0:T(8,128)(2,1)S(1)}, f32[1,256]{1,0:T(1,128)S(1)}) custom-call(bf16[3,66,64,256]{3,2,1,0:T(8,128)(2,1)S(1)} %bitcast.18, f32[4096,256]{1,0:T(8,128)S(1)} %get-tuple-element.69.refs_1_, ...), custom_call_target="tpu_custom_call" | custom-call | flops 9663676416 | bytes 4194304 | tf_op jit(solution)/shard_map/pallas_call | solution.py:678
  53.2 6.2 %shard_map.138 = (f32[4096,256]{1,0:T(8,128)S(1)}, f32[2,256]{1,0:T(2,128)S(1)}) custom-call(bf16[3,66,64,256]{3,2,1,0:T(8,128)(2,1)S(1)} %get-tuple-element.75.refs_0_.refs_1_, bf16[64,64,256]{2,1,0:T(8,128)(2,1)S(1)} %get-tuple-element.58.refs_0_.refs_1_, f32[2,256]{1,0:T(2,128)S(1)} %get-tuple-element.59.refs_4_.refs_1_.refs_2_.refs_3_, ...), custom_call_target="tpu_custom_call" | custom-call | flops 4831838208 | bytes 4194304 | tf_op jit(solution)/shard_map/pallas_call | solution.py:678
  59.9 5.0 %shard_map.140.refs_0_ = f32[4608,128]{1,0:T(8,128)S(1)} custom-call(bf16[2,256,4224]{2,1,0:T(8,128)(2,1)S(1)} %get-tuple-element.81.refs_0_, bf16[3,66,64,256]{3,2,1,0:T(8,128)(2,1)S(1)} %get-tuple-element.75.refs_0_.refs_1_), custom_call_target="tpu_custom_call" | custom-call | flops 4831838208 | bytes 4194304 | tf_op jit(solution)/shard_map/pallas_call | solution.py:678
  65.0 1.4 %collective-permute-done.9.refs_7_ = bf16[1152,128]{1,0:T(8,128)(2,1)S(1)} collective-permute-done((bf16[1152,128]{1,0:T(8,128)(2,1)S(1)}, bf16[1152,128]{1,0:T(8,128)(2,1)S(1)}, u32[]{:S(2)}, u32[]{:S(2)}) %collective-permute-start.9) | collective-permute-done | bytes 294944 | tf_op jit(solution)/shard_map/ppermute | solution.py:36
  66.8 3.7 %shard_map.139 = (f32[64,64,256]{2,1,0:T(8,128)}, f32[1,512]{1,0:T(1,128)}, f32[1,256]{1,0:T(1,128)S(1)}) custom-call(f32[4096,256]{1,0:T(8,128)S(1)} %get-tuple-element.76.refs_0_, bf16[64,64,256]{2,1,0:T(8,128)(2,1)S(1)} %bitcast.16, bf16[64,64,256]{2,1,0:T(8,128)(2,1)S(1)} %bitcast.14, f32[2,256]{1,0:T(2,128)S(1)} %get-tuple-element.59.refs_4_.refs_1_.refs_2_.refs_3_, ...), custom_call_target="tpu_custom_call" | custom-call | bytes 4194304 | tf_op jit(solution)/shard_map/pallas_call | solution.py:678
  70.7 1.5 %collective-permute-start.11 = (bf16[1424,128]{1,0:T(8,128)(2,1)S(1)}, bf16[1424,128]{1,0:T(8,128)(2,1)S(1)}, u32[]{:S(2)}, u32[]{:S(2)}) collective-permute-start(bf16[1424,128]{1,0:T(8,128)(2,1)S(1)} %get-tuple-element.92), channel_id=1, source_target_pairs={{0,16},{1,3},{2,18},{3,1},{4,20},{5,7},{6,22},{7,5},{8,24},{9,11},... | collective-permute-start | bytes 1093640 | tf_op jit(solution)/shard_map/ppermute | solution.py:36
  72.2 3.5 %shard_map.136 = (bf16[64,64,256]{2,1,0:T(8,128)(2,1)}, f32[1,256]{1,0:T(1,128)S(1)}) custom-call(bf16[66,64,256]{2,1,0:T(8,128)(2,1)S(1)} %get-tuple-element.72.refs_0_, bf16[64,64,256]{2,1,0:T(8,128)(2,1)S(1)} %get-tuple-element.58.refs_0_.refs_1_, f32[8,256]{1,0:T(8,128)S(1)} %get-tuple-element.66.refs_2_.refs_3_.refs_5_, ...), custom_call_target="tpu_custom_call" | custom-call | flops 2415919104 | bytes 4194304 | tf_op jit(solution)/shard_map/pallas_call | solution.py:678
  75.7 2.5 %collective-permute-done.11.refs_1_ = bf16[1424,128]{1,0:T(8,128)(2,1)S(1)} collective-permute-done((bf16[1424,128]{1,0:T(8,128)(2,1)S(1)}, bf16[1424,128]{1,0:T(8,128)(2,1)S(1)}, u32[]{:S(2)}, u32[]{:S(2)}) %collective-permute-start.11) | collective-permute-done | bytes 364576 | tf_op jit(solution)/shard_map/ppermute | solution.py:36
  79.3 3.5 %shard_map.137 = (bf16[64,64,256]{2,1,0:T(8,128)(2,1)}, f32[1,256]{1,0:T(1,128)S(1)}) custom-call(bf16[66,64,256]{2,1,0:T(8,128)(2,1)S(1)} %get-tuple-element.72.refs_0_, bf16[64,64,256]{2,1,0:T(8,128)(2,1)S(1)} %get-tuple-element.58.refs_0_.refs_1_, f32[8,256]{1,0:T(8,128)S(1)} %get-tuple-element.66.refs_2_.refs_3_.refs_5_, ...), custom_call_target="tpu_custom_call", output_to_operand_aliasing={{0}: (4, {})} | custom-call | flops 2415919104 | bytes 4194304 | tf_op jit(solution)/shard_map/pallas_call | solution.py:678
  82.8 2.7 %collective-permute-done.12.refs_1_ = bf16[1296,128]{1,0:T(8,128)(2,1)S(1)} collective-permute-done((bf16[1296,128]{1,0:T(8,128)(2,1)S(1)}, bf16[1296,128]{1,0:T(8,128)(2,1)S(1)}, u32[]{:S(2)}, u32[]{:S(2)}) %collective-permute-start.12) | collective-permute-done | bytes 331808 | tf_op jit(solution)/shard_map/ppermute | solution.py:36
  86.5 5.5 %collective-permute-done.13.refs_1_ = bf16[656,128]{1,0:T(8,128)(2,1)S(1)} collective-permute-done((bf16[656,128]{1,0:T(8,128)(2,1)S(1)}, bf16[656,128]{1,0:T(8,128)(2,1)S(1)}, u32[]{:S(2)}, u32[]{:S(2)}) %collective-permute-start.13) | collective-permute-done | bytes 167968 | tf_op jit(solution)/shard_map/ppermute | solution.py:36
  92.0 2.1 %collective-permute-start.14 = (bf16[336,128]{1,0:T(8,128)(2,1)S(1)}, bf16[336,128]{1,0:T(8,128)(2,1)S(1)}, u32[]{:S(2)}, u32[]{:S(2)}) collective-permute-start(bf16[336,128]{1,0:T(8,128)(2,1)S(1)} %get-tuple-element.102), channel_id=1, source_target_pairs={{0,8},{1,5},{2,10},{3,7},{4,12},{5,1},{6,14},{7,3},{8,0},{9,13},{1... | collective-permute-start | bytes 258056 | tf_op jit(solution)/shard_map/ppermute | solution.py:36
  94.1 3.4 %collective-permute-done.14.refs_1_ = bf16[336,128]{1,0:T(8,128)(2,1)S(1)} collective-permute-done((bf16[336,128]{1,0:T(8,128)(2,1)S(1)}, bf16[336,128]{1,0:T(8,128)(2,1)S(1)}, u32[]{:S(2)}, u32[]{:S(2)}) %collective-permute-start.14) | collective-permute-done | bytes 86048 | tf_op jit(solution)/shard_map/ppermute | solution.py:36
  (42 shorter events, 9.8 us)
Async XLA Ops:
  2.2 6.5 %collective-permute-start = (bf16[336,128]{1,0:T(8,128)(2,1)S(1)}, bf16[336,128]{1,0:T(8,128)(2,1)S(1)}, u32[]{:S(2)}, u32[]{:S(2)}) collective-permute-start(bf16[336,128]{1,0:T(8,128)(2,1)S(1)} %pad_maximum_fusion.refs_0_), channel_id=1, source_target_pairs={{0,8},{1,5},{2,10},{3,7},{4,12},{5,1},{6,14},{7,3},{8,0},{9,13},{1... | collective-permute-start | bytes 258056 | tf_op jit(solution)/shard_map/ppermute | solution.py:36
  8.7 6.1 %collective-permute-start.1 = (bf16[656,128]{1,0:T(8,128)(2,1)S(1)}, bf16[656,128]{1,0:T(8,128)(2,1)S(1)}, u32[]{:S(2)}, u32[]{:S(2)}) collective-permute-start(bf16[656,128]{1,0:T(8,128)(2,1)S(1)} %shard_map.128.refs_0_), channel_id=1, source_target_pairs={{0,4},{1,9},{2,6},{3,11},{4,0},{5,13},{6,2},{7,15},{8,12},{9,1},{1... | collective-permute-start | bytes 503816 | tf_op jit(solution)/shard_map/ppermute | solution.py:36
  14.8 7.5 %collective-permute-start.2 = (bf16[720,128]{1,0:T(8,128)(2,1)S(1)}, bf16[720,128]{1,0:T(8,128)(2,1)S(1)}, u32[]{:S(2)}, u32[]{:S(2)}) collective-permute-start(bf16[720,128]{1,0:T(8,128)(2,1)S(1)} %get-tuple-element.60.refs_0_), channel_id=1, source_target_pairs={{0,2},{1,17},{2,0},{3,19},{4,6},{5,21},{6,4},{7,23},{8,10},{9,25},... | collective-permute-start | bytes 552968 | tf_op jit(solution)/shard_map/ppermute | solution.py:36
  16.7 5.6 %collective-permute-start.3 = (bf16[576,128]{1,0:T(8,128)(2,1)S(1)}, bf16[576,128]{1,0:T(8,128)(2,1)S(1)}, u32[]{:S(2)}, u32[]{:S(2)}) collective-permute-start(bf16[576,128]{1,0:T(8,128)(2,1)S(1)} %get-tuple-element.61.refs_2_), channel_id=1, source_target_pairs={{0,16},{1,3},{2,18},{3,1},{4,20},{5,7},{6,22},{7,5},{8,24},{9,11},... | collective-permute-start | bytes 442376 | tf_op jit(solution)/shard_map/ppermute | solution.py:36
  22.3 11.2 %copy-start.2 = (bf16[1,512]{1,0:T(2,128)(2,1)S(1)}, bf16[1,512]{1,0:T(2,128)(2,1)}, u32[]{:S(2)}) copy-start(bf16[1,512]{1,0:T(2,128)(2,1)} %refs_1_.1) | copy-start | bytes 3076
  22.4 8.8 %collective-permute-start.4 = (bf16[1424,128]{1,0:T(8,128)(2,1)S(1)}, bf16[1424,128]{1,0:T(8,128)(2,1)S(1)}, u32[]{:S(2)}, u32[]{:S(2)}) collective-permute-start(bf16[1424,128]{1,0:T(8,128)(2,1)S(1)} %get-tuple-element.63.refs_0_), channel_id=1, source_target_pairs={{0,16},{1,3},{2,18},{3,1},{4,20},{5,7},{6,22},{7,5},{8,24},{9,11},... | collective-permute-start | bytes 1093640 | tf_op jit(solution)/shard_map/ppermute | solution.py:36
  23.5 6.8 %collective-permute-start.5 = (bf16[1152,128]{1,0:T(8,128)(2,1)S(1)}, bf16[1152,128]{1,0:T(8,128)(2,1)S(1)}, u32[]{:S(2)}, u32[]{:S(2)}) collective-permute-start(bf16[1152,128]{1,0:T(8,128)(2,1)S(1)} %get-tuple-element.64.refs_2_), channel_id=1, source_target_pairs={{0,2},{1,17},{2,0},{3,19},{4,6},{5,21},{6,4},{7,23},{8,10},{9,25},... | collective-permute-start | bytes 884744 | tf_op jit(solution)/shard_map/ppermute | solution.py:36
  31.2 2.3 %collective-permute-start.6 = (bf16[2832,128]{1,0:T(8,128)(2,1)S(1)}, bf16[2832,128]{1,0:T(8,128)(2,1)S(1)}, u32[]{:S(2)}, u32[]{:S(2)}) collective-permute-start(bf16[2832,128]{1,0:T(8,128)(2,1)S(1)} %get-tuple-element.65.refs_0_), channel_id=1, source_target_pairs={{0,1},{1,0},{2,3},{3,2},{4,5},{5,4},{6,7},{7,6},{8,9},{9,8},{10,11... | collective-permute-start | bytes 2174984 | tf_op jit(solution)/shard_map/ppermute | solution.py:36
  31.3 9.1 %collective-permute-start.7 = (bf16[2304,128]{1,0:T(8,128)(2,1)S(1)}, bf16[2304,128]{1,0:T(8,128)(2,1)S(1)}, u32[]{:S(2)}, u32[]{:S(2)}) collective-permute-start(bf16[2304,128]{1,0:T(8,128)(2,1)S(1)} %get-tuple-element.71.refs_0_), channel_id=1, source_target_pairs={{0,1},{1,0},{2,3},{3,2},{4,5},{5,4},{6,7},{7,6},{8,9},{9,8},{10,11... | collective-permute-start | bytes 1769480 | tf_op jit(solution)/shard_map/ppermute | solution.py:36
  34.0 6.7 %slice-start = ((s8[6488064]{0:T(1024)(128)(4,1)}), s8[4194304]{0:T(1024)(128)(4,1)S(1)}, s32[]{:S(2)}) async-start(s8[6488064]{0:T(1024)(128)(4,1)} %bitcast.17), calls=%async_computation | async-start | bytes 8388608
  34.0 6.7 %slice-start.1 = ((s8[6488064]{0:T(1024)(128)(4,1)}), s8[2293760]{0:T(1024)(128)(4,1)S(1)}, s32[]{:S(2)}) async-start(s8[6488064]{0:T(1024)(128)(4,1)} %bitcast.17), calls=%async_computation.1 | async-start | bytes 4587520
  53.0 6.4 %collective-permute-start.8 = (bf16[2304,128]{1,0:T(8,128)(2,1)S(1)}, bf16[2304,128]{1,0:T(8,128)(2,1)S(1)}, u32[]{:S(2)}, u32[]{:S(2)}) collective-permute-start(bf16[2304,128]{1,0:T(8,128)(2,1)S(1)} %get-tuple-element.85), channel_id=1, source_target_pairs={{0,1},{1,0},{2,3},{3,2},{4,5},{5,4},{6,7},{7,6},{8,9},{9,8},{10,11... | collective-permute-start | bytes 1769480 | tf_op jit(solution)/shard_map/ppermute | solution.py:36
  59.6 6.8 %collective-permute-start.9 = (bf16[1152,128]{1,0:T(8,128)(2,1)S(1)}, bf16[1152,128]{1,0:T(8,128)(2,1)S(1)}, u32[]{:S(2)}, u32[]{:S(2)}) collective-permute-start(bf16[1152,128]{1,0:T(8,128)(2,1)S(1)} %get-tuple-element.87), channel_id=1, source_target_pairs={{0,16},{1,3},{2,18},{3,1},{4,20},{5,7},{6,22},{7,5},{8,24},{9,11},... | collective-permute-start | bytes 884744 | tf_op jit(solution)/shard_map/ppermute | solution.py:36
  59.9 6.9 %copy-start.1 = (bf16[1,64,64,256]{3,2,1,0:T(8,128)(2,1)S(1)}, bf16[1,64,64,256]{3,2,1,0:T(8,128)(2,1)}, u32[]{:S(2)}) copy-start(bf16[1,64,64,256]{3,2,1,0:T(8,128)(2,1)} %param.7) | copy-start | bytes 6291460
  64.9 1.9 %copy-start = (bf16[1,64,64,256]{3,2,1,0:T(8,128)(2,1)S(1)}, bf16[1,64,64,256]{3,2,1,0:T(8,128)(2,1)}, u32[]{:S(2)}) copy-start(bf16[1,64,64,256]{3,2,1,0:T(8,128)(2,1)} %param.13) | copy-start | bytes 6291460
  66.7 3.8 %collective-permute-start.10 = (bf16[2832,128]{1,0:T(8,128)(2,1)S(1)}, bf16[2832,128]{1,0:T(8,128)(2,1)S(1)}, u32[]{:S(2)}, u32[]{:S(2)}) collective-permute-start(bf16[2832,128]{1,0:T(8,128)(2,1)S(1)} %get-tuple-element.89), channel_id=1, source_target_pairs={{0,1},{1,0},{2,3},{3,2},{4,5},{5,4},{6,7},{7,6},{8,9},{9,8},{10,11... | collective-permute-start | bytes 2174984 | tf_op jit(solution)/shard_map/ppermute | solution.py:36
  70.7 7.5 %collective-permute-start.11 = (bf16[1424,128]{1,0:T(8,128)(2,1)S(1)}, bf16[1424,128]{1,0:T(8,128)(2,1)S(1)}, u32[]{:S(2)}, u32[]{:S(2)}) collective-permute-start(bf16[1424,128]{1,0:T(8,128)(2,1)S(1)} %get-tuple-element.92), channel_id=1, source_target_pairs={{0,16},{1,3},{2,18},{3,1},{4,20},{5,7},{6,22},{7,5},{8,24},{9,11},... | collective-permute-start | bytes 1093640 | tf_op jit(solution)/shard_map/ppermute | solution.py:36
  78.3 7.2 %collective-permute-start.12 = (bf16[1296,128]{1,0:T(8,128)(2,1)S(1)}, bf16[1296,128]{1,0:T(8,128)(2,1)S(1)}, u32[]{:S(2)}, u32[]{:S(2)}) collective-permute-start(bf16[1296,128]{1,0:T(8,128)(2,1)S(1)} %get-tuple-element.97), channel_id=1, source_target_pairs={{0,2},{1,17},{2,0},{3,19},{4,6},{5,21},{6,4},{7,23},{8,10},{9,25},... | collective-permute-start | bytes 995336 | tf_op jit(solution)/shard_map/ppermute | solution.py:36
  85.6 6.4 %collective-permute-start.13 = (bf16[656,128]{1,0:T(8,128)(2,1)S(1)}, bf16[656,128]{1,0:T(8,128)(2,1)S(1)}, u32[]{:S(2)}, u32[]{:S(2)}) collective-permute-start(bf16[656,128]{1,0:T(8,128)(2,1)S(1)} %get-tuple-element.100), channel_id=1, source_target_pairs={{0,4},{1,9},{2,6},{3,11},{4,0},{5,13},{6,2},{7,15},{8,12},{9,1},{1... | collective-permute-start | bytes 503816 | tf_op jit(solution)/shard_map/ppermute | solution.py:36
  92.0 5.4 %collective-permute-start.14 = (bf16[336,128]{1,0:T(8,128)(2,1)S(1)}, bf16[336,128]{1,0:T(8,128)(2,1)S(1)}, u32[]{:S(2)}, u32[]{:S(2)}) collective-permute-start(bf16[336,128]{1,0:T(8,128)(2,1)S(1)} %get-tuple-element.102), channel_id=1, source_target_pairs={{0,8},{1,5},{2,10},{3,7},{4,12},{5,1},{6,14},{7,3},{8,0},{9,13},{1... | collective-permute-start | bytes 258056 | tf_op jit(solution)/shard_map/ppermute | solution.py:36

commit v4 on v3

--- a/solution.py
+++ b/solution.py
@@ -24,31 +24,27 @@
         assert 1 << self.bits == self.n and 1 << fsdp_bits == n_fsdp and fsdp_bits >= 3 and n_dp >= 2
         a, b = 1, fsdp_bits
         far = [bit for bit in range(self.bits - 1, 0, -1) if bit not in (a, b)]
-        self.far = len(far)
         self.order = {0: [*far, a, b], 1: [*far[::-1], b, a]}
         self.stages = self.bits - 1
         self.slots = 1 << self.stages
 
-    def swap(self, value, stage, turned=0):
+    def swap(self, value, stage):
         def bit(core):
-            return 0 if stage == self.stages else self.bit_of(stage, core, turned)
+            return 0 if stage == self.stages else self.order[core][stage]
 
         return lax.ppermute(value, AXES, [(i, i ^ (1 << bit(i & 1))) for i in range(self.n)])
 
-    def bit_of(self, stage, core, turned):
-        return self.order[core ^ turned if stage >= self.far else core][stage]
-
-    def mask(self, slot, core, turned):
-        return sum(1 << self.bit_of(i, core, turned) for i in range(self.stages) if slot >> i & 1)
+    def mask(self, slot, core):
+        return sum(1 << self.order[core][i] for i in range(self.stages) if slot >> i & 1)
 
     def me(self):
         return lax.axis_index("dp") * self.n_fsdp + lax.axis_index("fsdp")
 
-    def owner(self, slot, other, me, turned=0):
+    def owner(self, slot, other, me):
         core = me & 1
         if other:
             me, core = me ^ 1, 1 - core
-        return me ^ jnp.where(core == 0, self.mask(slot, 0, turned), self.mask(slot, 1, turned))
+        return me ^ jnp.where(core == 0, self.mask(slot, 0), self.mask(slot, 1))
 
 
 def owner(self, slot, other, me):
@@ -523,9 +519,9 @@
         out[2 * rows :, :] = mine[rows:, :] + got[rows:, :]
 
 
-def join_both_kernel(first, first_got, second, second_got, first_out, second_out):
-    join_kernel(first, first_got, first_out)
-    join_kernel(second, second_got, second_out, 0)
+def join_second_kernel(mine, got, out, mark):
+    join_kernel(mine, got, out, 0)
+    mark[...] = jnp.zeros_like(mark)
 
 
 def part_kernel(cuts, mine, got, first, second):
@@ -569,12 +565,12 @@
     send[to:, :] = values.astype(BF16)
 
 
-def place_blocks(wires, cuts, mine, got, flats, turned=0):
+def place_blocks(wires, cuts, mine, got, flats):
     me = wires.me()
     block = sum(cuts)
     for slot in range(wires.slots):
         for other, source in ((False, mine), (True, got)):
-            owner = wires.owner(slot, other, me, turned)
+            owner = wires.owner(slot, other, me)
             values = source[slot * block : (slot + 1) * block, :].astype(F32)
             at = 0
             for flat, rows in zip(flats, cuts):
@@ -601,7 +597,7 @@
 
 
 def arrange_second_kernel(wires, cuts, mine, got, second, flat_two):
-    place_blocks(wires, cuts, mine, got, (flat_two,), 1)
+    place_blocks(wires, cuts, mine, got, (flat_two,))
     unflatten(flat_two, second, 0)
 
 
@@ -687,7 +683,7 @@
         + [pltpu.SemaphoreType.DMA((n,)) for n in semaphores],
         input_output_aliases=same or {},
         compiler_params=pltpu.CompilerParams(vmem_limit_bytes=VMEM_BYTES),
-        cost_estimate=pl.CostEstimate(flops=flops, bytes_accessed=size, transcendentals=0),
+        cost_estimate=pl.CostEstimate(flops=0, bytes_accessed=0, transcendentals=0),
     )(*args, *after)
 
 
@@ -696,35 +692,33 @@
 
 
 def gather_start(wires, cuts, held, beside):
-    part = wires.far - 1
-    for stage in range(part):
+    last = wires.stages - 1
+    for stage in range(last - 1):
         after = beside.get(stage, ())
         held, = call(join_kernel, [joined(held)], held, wires.swap(held, stage), after=after)
-    got = wires.swap(held, part)
-    slots = 2 << part
+    got = wires.swap(held, last - 1)
+    slots = wires.slots // 2
     shapes = [(slots * sum(cuts[:-1]) + VEC_ROWS, LANES), (slots * cuts[-1], LANES)]
     outs = [(shape, BF16) for shape in shapes]
-    first, second = call(functools.partial(part_kernel, cuts), outs, held, got, after=beside.get(part, ()))
-    for stage in range(wires.far, wires.stages):
-        first_got, second_got = wires.swap(first, stage), wires.swap(second, stage, 1)
-        outs = [joined(first), joined(second, 0)]
-        after = beside.get(stage, ())
-        first, second = call(join_both_kernel, outs, first, first_got, second, second_got, after=after)
-    return first, wires.swap(first, wires.stages), second, wires.swap(second, wires.stages)
-
-
-def in_order(wires, cuts, mine, got, turned=0):
+    first, second = call(functools.partial(part_kernel, cuts), outs, held, got, after=beside.get(last - 1, ()))
+    first_got, second_got = wires.swap(first, last), wires.swap(second, last)
+    first, = call(join_kernel, [joined(first)], first, first_got, after=beside.get(last, ()))
+    second, mark = call(join_second_kernel, [joined(second, 0), ((1, LANES), F32)], second, second_got)
+    return first, wires.swap(first, wires.stages), second, wires.swap(second, wires.stages), mark
+
+
+def in_order(wires, cuts, mine, got):
     block = sum(cuts)
     rows = wires.slots * block
     both = jnp.concatenate([mine[:rows], got[:rows]]).reshape(wires.n, block, LANES)
     me = wires.me()
-    owners = jnp.stack([wires.owner(j, other, me, turned) for other in (False, True) for j in range(wires.slots)])
+    owners = jnp.stack([wires.owner(j, other, me) for other in (False, True) for j in range(wires.slots)])
     both = jnp.zeros_like(both).at[owners].set(both)
     ends = [sum(cuts[:i]) for i in range(len(cuts) + 1)]
     return [both[:, a:b].reshape(-1, 2 * LANES) for a, b in zip(ends, ends[1:])]
 
 
-def arrange_first(wires, cuts, mine, got, embedding):
+def arrange_first(wires, cuts, mine, got, embedding, after):
     channels = 2 * LANES
     totals = [wires.n * rows for rows in cuts]
     if all(rows % 8 == 0 for rows in cuts):
@@ -735,6 +729,7 @@
             got,
             embedding,
             scratch=[((rows, LANES), F32) for rows in (*totals, VEC_ROWS)],
+            after=after,
         )
     one, project = in_order(wires, cuts, mine, got)
     vec = (mine[-VEC_ROWS:].astype(F32) + got[-VEC_ROWS:].astype(F32)).reshape(VEC_ROWS // 2, channels)
@@ -747,7 +742,7 @@
     if cuts[0] % 8 == 0:
         body = functools.partial(arrange_second_kernel, wires, cuts)
         return call(body, [((rows // 2, 2 * LANES), BF16)], mine, got, scratch=[((rows, LANES), F32)], after=after)[0]
-    return in_order(wires, cuts, mine, got, 1)[0]
+    return in_order(wires, cuts, mine, got)[0]
 
 
 def out_of_order(wires, cuts, parts, tail):
@@ -822,8 +817,8 @@
     placed = lax.dynamic_slice(jnp.pad(vectors, (wide, wide - n_vec)), (wide - wires.me() * n_vec,), (wide,))
     start = jnp.concatenate([v.reshape(-1, LANES) for v in (conv_first, projection, conv_second, placed)])
     beside = {wires.stages - 2: (g_sum,), wires.stages - 1: (stats,)}
-    one, one_got, two, two_got = gather_start(wires, (cuts[0], cuts[2], cuts[1]), start, beside)
-    first, vec, time = arrange_first(wires, (cuts[0], cuts[2]), one, one_got, embedding)
+    one, one_got, two, two_got, mark = gather_start(wires, (cuts[0], cuts[2], cuts[1]), start, beside)
+    first, vec, time = arrange_first(wires, (cuts[0], cuts[2]), one, one_got, embedding, (mark,))
 
     turned_one, raw, stats_two = call(
         first_kernel, [turned, flat, pair], x_near, stats, vec, time, first, scratch=[three], flops=conv_flops
@@ -885,7 +880,7 @@
         )
         output_done.append(done)
     one_got = wires.swap(one_send, last)
-    one_send, one = call(halve_kernel, halved(one), one, one_got, after=(input_done,))
+    one_send, one = call(halve_kernel, halved(one), one, one_got)
     one_got = wires.swap(one_send, last - 1)
     wide, narrow = sum(one_cuts), cuts[1]
     shape = (wires.slots // 4 * (wide + narrow) + VEC_ROWS, LANES)
@@ -899,7 +894,7 @@
         after=(output_done[0],),
     )
     for stage in range(last - 2, 0, -1):
-        after = (output_done[1],) if stage == last - 2 else ()
+        after = {last - 2: (output_done[1],), last - 3: (input_done,)}.get(stage, ())
         send, keep = call(halve_kernel, halved(keep), keep, wires.swap(send, stage), after=after)
     all_cuts = (*one_cuts, cuts[1])
     first_sum, project_sum, second_sum, vec_sum = call(

time: 98.4 us -> 96.3 us (0.979)
  waiting for transfers between devices: 28 us -> 23.3 us
  starting transfers between devices: 17.9 us -> 20.6 us
    ppermute x15 -> x14, waiting for transfers between devices: 28 us -> 23.3 us  [swap(): lax.ppermute(value, AXES, [(i, i ^ 1 << bit(i & 1)) for i in range(self.n)])]
    ppermute x15 -> x14, starting transfers between devices: 17.9 us -> 20.6 us  [swap(): lax.ppermute(value, AXES, [(i, i ^ 1 << bit(i & 1)) for i in range(self.n)])]
    pallas_call x23 -> x24, Pallas kernels: 49.8 us -> 49.7 us  [call(): pl.pallas_call(run, out_shape=[pltpu.HBM(shape, dtype) if i in far_outs e...]
  transfers between devices with their start and end apart: 15 -> 14, of which waited for: 10 -> 10; matrix products, arithmetic and copies ran while one was open for 0% -> 0% of each run, Pallas kernels for 36% -> 37%
where the time goes in v4:
time: 96.3 us; the launch traced here: 96.1 us
  Pallas kernels  49.7 us (52%)
  waiting for transfers between devices  23.3 us (24%)
  starting transfers between devices  20.6 us (21%)
    pallas_call x24, Pallas kernels, call(): pl.pallas_call(run, out_shape=[pltpu.HBM(shape, dtype) if i in far_outs e...  49.7 us
    ppermute x14, waiting for transfers between devices, swap(): lax.ppermute(value, AXES, [(i, i ^ 1 << bit(i & 1)) for i in range(self.n)])  23.3 us
    ppermute x14, starting transfers between devices, swap(): lax.ppermute(value, AXES, [(i, i ^ 1 << bit(i & 1)) for i in range(self.n)])  20.6 us
  transfers between devices with their start and end apart: 14, of which 10 were waited for; matrix products, arithmetic and copies ran while one was open for 0% of the time, Pallas kernels for 37%

profile of v4, /device:TPU:0, one launch (start us, length us, event | category | flops | bytes accessed | tf_op | source)
XLA Modules:
  0.0 96.1 jit_solution(15485573786260256096)
XLA Ops:
  2.2 4.0 %collective-permute-start = (bf16[336,128]{1,0:T(8,128)(2,1)S(1)}, bf16[336,128]{1,0:T(8,128)(2,1)S(1)}, u32[]{:S(2)}, u32[]{:S(2)}) collective-permute-start(bf16[336,128]{1,0:T(8,128)(2,1)S(1)} %pad_maximum_fusion.refs_0_), channel_id=1, source_target_pairs={{0,8},{1,5},{2,10},{3,7},{4,12},{5,1},{6,14},{7,3},{8,0},{9,13},{1... | collective-permute-start | bytes 258056 | tf_op jit(solution)/shard_map/ppermute | solution.py:35
  6.2 2.5 %collective-permute-done.refs_1_ = bf16[336,128]{1,0:T(8,128)(2,1)S(1)} collective-permute-done((bf16[336,128]{1,0:T(8,128)(2,1)S(1)}, bf16[336,128]{1,0:T(8,128)(2,1)S(1)}, u32[]{:S(2)}, u32[]{:S(2)}) %collective-permute-start) | collective-permute-done | bytes 86048 | tf_op jit(solution)/shard_map/ppermute | solution.py:35
  8.7 2.0 %collective-permute-start.1 = (bf16[656,128]{1,0:T(8,128)(2,1)S(1)}, bf16[656,128]{1,0:T(8,128)(2,1)S(1)}, u32[]{:S(2)}, u32[]{:S(2)}) collective-permute-start(bf16[656,128]{1,0:T(8,128)(2,1)S(1)} %shard_map.128.refs_0_), channel_id=1, source_target_pairs={{0,4},{1,9},{2,6},{3,11},{4,0},{5,13},{6,2},{7,15},{8,12},{9,1},{1... | collective-permute-start | bytes 503816 | tf_op jit(solution)/shard_map/ppermute | solution.py:35
  10.7 4.1 %collective-permute-done.1.refs_1_ = bf16[656,128]{1,0:T(8,128)(2,1)S(1)} collective-permute-done((bf16[656,128]{1,0:T(8,128)(2,1)S(1)}, bf16[656,128]{1,0:T(8,128)(2,1)S(1)}, u32[]{:S(2)}, u32[]{:S(2)}) %collective-permute-start.1) | collective-permute-done | bytes 167968 | tf_op jit(solution)/shard_map/ppermute | solution.py:35
  14.8 1.9 %collective-permute-start.2 = (bf16[1296,128]{1,0:T(8,128)(2,1)S(1)}, bf16[1296,128]{1,0:T(8,128)(2,1)S(1)}, u32[]{:S(2)}, u32[]{:S(2)}) collective-permute-start(bf16[1296,128]{1,0:T(8,128)(2,1)S(1)} %shard_map.129.refs_0_), channel_id=1, source_target_pairs={{0,2},{1,17},{2,0},{3,19},{4,6},{5,21},{6,4},{7,23},{8,10},{9,25},... | collective-permute-start | bytes 995336 | tf_op jit(solution)/shard_map/ppermute | solution.py:35
  16.7 4.0 %shard_map.126 = (bf16[3,66,64,256]{3,2,1,0:T(8,128)(2,1)}, f32[1,256]{1,0:T(1,128)S(1)}) custom-call(bf16[64,64,256]{2,1,0:T(8,128)(2,1)} %bitcast.13), custom_call_target="tpu_custom_call" | custom-call | tf_op jit(solution)/shard_map/pallas_call | solution.py:674
  22.0 2.0 %collective-permute-start.3 = (bf16[1424,128]{1,0:T(8,128)(2,1)S(1)}, bf16[1424,128]{1,0:T(8,128)(2,1)S(1)}, u32[]{:S(2)}, u32[]{:S(2)}) collective-permute-start(bf16[1424,128]{1,0:T(8,128)(2,1)S(1)} %get-tuple-element.59.refs_0_), channel_id=1, source_target_pairs={{0,16},{1,3},{2,18},{3,1},{4,20},{5,7},{6,22},{7,5},{8,24},{9,11},... | collective-permute-start | bytes 1093640 | tf_op jit(solution)/shard_map/ppermute | solution.py:35
  24.1 2.8 %shard_map.127 = (f32[2,256]{1,0:T(2,128)S(1)}, bf16[64,64,256]{2,1,0:T(8,128)(2,1)S(1)}) custom-call(bf16[64,64,256]{2,1,0:T(8,128)(2,1)} %bitcast.15), custom_call_target="tpu_custom_call" | custom-call | tf_op jit(solution)/shard_map/pallas_call | solution.py:674
  26.9 2.6 %collective-permute-done.3.refs_1_ = bf16[1424,128]{1,0:T(8,128)(2,1)S(1)} collective-permute-done((bf16[1424,128]{1,0:T(8,128)(2,1)S(1)}, bf16[1424,128]{1,0:T(8,128)(2,1)S(1)}, u32[]{:S(2)}, u32[]{:S(2)}) %collective-permute-start.3) | collective-permute-done | bytes 364576 | tf_op jit(solution)/shard_map/ppermute | solution.py:35
  29.7 3.0 %collective-permute-done.5.refs_1_ = bf16[1152,128]{1,0:T(8,128)(2,1)S(1)} collective-permute-done((bf16[1152,128]{1,0:T(8,128)(2,1)S(1)}, bf16[1152,128]{1,0:T(8,128)(2,1)S(1)}, u32[]{:S(2)}, u32[]{:S(2)}) %collective-permute-start.5) | collective-permute-done | bytes 294944 | tf_op jit(solution)/shard_map/ppermute | solution.py:35
  33.4 6.4 %shard_map.134 = (bf16[2,256,4224]{2,1,0:T(8,128)(2,1)S(1)}, f32[4096,256]{1,0:T(8,128)S(1)}, f32[2,256]{1,0:T(2,128)S(1)}) custom-call(bf16[64,64,256]{2,1,0:T(8,128)(2,1)S(1)} %get-tuple-element.56.refs_0_.refs_1_, f32[2,256]{1,0:T(2,128)S(1)} %get-tuple-element.57.refs_2_.refs_1_.refs_3_, f32[8,256]{1,0:T(8,128)S(1)} %get-tuple-element.62.refs_2_.refs_3_.refs_5_, ...), custom_call_target="tpu_custom_call" | custom-call | tf_op jit(solution)/shard_map/pallas_call | solution.py:674
  40.1 12.0 %shard_map.136 = (bf16[66,64,256]{2,1,0:T(8,128)(2,1)S(1)}, f32[2,256]{1,0:T(2,128)S(1)}, f32[4608,128]{1,0:T(8,128)S(1)}, bf16[3,66,64,256]{3,2,1,0:T(8,128)(2,1)S(1)}, f32[1,256]{1,0:T(1,128)S(1)}) custom-call(bf16[3,66,64,256]{3,2,1,0:T(8,128)(2,1)S(1)} %copy-done.2, f32[4096,256]{1,0:T(8,128)S(1)} %get-tuple-element.65.refs_1_, ...), custom_call_target="tpu_custom_call" | custom-call | tf_op jit(solution)/shard_map/pallas_call | solution.py:674
  52.9 6.1 %shard_map.139 = (f32[4096,256]{1,0:T(8,128)S(1)}, f32[2,256]{1,0:T(2,128)S(1)}) custom-call(bf16[3,66,64,256]{3,2,1,0:T(8,128)(2,1)S(1)} %get-tuple-element.71.refs_0_.refs_1_, bf16[64,64,256]{2,1,0:T(8,128)(2,1)S(1)} %get-tuple-element.56.refs_0_.refs_1_, f32[2,256]{1,0:T(2,128)S(1)} %get-tuple-element.57.refs_2_.refs_1_.refs_3_, ...), custom_call_target="tpu_custom_call" | custom-call | tf_op jit(solution)/shard_map/pallas_call | solution.py:674
  59.1 2.0 %collective-permute-start.8 = (bf16[1152,128]{1,0:T(8,128)(2,1)S(1)}, bf16[1152,128]{1,0:T(8,128)(2,1)S(1)}, u32[]{:S(2)}, u32[]{:S(2)}) collective-permute-start(bf16[1152,128]{1,0:T(8,128)(2,1)S(1)} %get-tuple-element.83), channel_id=1, source_target_pairs={{0,16},{1,3},{2,18},{3,1},{4,20},{5,7},{6,22},{7,5},{8,24},{9,11},... | collective-permute-start | bytes 884744 | tf_op jit(solution)/shard_map/ppermute | solution.py:35
  61.1 5.0 %shard_map.141.refs_0_ = f32[4608,128]{1,0:T(8,128)S(1)} custom-call(bf16[2,256,4224]{2,1,0:T(8,128)(2,1)S(1)} %get-tuple-element.77.refs_0_, bf16[3,66,64,256]{3,2,1,0:T(8,128)(2,1)S(1)} %get-tuple-element.71.refs_0_.refs_1_), custom_call_target="tpu_custom_call" | custom-call | tf_op jit(solution)/shard_map/pallas_call | solution.py:674
  66.6 2.2 %collective-permute-done.9.refs_1_ = bf16[2832,128]{1,0:T(8,128)(2,1)S(1)} collective-permute-done((bf16[2832,128]{1,0:T(8,128)(2,1)S(1)}, bf16[2832,128]{1,0:T(8,128)(2,1)S(1)}, u32[]{:S(2)}, u32[]{:S(2)}) %collective-permute-start.9) | collective-permute-done | bytes 725024 | tf_op jit(solution)/shard_map/ppermute | solution.py:35
  69.0 1.7 %collective-permute-start.10 = (bf16[1424,128]{1,0:T(8,128)(2,1)S(1)}, bf16[1424,128]{1,0:T(8,128)(2,1)S(1)}, u32[]{:S(2)}, u32[]{:S(2)}) collective-permute-start(bf16[1424,128]{1,0:T(8,128)(2,1)S(1)} %get-tuple-element.87), channel_id=1, source_target_pairs={{0,16},{1,3},{2,18},{3,1},{4,20},{5,7},{6,22},{7,5},{8,24},{9,11},... | collective-permute-start | bytes 1093640 | tf_op jit(solution)/shard_map/ppermute | solution.py:35
  70.7 3.7 %shard_map.137 = (bf16[64,64,256]{2,1,0:T(8,128)(2,1)}, f32[1,256]{1,0:T(1,128)S(1)}) custom-call(bf16[66,64,256]{2,1,0:T(8,128)(2,1)S(1)} %get-tuple-element.68.refs_0_, bf16[64,64,256]{2,1,0:T(8,128)(2,1)S(1)} %get-tuple-element.56.refs_0_.refs_1_, f32[8,256]{1,0:T(8,128)S(1)} %get-tuple-element.62.refs_2_.refs_3_.refs_5_, ...), custom_call_target="tpu_custom_call" | custom-call | tf_op jit(solution)/shard_map/pallas_call | solution.py:674
  74.4 2.1 %collective-permute-done.10.refs_1_ = bf16[1424,128]{1,0:T(8,128)(2,1)S(1)} collective-permute-done((bf16[1424,128]{1,0:T(8,128)(2,1)S(1)}, bf16[1424,128]{1,0:T(8,128)(2,1)S(1)}, u32[]{:S(2)}, u32[]{:S(2)}) %collective-permute-start.10) | collective-permute-done | bytes 364576 | tf_op jit(solution)/shard_map/ppermute | solution.py:35
  78.3 3.4 %shard_map.138 = (bf16[64,64,256]{2,1,0:T(8,128)(2,1)}, f32[1,256]{1,0:T(1,128)S(1)}) custom-call(bf16[66,64,256]{2,1,0:T(8,128)(2,1)S(1)} %get-tuple-element.68.refs_0_, bf16[64,64,256]{2,1,0:T(8,128)(2,1)S(1)} %get-tuple-element.56.refs_0_.refs_1_, f32[8,256]{1,0:T(8,128)S(1)} %get-tuple-element.62.refs_2_.refs_3_.refs_5_, ...), custom_call_target="tpu_custom_call", output_to_operand_aliasing={{0}: (4, {})} | custom-call | tf_op jit(solution)/shard_map/pallas_call | solution.py:674
  81.8 2.0 %collective-permute-done.11.refs_1_ = bf16[1296,128]{1,0:T(8,128)(2,1)S(1)} collective-permute-done((bf16[1296,128]{1,0:T(8,128)(2,1)S(1)}, bf16[1296,128]{1,0:T(8,128)(2,1)S(1)}, u32[]{:S(2)}, u32[]{:S(2)}) %collective-permute-start.11) | collective-permute-done | bytes 331808 | tf_op jit(solution)/shard_map/ppermute | solution.py:35
  85.0 3.5 %shard_map.140 = (f32[64,64,256]{2,1,0:T(8,128)}, f32[1,512]{1,0:T(1,128)}, f32[1,256]{1,0:T(1,128)S(1)}) custom-call(f32[4096,256]{1,0:T(8,128)S(1)} %get-tuple-element.72.refs_0_, bf16[64,64,256]{2,1,0:T(8,128)(2,1)S(1)} %bitcast.16, bf16[64,64,256]{2,1,0:T(8,128)(2,1)S(1)} %bitcast.14, f32[2,256]{1,0:T(2,128)S(1)} %get-tuple-element.57.refs_2_.refs_1_.refs_3_, ...), custom_call_target="tpu_custom_call" | custom-call | tf_op jit(solution)/shard_map/pallas_call | solution.py:674
  89.6 3.3 %collective-permute-start.13 = (bf16[336,128]{1,0:T(8,128)(2,1)S(1)}, bf16[336,128]{1,0:T(8,128)(2,1)S(1)}, u32[]{:S(2)}, u32[]{:S(2)}) collective-permute-start(bf16[336,128]{1,0:T(8,128)(2,1)S(1)} %get-tuple-element.98), channel_id=1, source_target_pairs={{0,8},{1,5},{2,10},{3,7},{4,12},{5,1},{6,14},{7,3},{8,0},{9,13},{1... | collective-permute-start | bytes 258056 | tf_op jit(solution)/shard_map/ppermute | solution.py:35
  92.9 2.5 %collective-permute-done.13.refs_1_ = bf16[336,128]{1,0:T(8,128)(2,1)S(1)} collective-permute-done((bf16[336,128]{1,0:T(8,128)(2,1)S(1)}, bf16[336,128]{1,0:T(8,128)(2,1)S(1)}, u32[]{:S(2)}, u32[]{:S(2)}) %collective-permute-start.13) | collective-permute-done | bytes 86048 | tf_op jit(solution)/shard_map/ppermute | solution.py:35
  (38 shorter events, 10.3 us)
Async XLA Ops:
  2.2 6.5 %collective-permute-start = (bf16[336,128]{1,0:T(8,128)(2,1)S(1)}, bf16[336,128]{1,0:T(8,128)(2,1)S(1)}, u32[]{:S(2)}, u32[]{:S(2)}) collective-permute-start(bf16[336,128]{1,0:T(8,128)(2,1)S(1)} %pad_maximum_fusion.refs_0_), channel_id=1, source_target_pairs={{0,8},{1,5},{2,10},{3,7},{4,12},{5,1},{6,14},{7,3},{8,0},{9,13},{1... | collective-permute-start | bytes 258056 | tf_op jit(solution)/shard_map/ppermute | solution.py:35
  8.7 6.1 %collective-permute-start.1 = (bf16[656,128]{1,0:T(8,128)(2,1)S(1)}, bf16[656,128]{1,0:T(8,128)(2,1)S(1)}, u32[]{:S(2)}, u32[]{:S(2)}) collective-permute-start(bf16[656,128]{1,0:T(8,128)(2,1)S(1)} %shard_map.128.refs_0_), channel_id=1, source_target_pairs={{0,4},{1,9},{2,6},{3,11},{4,0},{5,13},{6,2},{7,15},{8,12},{9,1},{1... | collective-permute-start | bytes 503816 | tf_op jit(solution)/shard_map/ppermute | solution.py:35
  14.8 7.2 %collective-permute-start.2 = (bf16[1296,128]{1,0:T(8,128)(2,1)S(1)}, bf16[1296,128]{1,0:T(8,128)(2,1)S(1)}, u32[]{:S(2)}, u32[]{:S(2)}) collective-permute-start(bf16[1296,128]{1,0:T(8,128)(2,1)S(1)} %shard_map.129.refs_0_), channel_id=1, source_target_pairs={{0,2},{1,17},{2,0},{3,19},{4,6},{5,21},{6,4},{7,23},{8,10},{9,25},... | collective-permute-start | bytes 995336 | tf_op jit(solution)/shard_map/ppermute | solution.py:35
  22.0 10.8 %copy-start.3 = (bf16[1,512]{1,0:T(2,128)(2,1)S(1)}, bf16[1,512]{1,0:T(2,128)(2,1)}, u32[]{:S(2)}) copy-start(bf16[1,512]{1,0:T(2,128)(2,1)} %refs_1_.1) | copy-start | bytes 3076
  22.0 7.5 %collective-permute-start.3 = (bf16[1424,128]{1,0:T(8,128)(2,1)S(1)}, bf16[1424,128]{1,0:T(8,128)(2,1)S(1)}, u32[]{:S(2)}, u32[]{:S(2)}) collective-permute-start(bf16[1424,128]{1,0:T(8,128)(2,1)S(1)} %get-tuple-element.59.refs_0_), channel_id=1, source_target_pairs={{0,16},{1,3},{2,18},{3,1},{4,20},{5,7},{6,22},{7,5},{8,24},{9,11},... | collective-permute-start | bytes 1093640 | tf_op jit(solution)/shard_map/ppermute | solution.py:35
  24.0 8.7 %collective-permute-start.5 = (bf16[1152,128]{1,0:T(8,128)(2,1)S(1)}, bf16[1152,128]{1,0:T(8,128)(2,1)S(1)}, u32[]{:S(2)}, u32[]{:S(2)}) collective-permute-start(bf16[1152,128]{1,0:T(8,128)(2,1)S(1)} %get-tuple-element.60.refs_0_), channel_id=1, source_target_pairs={{0,16},{1,3},{2,18},{3,1},{4,20},{5,7},{6,22},{7,5},{8,24},{9,11},... | collective-permute-start | bytes 884744 | tf_op jit(solution)/shard_map/ppermute | solution.py:35
  29.6 3.2 %collective-permute-start.4 = (bf16[2832,128]{1,0:T(8,128)(2,1)S(1)}, bf16[2832,128]{1,0:T(8,128)(2,1)S(1)}, u32[]{:S(2)}, u32[]{:S(2)}) collective-permute-start(bf16[2832,128]{1,0:T(8,128)(2,1)S(1)} %shard_map.131.refs_0_), channel_id=1, source_target_pairs={{0,1},{1,0},{2,3},{3,2},{4,5},{5,4},{6,7},{7,6},{8,9},{9,8},{10,11... | collective-permute-start | bytes 2174984 | tf_op jit(solution)/shard_map/ppermute | solution.py:35
  32.8 7.0 %collective-permute-start.6 = (bf16[2304,128]{1,0:T(8,128)(2,1)S(1)}, bf16[2304,128]{1,0:T(8,128)(2,1)S(1)}, u32[]{:S(2)}, u32[]{:S(2)}) collective-permute-start(bf16[2304,128]{1,0:T(8,128)(2,1)S(1)} %get-tuple-element.67.refs_0_), channel_id=1, source_target_pairs={{0,1},{1,0},{2,3},{3,2},{4,5},{5,4},{6,7},{7,6},{8,9},{9,8},{10,11... | collective-permute-start | bytes 1769480 | tf_op jit(solution)/shard_map/ppermute | solution.py:35
  32.9 7.2 %copy-start.2 = (bf16[3,66,64,256]{3,2,1,0:T(8,128)(2,1)S(1)}, bf16[3,66,64,256]{3,2,1,0:T(8,128)(2,1)}, u32[]{:S(2)}) copy-start(bf16[3,66,64,256]{3,2,1,0:T(8,128)(2,1)} %get-tuple-element.55.refs_0_) | copy-start | bytes 19464196
  52.3 6.7 %collective-permute-start.7 = (bf16[2304,128]{1,0:T(8,128)(2,1)S(1)}, bf16[2304,128]{1,0:T(8,128)(2,1)S(1)}, u32[]{:S(2)}, u32[]{:S(2)}) collective-permute-start(bf16[2304,128]{1,0:T(8,128)(2,1)S(1)} %get-tuple-element.81), channel_id=1, source_target_pairs={{0,1},{1,0},{2,3},{3,2},{4,5},{5,4},{6,7},{7,6},{8,9},{9,8},{10,11... | collective-permute-start | bytes 1769480 | tf_op jit(solution)/shard_map/ppermute | solution.py:35
  59.1 7.0 %collective-permute-start.8 = (bf16[1152,128]{1,0:T(8,128)(2,1)S(1)}, bf16[1152,128]{1,0:T(8,128)(2,1)S(1)}, u32[]{:S(2)}, u32[]{:S(2)}) collective-permute-start(bf16[1152,128]{1,0:T(8,128)(2,1)S(1)} %get-tuple-element.83), channel_id=1, source_target_pairs={{0,16},{1,3},{2,18},{3,1},{4,20},{5,7},{6,22},{7,5},{8,24},{9,11},... | collective-permute-start | bytes 884744 | tf_op jit(solution)/shard_map/ppermute | solution.py:35
  66.5 2.3 %collective-permute-start.9 = (bf16[2832,128]{1,0:T(8,128)(2,1)S(1)}, bf16[2832,128]{1,0:T(8,128)(2,1)S(1)}, u32[]{:S(2)}, u32[]{:S(2)}) collective-permute-start(bf16[2832,128]{1,0:T(8,128)(2,1)S(1)} %get-tuple-element.85), channel_id=1, source_target_pairs={{0,1},{1,0},{2,3},{3,2},{4,5},{5,4},{6,7},{7,6},{8,9},{9,8},{10,11... | collective-permute-start | bytes 2174984 | tf_op jit(solution)/shard_map/ppermute | solution.py:35
  69.0 7.5 %collective-permute-start.10 = (bf16[1424,128]{1,0:T(8,128)(2,1)S(1)}, bf16[1424,128]{1,0:T(8,128)(2,1)S(1)}, u32[]{:S(2)}, u32[]{:S(2)}) collective-permute-start(bf16[1424,128]{1,0:T(8,128)(2,1)S(1)} %get-tuple-element.87), channel_id=1, source_target_pairs={{0,16},{1,3},{2,18},{3,1},{4,20},{5,7},{6,22},{7,5},{8,24},{9,11},... | collective-permute-start | bytes 1093640 | tf_op jit(solution)/shard_map/ppermute | solution.py:35
  76.6 7.2 %collective-permute-start.11 = (bf16[1296,128]{1,0:T(8,128)(2,1)S(1)}, bf16[1296,128]{1,0:T(8,128)(2,1)S(1)}, u32[]{:S(2)}, u32[]{:S(2)}) collective-permute-start(bf16[1296,128]{1,0:T(8,128)(2,1)S(1)} %get-tuple-element.92), channel_id=1, source_target_pairs={{0,2},{1,17},{2,0},{3,19},{4,6},{5,21},{6,4},{7,23},{8,10},{9,25},... | collective-permute-start | bytes 995336 | tf_op jit(solution)/shard_map/ppermute | solution.py:35
  78.3 6.7 %copy-start = (bf16[1,64,64,256]{3,2,1,0:T(8,128)(2,1)S(1)}, bf16[1,64,64,256]{3,2,1,0:T(8,128)(2,1)}, u32[]{:S(2)}) copy-start(bf16[1,64,64,256]{3,2,1,0:T(8,128)(2,1)} %param.13) | copy-start | bytes 6291460
  78.3 6.7 %copy-start.1 = (bf16[1,64,64,256]{3,2,1,0:T(8,128)(2,1)S(1)}, bf16[1,64,64,256]{3,2,1,0:T(8,128)(2,1)}, u32[]{:S(2)}) copy-start(bf16[1,64,64,256]{3,2,1,0:T(8,128)(2,1)} %param.7) | copy-start | bytes 6291460
  83.9 5.7 %collective-permute-start.12 = (bf16[656,128]{1,0:T(8,128)(2,1)S(1)}, bf16[656,128]{1,0:T(8,128)(2,1)S(1)}, u32[]{:S(2)}, u32[]{:S(2)}) collective-permute-start(bf16[656,128]{1,0:T(8,128)(2,1)S(1)} %get-tuple-element.95), channel_id=1, source_target_pairs={{0,4},{1,9},{2,6},{3,11},{4,0},{5,13},{6,2},{7,15},{8,12},{9,1},{1... | collective-permute-start | bytes 503816 | tf_op jit(solution)/shard_map/ppermute | solution.py:35
  89.6 5.8 %collective-permute-start.13 = (bf16[336,128]{1,0:T(8,128)(2,1)S(1)}, bf16[336,128]{1,0:T(8,128)(2,1)S(1)}, u32[]{:S(2)}, u32[]{:S(2)}) collective-permute-start(bf16[336,128]{1,0:T(8,128)(2,1)S(1)} %get-tuple-element.98), channel_id=1, source_target_pairs={{0,8},{1,5},{2,10},{3,7},{4,12},{5,1},{6,14},{7,3},{8,0},{9,13},{1... | collective-permute-start | bytes 258056 | tf_op jit(solution)/shard_map/ppermute | solution.py:35

commit v5 on v4

--- a/solution.py
+++ b/solution.py
@@ -549,16 +549,15 @@
     halve_kernel(keep, got, send_next, keep_next, 0)
 
 
-def merge_kernel(wide, narrow, one, one_got, two_send, two, send, keep):
-    slots = two.shape[0] // narrow
+def merge_kernel(wide, narrow, one, one_got, two, two_got, send, keep):
+    slots = two.shape[0] // narrow // 2
     for slot in range(slots):
         to = slot * (wide + narrow)
-        at, up = slot * wide, (slots + slot) * wide
-        keep[to : to + wide, :] = one[at : at + wide, :] + one_got[at : at + wide, :].astype(F32)
-        send[to : to + wide, :] = (one[up : up + wide, :] + one_got[up : up + wide, :].astype(F32)).astype(BF16)
-        at, to, up = slot * narrow, to + wide, to + wide + narrow
-        keep[to:up, :] = two[at : at + narrow, :]
-        send[to:up, :] = two_send[at : at + narrow, :]
+        for mine, got, rows in ((one, one_got, wide), (two, two_got, narrow)):
+            at, up = slot * rows, (slots + slot) * rows
+            keep[to : to + rows, :] = mine[at : at + rows, :] + got[at : at + rows, :].astype(F32)
+            send[to : to + rows, :] = (mine[up : up + rows, :] + got[up : up + rows, :].astype(F32)).astype(BF16)
+            to += rows
     at, to = 2 * slots * wide, slots * (wide + narrow)
     values = one[at:, :] + one_got[at:, :].astype(F32)
     keep[to:, :] = values
@@ -622,31 +621,30 @@
 
 
 def pack_first_kernel(
-    wires, cuts, flat_one, embedding, dc_sum, sums_one, sums_two, g_sum, two, two_got,
-    send, keep, two_send, two_keep, flat_project,
+    wires, cuts, flat_one, dc_sum, sums_one, sums_two, g_sum, two, two_got, send, keep, two_send, two_keep
 ):
     halve_kernel(two, two_got, two_send, two_keep, 0)
+    take_blocks(wires, cuts, (flat_one,), send, keep)
+    at = wires.slots * sum(cuts)
+    vectors = [sums_one[0:1, :], sums_one[1:2, :], dc_sum[...], sums_two[0:1, :], sums_two[1:2, :], g_sum[...]]
+    halves = [row[:, i * LANES : (i + 1) * LANES] for row in vectors for i in range(2)]
+    values = jnp.concatenate(halves + [jnp.zeros((VEC_ROWS - len(halves), LANES), F32)], axis=0)
+    keep[at : at + VEC_ROWS, :] = values
+    send[at : at + VEC_ROWS, :] = values.astype(BF16)
+
+
+def pack_second_kernel(wires, cuts, flat_two, embedding, dc_sum, send, keep, flat_project):
     emb = embedding[...].astype(F32)
     q = (emb * sigmoid(emb)).astype(BF16).astype(F32)
     q = jnp.broadcast_to(q, (LANES, q.shape[1])).T
     dc = dc_sum[...]
     store_flat(flat_project, 0, jnp.concatenate([q * dc[:, :LANES], q * dc[:, LANES:]], axis=1))
-    take_blocks(wires, cuts, (flat_one, flat_project), send, keep)
-    at = wires.slots * sum(cuts)
-    vectors = [sums_one[0:1, :], sums_one[1:2, :], dc, sums_two[0:1, :], sums_two[1:2, :], g_sum[...]]
-    halves = [row[:, i * LANES : (i + 1) * LANES] for row in vectors for i in range(2)]
-    values = jnp.concatenate(halves + [jnp.zeros((VEC_ROWS - len(halves), LANES), F32)], axis=0)
-    keep[at : at + VEC_ROWS, :] = values
-    send[at : at + VEC_ROWS, :] = values.astype(BF16)
-
-
-def pack_second_kernel(wires, cuts, flat, send, keep):
-    take_blocks(wires, cuts, (flat,), send, keep)
-
-
-def finish_kernel(wires, cuts, n_vec, keep, got, one, project, two, vec):
+    take_blocks(wires, cuts, (flat_two, flat_project), send, keep)
+
+
+def finish_kernel(wires, cuts, n_vec, keep, got, one, two, project, vec):
     at = 0
-    for out, rows in zip((one, project, two), cuts):
+    for out, rows in zip((one, two, project), cuts):
         out[...] = keep[at : at + rows, :] + got[at : at + rows, :].astype(F32)
         at += rows
     vectors = keep[at : at + VEC_ROWS, :] + got[at : at + VEC_ROWS, :].astype(F32)
@@ -755,34 +753,40 @@
     return halves[0].astype(BF16), halves[1]
 
 
-def pack_first(wires, cuts, flat_one, embedding, dc_sum, sums_one, sums_two, g_sum, two, two_got):
+def pack_first(wires, cuts, flat_one, dc_sum, sums_one, sums_two, g_sum, two, two_got):
     shape = (wires.slots * sum(cuts) + VEC_ROWS, LANES)
     if all(rows % 8 == 0 for rows in cuts):
         return call(
             functools.partial(pack_first_kernel, wires, cuts),
             [(shape, BF16), (shape, F32), *halved(two, 0)],
             flat_one,
-            embedding,
             dc_sum,
             sums_one,
             sums_two,
             g_sum,
             two,
             two_got,
+        )
+    vec = jnp.concatenate([sums_one, dc_sum, sums_two, g_sum]).reshape(-1, LANES)
+    vec = jnp.pad(vec, ((0, VEC_ROWS - vec.shape[0]), (0, 0)))
+    send, keep = out_of_order(wires, cuts, (flat_one,), vec)
+    return send, keep, *call(halve_second_kernel, halved(two, 0), two, two_got)
+
+
+def pack_second(wires, cuts, flat_two, embedding, dc_sum):
+    if all(rows % 8 == 0 for rows in cuts):
+        shape = (wires.slots * sum(cuts), LANES)
+        return call(
+            functools.partial(pack_second_kernel, wires, cuts),
+            [(shape, BF16), (shape, F32)],
+            flat_two,
+            embedding,
+            dc_sum,
             scratch=[((wires.n * cuts[1], LANES), F32)],
         )
     q = jax.nn.silu(embedding.astype(F32)).astype(BF16).astype(F32).reshape(-1, 1)
-    vec = jnp.concatenate([sums_one, dc_sum, sums_two, g_sum]).reshape(-1, LANES)
-    vec = jnp.pad(vec, ((0, VEC_ROWS - vec.shape[0]), (0, 0)))
-    send, keep = out_of_order(wires, cuts, (flat_one, (q * dc_sum).reshape(-1, LANES)), vec)
-    return send, keep, *call(halve_second_kernel, halved(two, 0), two, two_got)
-
-
-def pack_second(wires, cuts, flat):
-    if cuts[0] % 8 == 0:
-        shape = (wires.slots * cuts[0], LANES)
-        return call(functools.partial(pack_second_kernel, wires, cuts), [(shape, BF16), (shape, F32)], flat)
-    return out_of_order(wires, cuts, (flat,), jnp.zeros((0, LANES), F32))
+    parts = (flat_two, (q * dc_sum).reshape(-1, LANES))
+    return out_of_order(wires, cuts, parts, jnp.zeros((0, LANES), F32))
 
 
 def halved(keep, tail=VEC_ROWS):
@@ -836,15 +840,12 @@
         flops=2 * conv_flops,
     )
     last = wires.stages
-    two_send, two = pack_second(wires, cuts[1:2], grad_two)
+    two_send, two = pack_second(wires, cuts[1:], grad_two, embedding, dc_sum)
     two_got = wires.swap(two_send, last)
     dh_one, sums_one = call(third_kernel, [flat, pair], e_three, x_near, stats, vec, first, flops=conv_flops)
-    two_send, two = call(halve_second_kernel, halved(two, 0), two, two_got, after=(sums_one,))
-    two_got = wires.swap(two_send, last - 1)
     grad_one, = call(grad_kernel, [taps], turned_one, e_three, flops=conv_flops)
-    one_cuts = (cuts[0], cuts[2])
     one_send, one, two_send, two = pack_first(
-        wires, one_cuts, grad_one, embedding, dc_sum, sums_one, sums_two, g_sum, two, two_got
+        wires, cuts[:1], grad_one, dc_sum, sums_one, sums_two, g_sum, two, two_got
     )
     input_grad, embedding_grad, input_done = call(
         input_kernel,
@@ -879,31 +880,29 @@
             flops=conv_flops // parts,
         )
         output_done.append(done)
-    one_got = wires.swap(one_send, last)
-    one_send, one = call(halve_kernel, halved(one), one, one_got)
+    two_got = wires.swap(two_send, last - 1)
+    one_send, one = call(halve_kernel, halved(one), one, wires.swap(one_send, last))
     one_got = wires.swap(one_send, last - 1)
-    wide, narrow = sum(one_cuts), cuts[1]
+    wide, narrow = cuts[0], sum(cuts[1:])
     shape = (wires.slots // 4 * (wide + narrow) + VEC_ROWS, LANES)
     send, keep = call(
         functools.partial(merge_kernel, wide, narrow),
         [(shape, BF16), (shape, F32)],
         one,
         one_got,
-        two_send,
         two,
-        after=(output_done[0],),
+        two_got,
+        after=output_done[:1],
     )
     for stage in range(last - 2, 0, -1):
-        after = {last - 2: (output_done[1],), last - 3: (input_done,)}.get(stage, ())
+        after = {last - 3: (input_done,), last - 2: (output_done[1],)}.get(stage, ())
         send, keep = call(halve_kernel, halved(keep), keep, wires.swap(send, stage), after=after)
-    all_cuts = (*one_cuts, cuts[1])
-    first_sum, project_sum, second_sum, vec_sum = call(
-        functools.partial(finish_kernel, wires, all_cuts, n_vec),
-        [*[((rows, LANES), F32) for rows in all_cuts], ((1, n_vec), F32)],
+    summed = call(
+        functools.partial(finish_kernel, wires, cuts, n_vec),
+        [*[((rows, LANES), F32) for rows in cuts], ((1, n_vec), F32)],
         keep,
         wires.swap(send, 0),
     )
-    summed = (first_sum, second_sum, project_sum, vec_sum)
     return (output[0][None], input_grad[None], embedding_grad, *[v.reshape(-1) for v in summed])
 
 

time: 96.3 us -> 95.3 us (0.990)
  waiting for transfers between devices: 23.3 us -> 21.8 us
    ppermute x14, waiting for transfers between devices: 23.3 us -> 21.8 us  [swap(): lax.ppermute(value, AXES, [(i, i ^ 1 << bit(i & 1)) for i in range(self.n)])]
    pallas_call x24 -> x23, Pallas kernels: 49.7 us -> 49.6 us  [call(): pl.pallas_call(run, out_shape=[pltpu.HBM(shape, dtype) if i in far_outs e...]
  transfers between devices with their start and end apart: 14 -> 14, of which waited for: 10 -> 9; matrix products, arithmetic and copies ran while one was open for 0% -> 0% of each run, Pallas kernels for 37% -> 38%
where the time goes in v5:
time: 95.3 us; the launch traced here: 95 us
  Pallas kernels  49.6 us (52%)
  waiting for transfers between devices  21.8 us (23%)
  starting transfers between devices  21.2 us (22%)
    pallas_call x23, Pallas kernels, call(): pl.pallas_call(run, out_shape=[pltpu.HBM(shape, dtype) if i in far_outs e...  49.6 us
    ppermute x14, waiting for transfers between devices, swap(): lax.ppermute(value, AXES, [(i, i ^ 1 << bit(i & 1)) for i in range(self.n)])  21.8 us
    ppermute x14, starting transfers between devices, swap(): lax.ppermute(value, AXES, [(i, i ^ 1 << bit(i & 1)) for i in range(self.n)])  21.2 us
  transfers between devices with their start and end apart: 14, of which 9 were waited for; matrix products, arithmetic and copies ran while one was open for 0% of the time, Pallas kernels for 38%

profile of v5, /device:TPU:0, one launch (start us, length us, event | category | flops | bytes accessed | tf_op | source)
XLA Modules:
  0.0 95.0 jit_solution(8626771177869147943)
XLA Ops:
  2.2 4.0 %collective-permute-start = (bf16[336,128]{1,0:T(8,128)(2,1)S(1)}, bf16[336,128]{1,0:T(8,128)(2,1)S(1)}, u32[]{:S(2)}, u32[]{:S(2)}) collective-permute-start(bf16[336,128]{1,0:T(8,128)(2,1)S(1)} %pad_maximum_fusion.refs_0_), channel_id=1, source_target_pairs={{0,8},{1,5},{2,10},{3,7},{4,12},{5,1},{6,14},{7,3},{8,0},{9,13},{1... | collective-permute-start | bytes 258056 | tf_op jit(solution)/shard_map/ppermute | solution.py:35
  6.2 2.5 %collective-permute-done.refs_1_ = bf16[336,128]{1,0:T(8,128)(2,1)S(1)} collective-permute-done((bf16[336,128]{1,0:T(8,128)(2,1)S(1)}, bf16[336,128]{1,0:T(8,128)(2,1)S(1)}, u32[]{:S(2)}, u32[]{:S(2)}) %collective-permute-start) | collective-permute-done | bytes 86048 | tf_op jit(solution)/shard_map/ppermute | solution.py:35
  8.7 2.0 %collective-permute-start.1 = (bf16[656,128]{1,0:T(8,128)(2,1)S(1)}, bf16[656,128]{1,0:T(8,128)(2,1)S(1)}, u32[]{:S(2)}, u32[]{:S(2)}) collective-permute-start(bf16[656,128]{1,0:T(8,128)(2,1)S(1)} %shard_map.128.refs_0_), channel_id=1, source_target_pairs={{0,4},{1,9},{2,6},{3,11},{4,0},{5,13},{6,2},{7,15},{8,12},{9,1},{1... | collective-permute-start | bytes 503816 | tf_op jit(solution)/shard_map/ppermute | solution.py:35
  10.7 4.1 %collective-permute-done.1.refs_1_ = bf16[656,128]{1,0:T(8,128)(2,1)S(1)} collective-permute-done((bf16[656,128]{1,0:T(8,128)(2,1)S(1)}, bf16[656,128]{1,0:T(8,128)(2,1)S(1)}, u32[]{:S(2)}, u32[]{:S(2)}) %collective-permute-start.1) | collective-permute-done | bytes 167968 | tf_op jit(solution)/shard_map/ppermute | solution.py:35
  14.8 1.9 %collective-permute-start.2 = (bf16[1296,128]{1,0:T(8,128)(2,1)S(1)}, bf16[1296,128]{1,0:T(8,128)(2,1)S(1)}, u32[]{:S(2)}, u32[]{:S(2)}) collective-permute-start(bf16[1296,128]{1,0:T(8,128)(2,1)S(1)} %shard_map.129.refs_0_), channel_id=1, source_target_pairs={{0,2},{1,17},{2,0},{3,19},{4,6},{5,21},{6,4},{7,23},{8,10},{9,25},... | collective-permute-start | bytes 995336 | tf_op jit(solution)/shard_map/ppermute | solution.py:35
  16.7 4.0 %shard_map.126 = (bf16[3,66,64,256]{3,2,1,0:T(8,128)(2,1)}, f32[1,256]{1,0:T(1,128)S(1)}) custom-call(bf16[64,64,256]{2,1,0:T(8,128)(2,1)} %bitcast.13), custom_call_target="tpu_custom_call" | custom-call | tf_op jit(solution)/shard_map/pallas_call | solution.py:672
  22.0 2.0 %collective-permute-start.3 = (bf16[1424,128]{1,0:T(8,128)(2,1)S(1)}, bf16[1424,128]{1,0:T(8,128)(2,1)S(1)}, u32[]{:S(2)}, u32[]{:S(2)}) collective-permute-start(bf16[1424,128]{1,0:T(8,128)(2,1)S(1)} %get-tuple-element.57.refs_0_), channel_id=1, source_target_pairs={{0,16},{1,3},{2,18},{3,1},{4,20},{5,7},{6,22},{7,5},{8,24},{9,11},... | collective-permute-start | bytes 1093640 | tf_op jit(solution)/shard_map/ppermute | solution.py:35
  24.1 2.8 %shard_map.127 = (f32[2,256]{1,0:T(2,128)S(1)}, bf16[64,64,256]{2,1,0:T(8,128)(2,1)S(1)}) custom-call(bf16[64,64,256]{2,1,0:T(8,128)(2,1)} %bitcast.15), custom_call_target="tpu_custom_call" | custom-call | tf_op jit(solution)/shard_map/pallas_call | solution.py:672
  26.9 2.6 %collective-permute-done.3.refs_1_ = bf16[1424,128]{1,0:T(8,128)(2,1)S(1)} collective-permute-done((bf16[1424,128]{1,0:T(8,128)(2,1)S(1)}, bf16[1424,128]{1,0:T(8,128)(2,1)S(1)}, u32[]{:S(2)}, u32[]{:S(2)}) %collective-permute-start.3) | collective-permute-done | bytes 364576 | tf_op jit(solution)/shard_map/ppermute | solution.py:35
  29.7 3.0 %collective-permute-done.5.refs_1_ = bf16[1152,128]{1,0:T(8,128)(2,1)S(1)} collective-permute-done((bf16[1152,128]{1,0:T(8,128)(2,1)S(1)}, bf16[1152,128]{1,0:T(8,128)(2,1)S(1)}, u32[]{:S(2)}, u32[]{:S(2)}) %collective-permute-start.5) | collective-permute-done | bytes 294944 | tf_op jit(solution)/shard_map/ppermute | solution.py:35
  33.4 6.4 %shard_map.134 = (bf16[2,256,4224]{2,1,0:T(8,128)(2,1)S(1)}, f32[4096,256]{1,0:T(8,128)S(1)}, f32[2,256]{1,0:T(2,128)S(1)}) custom-call(bf16[64,64,256]{2,1,0:T(8,128)(2,1)S(1)} %get-tuple-element.54.refs_0_.refs_1_, f32[2,256]{1,0:T(2,128)S(1)} %get-tuple-element.55.refs_2_.refs_1_.refs_3_, f32[8,256]{1,0:T(8,128)S(1)} %get-tuple-element.60.refs_2_.refs_3_.refs_5_, ...), custom_call_target="tpu_custom_call" | custom-call | tf_op jit(solution)/shard_map/pallas_call | solution.py:672
  40.1 12.0 %shard_map.136 = (bf16[66,64,256]{2,1,0:T(8,128)(2,1)S(1)}, f32[2,256]{1,0:T(2,128)S(1)}, f32[4608,128]{1,0:T(8,128)S(1)}, bf16[3,66,64,256]{3,2,1,0:T(8,128)(2,1)S(1)}, f32[1,256]{1,0:T(1,128)S(1)}) custom-call(bf16[3,66,64,256]{3,2,1,0:T(8,128)(2,1)S(1)} %copy-done.2, f32[4096,256]{1,0:T(8,128)S(1)} %get-tuple-element.63.refs_1_, ...), custom_call_target="tpu_custom_call" | custom-call | tf_op jit(solution)/shard_map/pallas_call | solution.py:672
  53.0 6.1 %shard_map.139 = (f32[4096,256]{1,0:T(8,128)S(1)}, f32[2,256]{1,0:T(2,128)S(1)}) custom-call(bf16[3,66,64,256]{3,2,1,0:T(8,128)(2,1)S(1)} %get-tuple-element.69.refs_0_.refs_1_, bf16[64,64,256]{2,1,0:T(8,128)(2,1)S(1)} %get-tuple-element.54.refs_0_.refs_1_, f32[2,256]{1,0:T(2,128)S(1)} %get-tuple-element.55.refs_2_.refs_1_.refs_3_, ...), custom_call_target="tpu_custom_call" | custom-call | tf_op jit(solution)/shard_map/pallas_call | solution.py:672
  59.1 5.0 %shard_map.141.refs_0_ = f32[4608,128]{1,0:T(8,128)S(1)} custom-call(bf16[2,256,4224]{2,1,0:T(8,128)(2,1)S(1)} %get-tuple-element.75.refs_0_, bf16[3,66,64,256]{3,2,1,0:T(8,128)(2,1)S(1)} %get-tuple-element.69.refs_0_.refs_1_), custom_call_target="tpu_custom_call" | custom-call | tf_op jit(solution)/shard_map/pallas_call | solution.py:672
  64.5 1.9 %collective-permute-start.10 = (bf16[1408,128]{1,0:T(8,128)(2,1)S(1)}, bf16[1408,128]{1,0:T(8,128)(2,1)S(1)}, u32[]{:S(2)}, u32[]{:S(2)}) collective-permute-start(bf16[1408,128]{1,0:T(8,128)(2,1)S(1)} %get-tuple-element.85), channel_id=1, source_target_pairs={{0,16},{1,3},{2,18},{3,1},{4,20},{5,7},{6,22},{7,5},{8,24},{9,11},... | collective-permute-start | bytes 1081352 | tf_op jit(solution)/shard_map/ppermute | solution.py:35
  66.7 2.0 %collective-permute-start.9 = (bf16[1168,128]{1,0:T(8,128)(2,1)S(1)}, bf16[1168,128]{1,0:T(8,128)(2,1)S(1)}, u32[]{:S(2)}, u32[]{:S(2)}) collective-permute-start(bf16[1168,128]{1,0:T(8,128)(2,1)S(1)} %get-tuple-element.83), channel_id=1, source_target_pairs={{0,16},{1,3},{2,18},{3,1},{4,20},{5,7},{6,22},{7,5},{8,24},{9,11},... | collective-permute-start | bytes 897032 | tf_op jit(solution)/shard_map/ppermute | solution.py:35
  68.6 3.7 %shard_map.137 = (bf16[64,64,256]{2,1,0:T(8,128)(2,1)}, f32[1,256]{1,0:T(1,128)S(1)}) custom-call(bf16[66,64,256]{2,1,0:T(8,128)(2,1)S(1)} %get-tuple-element.66.refs_0_, bf16[64,64,256]{2,1,0:T(8,128)(2,1)S(1)} %get-tuple-element.54.refs_0_.refs_1_, f32[8,256]{1,0:T(8,128)S(1)} %get-tuple-element.60.refs_2_.refs_3_.refs_5_, ...), custom_call_target="tpu_custom_call" | custom-call | tf_op jit(solution)/shard_map/pallas_call | solution.py:672
  72.3 2.9 %collective-permute-done.9.refs_1_ = bf16[1168,128]{1,0:T(8,128)(2,1)S(1)} collective-permute-done((bf16[1168,128]{1,0:T(8,128)(2,1)S(1)}, bf16[1168,128]{1,0:T(8,128)(2,1)S(1)}, u32[]{:S(2)}, u32[]{:S(2)}) %collective-permute-start.9) | collective-permute-done | bytes 299040 | tf_op jit(solution)/shard_map/ppermute | solution.py:35
  75.3 1.9 %collective-permute-start.11 = (bf16[1296,128]{1,0:T(8,128)(2,1)S(1)}, bf16[1296,128]{1,0:T(8,128)(2,1)S(1)}, u32[]{:S(2)}, u32[]{:S(2)}) collective-permute-start(bf16[1296,128]{1,0:T(8,128)(2,1)S(1)} %get-tuple-element.88), channel_id=1, source_target_pairs={{0,2},{1,17},{2,0},{3,19},{4,6},{5,21},{6,4},{7,23},{8,10},{9,25},... | collective-permute-start | bytes 995336 | tf_op jit(solution)/shard_map/ppermute | solution.py:35
  77.3 3.4 %shard_map.138 = (bf16[64,64,256]{2,1,0:T(8,128)(2,1)}, f32[1,256]{1,0:T(1,128)S(1)}) custom-call(bf16[66,64,256]{2,1,0:T(8,128)(2,1)S(1)} %get-tuple-element.66.refs_0_, bf16[64,64,256]{2,1,0:T(8,128)(2,1)S(1)} %get-tuple-element.54.refs_0_.refs_1_, f32[8,256]{1,0:T(8,128)S(1)} %get-tuple-element.60.refs_2_.refs_3_.refs_5_, ...), custom_call_target="tpu_custom_call", output_to_operand_aliasing={{0}: (4, {})} | custom-call | tf_op jit(solution)/shard_map/pallas_call | solution.py:672
  80.7 1.8 %collective-permute-done.11.refs_1_ = bf16[1296,128]{1,0:T(8,128)(2,1)S(1)} collective-permute-done((bf16[1296,128]{1,0:T(8,128)(2,1)S(1)}, bf16[1296,128]{1,0:T(8,128)(2,1)S(1)}, u32[]{:S(2)}, u32[]{:S(2)}) %collective-permute-start.11) | collective-permute-done | bytes 331808 | tf_op jit(solution)/shard_map/ppermute | solution.py:35
  84.0 3.5 %shard_map.140 = (f32[64,64,256]{2,1,0:T(8,128)}, f32[1,512]{1,0:T(1,128)}, f32[1,256]{1,0:T(1,128)S(1)}) custom-call(f32[4096,256]{1,0:T(8,128)S(1)} %get-tuple-element.70.refs_0_, bf16[64,64,256]{2,1,0:T(8,128)(2,1)S(1)} %bitcast.16, bf16[64,64,256]{2,1,0:T(8,128)(2,1)S(1)} %bitcast.14, f32[2,256]{1,0:T(2,128)S(1)} %get-tuple-element.55.refs_2_.refs_1_.refs_3_, ...), custom_call_target="tpu_custom_call" | custom-call | tf_op jit(solution)/shard_map/pallas_call | solution.py:672
  88.7 3.2 %collective-permute-start.13 = (bf16[336,128]{1,0:T(8,128)(2,1)S(1)}, bf16[336,128]{1,0:T(8,128)(2,1)S(1)}, u32[]{:S(2)}, u32[]{:S(2)}) collective-permute-start(bf16[336,128]{1,0:T(8,128)(2,1)S(1)} %get-tuple-element.94), channel_id=1, source_target_pairs={{0,8},{1,5},{2,10},{3,7},{4,12},{5,1},{6,14},{7,3},{8,0},{9,13},{1... | collective-permute-start | bytes 258056 | tf_op jit(solution)/shard_map/ppermute | solution.py:35
  91.9 2.5 %collective-permute-done.13.refs_1_ = bf16[336,128]{1,0:T(8,128)(2,1)S(1)} collective-permute-done((bf16[336,128]{1,0:T(8,128)(2,1)S(1)}, bf16[336,128]{1,0:T(8,128)(2,1)S(1)}, u32[]{:S(2)}, u32[]{:S(2)}) %collective-permute-start.13) | collective-permute-done | bytes 86048 | tf_op jit(solution)/shard_map/ppermute | solution.py:35
  (37 shorter events, 8.9 us)
Async XLA Ops:
  2.2 6.5 %collective-permute-start = (bf16[336,128]{1,0:T(8,128)(2,1)S(1)}, bf16[336,128]{1,0:T(8,128)(2,1)S(1)}, u32[]{:S(2)}, u32[]{:S(2)}) collective-permute-start(bf16[336,128]{1,0:T(8,128)(2,1)S(1)} %pad_maximum_fusion.refs_0_), channel_id=1, source_target_pairs={{0,8},{1,5},{2,10},{3,7},{4,12},{5,1},{6,14},{7,3},{8,0},{9,13},{1... | collective-permute-start | bytes 258056 | tf_op jit(solution)/shard_map/ppermute | solution.py:35
  8.7 6.1 %collective-permute-start.1 = (bf16[656,128]{1,0:T(8,128)(2,1)S(1)}, bf16[656,128]{1,0:T(8,128)(2,1)S(1)}, u32[]{:S(2)}, u32[]{:S(2)}) collective-permute-start(bf16[656,128]{1,0:T(8,128)(2,1)S(1)} %shard_map.128.refs_0_), channel_id=1, source_target_pairs={{0,4},{1,9},{2,6},{3,11},{4,0},{5,13},{6,2},{7,15},{8,12},{9,1},{1... | collective-permute-start | bytes 503816 | tf_op jit(solution)/shard_map/ppermute | solution.py:35
  14.8 7.2 %collective-permute-start.2 = (bf16[1296,128]{1,0:T(8,128)(2,1)S(1)}, bf16[1296,128]{1,0:T(8,128)(2,1)S(1)}, u32[]{:S(2)}, u32[]{:S(2)}) collective-permute-start(bf16[1296,128]{1,0:T(8,128)(2,1)S(1)} %shard_map.129.refs_0_), channel_id=1, source_target_pairs={{0,2},{1,17},{2,0},{3,19},{4,6},{5,21},{6,4},{7,23},{8,10},{9,25},... | collective-permute-start | bytes 995336 | tf_op jit(solution)/shard_map/ppermute | solution.py:35
  22.0 10.8 %copy-start.3 = (bf16[1,512]{1,0:T(2,128)(2,1)S(1)}, bf16[1,512]{1,0:T(2,128)(2,1)}, u32[]{:S(2)}) copy-start(bf16[1,512]{1,0:T(2,128)(2,1)} %refs_1_.1) | copy-start | bytes 3076
  22.0 7.5 %collective-permute-start.3 = (bf16[1424,128]{1,0:T(8,128)(2,1)S(1)}, bf16[1424,128]{1,0:T(8,128)(2,1)S(1)}, u32[]{:S(2)}, u32[]{:S(2)}) collective-permute-start(bf16[1424,128]{1,0:T(8,128)(2,1)S(1)} %get-tuple-element.57.refs_0_), channel_id=1, source_target_pairs={{0,16},{1,3},{2,18},{3,1},{4,20},{5,7},{6,22},{7,5},{8,24},{9,11},... | collective-permute-start | bytes 1093640 | tf_op jit(solution)/shard_map/ppermute | solution.py:35
  24.0 8.7 %collective-permute-start.5 = (bf16[1152,128]{1,0:T(8,128)(2,1)S(1)}, bf16[1152,128]{1,0:T(8,128)(2,1)S(1)}, u32[]{:S(2)}, u32[]{:S(2)}) collective-permute-start(bf16[1152,128]{1,0:T(8,128)(2,1)S(1)} %get-tuple-element.58.refs_0_), channel_id=1, source_target_pairs={{0,16},{1,3},{2,18},{3,1},{4,20},{5,7},{6,22},{7,5},{8,24},{9,11},... | collective-permute-start | bytes 884744 | tf_op jit(solution)/shard_map/ppermute | solution.py:35
  29.6 3.2 %collective-permute-start.4 = (bf16[2832,128]{1,0:T(8,128)(2,1)S(1)}, bf16[2832,128]{1,0:T(8,128)(2,1)S(1)}, u32[]{:S(2)}, u32[]{:S(2)}) collective-permute-start(bf16[2832,128]{1,0:T(8,128)(2,1)S(1)} %shard_map.131.refs_0_), channel_id=1, source_target_pairs={{0,1},{1,0},{2,3},{3,2},{4,5},{5,4},{6,7},{7,6},{8,9},{9,8},{10,11... | collective-permute-start | bytes 2174984 | tf_op jit(solution)/shard_map/ppermute | solution.py:35
  32.8 7.0 %collective-permute-start.6 = (bf16[2304,128]{1,0:T(8,128)(2,1)S(1)}, bf16[2304,128]{1,0:T(8,128)(2,1)S(1)}, u32[]{:S(2)}, u32[]{:S(2)}) collective-permute-start(bf16[2304,128]{1,0:T(8,128)(2,1)S(1)} %get-tuple-element.65.refs_0_), channel_id=1, source_target_pairs={{0,1},{1,0},{2,3},{3,2},{4,5},{5,4},{6,7},{7,6},{8,9},{9,8},{10,11... | collective-permute-start | bytes 1769480 | tf_op jit(solution)/shard_map/ppermute | solution.py:35
  32.9 7.2 %copy-start.2 = (bf16[3,66,64,256]{3,2,1,0:T(8,128)(2,1)S(1)}, bf16[3,66,64,256]{3,2,1,0:T(8,128)(2,1)}, u32[]{:S(2)}) copy-start(bf16[3,66,64,256]{3,2,1,0:T(8,128)(2,1)} %get-tuple-element.53.refs_0_) | copy-start | bytes 19464196
  52.4 11.7 %collective-permute-start.7 = (bf16[2816,128]{1,0:T(8,128)(2,1)S(1)}, bf16[2816,128]{1,0:T(8,128)(2,1)S(1)}, u32[]{:S(2)}, u32[]{:S(2)}) collective-permute-start(bf16[2816,128]{1,0:T(8,128)(2,1)S(1)} %get-tuple-element.79), channel_id=1, source_target_pairs={{0,1},{1,0},{2,3},{3,2},{4,5},{5,4},{6,7},{7,6},{8,9},{9,8},{10,11... | collective-permute-start | bytes 2162696 | tf_op jit(solution)/shard_map/ppermute | solution.py:35
  64.4 2.1 %collective-permute-start.8 = (bf16[2320,128]{1,0:T(8,128)(2,1)S(1)}, bf16[2320,128]{1,0:T(8,128)(2,1)S(1)}, u32[]{:S(2)}, u32[]{:S(2)}) collective-permute-start(bf16[2320,128]{1,0:T(8,128)(2,1)S(1)} %get-tuple-element.81), channel_id=1, source_target_pairs={{0,1},{1,0},{2,3},{3,2},{4,5},{5,4},{6,7},{7,6},{8,9},{9,8},{10,11... | collective-permute-start | bytes 1781768 | tf_op jit(solution)/shard_map/ppermute | solution.py:35
  64.5 7.7 %collective-permute-start.10 = (bf16[1408,128]{1,0:T(8,128)(2,1)S(1)}, bf16[1408,128]{1,0:T(8,128)(2,1)S(1)}, u32[]{:S(2)}, u32[]{:S(2)}) collective-permute-start(bf16[1408,128]{1,0:T(8,128)(2,1)S(1)} %get-tuple-element.85), channel_id=1, source_target_pairs={{0,16},{1,3},{2,18},{3,1},{4,20},{5,7},{6,22},{7,5},{8,24},{9,11},... | collective-permute-start | bytes 1081352 | tf_op jit(solution)/shard_map/ppermute | solution.py:35
  66.7 8.6 %collective-permute-start.9 = (bf16[1168,128]{1,0:T(8,128)(2,1)S(1)}, bf16[1168,128]{1,0:T(8,128)(2,1)S(1)}, u32[]{:S(2)}, u32[]{:S(2)}) collective-permute-start(bf16[1168,128]{1,0:T(8,128)(2,1)S(1)} %get-tuple-element.83), channel_id=1, source_target_pairs={{0,16},{1,3},{2,18},{3,1},{4,20},{5,7},{6,22},{7,5},{8,24},{9,11},... | collective-permute-start | bytes 897032 | tf_op jit(solution)/shard_map/ppermute | solution.py:35
  75.3 7.2 %collective-permute-start.11 = (bf16[1296,128]{1,0:T(8,128)(2,1)S(1)}, bf16[1296,128]{1,0:T(8,128)(2,1)S(1)}, u32[]{:S(2)}, u32[]{:S(2)}) collective-permute-start(bf16[1296,128]{1,0:T(8,128)(2,1)S(1)} %get-tuple-element.88), channel_id=1, source_target_pairs={{0,2},{1,17},{2,0},{3,19},{4,6},{5,21},{6,4},{7,23},{8,10},{9,25},... | collective-permute-start | bytes 995336 | tf_op jit(solution)/shard_map/ppermute | solution.py:35
  77.3 6.7 %copy-start = (bf16[1,64,64,256]{3,2,1,0:T(8,128)(2,1)S(1)}, bf16[1,64,64,256]{3,2,1,0:T(8,128)(2,1)}, u32[]{:S(2)}) copy-start(bf16[1,64,64,256]{3,2,1,0:T(8,128)(2,1)} %param.13) | copy-start | bytes 6291460
  77.3 6.7 %copy-start.1 = (bf16[1,64,64,256]{3,2,1,0:T(8,128)(2,1)S(1)}, bf16[1,64,64,256]{3,2,1,0:T(8,128)(2,1)}, u32[]{:S(2)}) copy-start(bf16[1,64,64,256]{3,2,1,0:T(8,128)(2,1)} %param.7) | copy-start | bytes 6291460
  82.6 6.0 %collective-permute-start.12 = (bf16[656,128]{1,0:T(8,128)(2,1)S(1)}, bf16[656,128]{1,0:T(8,128)(2,1)S(1)}, u32[]{:S(2)}, u32[]{:S(2)}) collective-permute-start(bf16[656,128]{1,0:T(8,128)(2,1)S(1)} %get-tuple-element.91), channel_id=1, source_target_pairs={{0,4},{1,9},{2,6},{3,11},{4,0},{5,13},{6,2},{7,15},{8,12},{9,1},{1... | collective-permute-start | bytes 503816 | tf_op jit(solution)/shard_map/ppermute | solution.py:35
  88.7 5.6 %collective-permute-start.13 = (bf16[336,128]{1,0:T(8,128)(2,1)S(1)}, bf16[336,128]{1,0:T(8,128)(2,1)S(1)}, u32[]{:S(2)}, u32[]{:S(2)}) collective-permute-start(bf16[336,128]{1,0:T(8,128)(2,1)S(1)} %get-tuple-element.94), channel_id=1, source_target_pairs={{0,8},{1,5},{2,10},{3,7},{4,12},{5,1},{6,14},{7,3},{8,0},{9,13},{1... | collective-permute-start | bytes 258056 | tf_op jit(solution)/shard_map/ppermute | solution.py:35

commit v6 on v5

--- a/solution.py
+++ b/solution.py
@@ -59,7 +59,7 @@
 PIECE = 64
 F32 = jnp.float32
 BF16 = jnp.bfloat16
-VMEM_BYTES = 14 * 1024 * 1024
+VMEM_BYTES = 15 * 1024 * 1024
 
 
 def group_sum(totals):
@@ -96,9 +96,11 @@
 
 def store_three(three, row, value):
     width = value.shape[0]
-    column = lax.broadcasted_iota(jnp.int32, value.shape, 0)
-    left = jnp.where(column == 0, 0.0, pltpu.roll(value, 1, 0))
-    right = jnp.where(column == width - 1, 0.0, pltpu.roll(value, width - 1, 0))
+    column = lax.broadcasted_iota(jnp.int32, (8, value.shape[1]), 0)
+    left = pltpu.roll(value, 1, 0)
+    left = jnp.concatenate([jnp.where(column == 0, 0.0, left[:8]), left[8:]], axis=0)
+    right = pltpu.roll(value, width - 1, 0)
+    right = jnp.concatenate([right[: width - 8], jnp.where(column == 7, 0.0, right[width - 8 :])], axis=0)
     three[0, row + 1] = left.astype(three.dtype)
     three[1, row + 1] = value.astype(three.dtype)
     three[2, row + 1] = right.astype(three.dtype)
@@ -151,8 +153,8 @@
     for step in range(steps):
         others = conv_rows(accs, step - 1, (step - 1) % 2, use) if step else ()
         conv_step(accs, three, kernel, step, step % 2, back, others)
-    for other in conv_rows(accs, steps - 1, (steps - 1) % 2, use):
-        other()
+    assert steps % 2 == 0
+    return conv_rows(accs, steps - 1, 1, use)
 
 
 class Sums:
@@ -200,48 +202,59 @@
                 others.pop(0)()
 
 
-def kernel_grad(accs, turned, three, flat, beside, carry):
+def kernel_grad(accs, turned, three, flat, first, more):
     height, channels = three.shape[1] - 2, three.shape[3]
     chunks = height // ROWS
-
-    def outer(i, carry):
-        kept = [carry]
-
-        def other(row):
-            kept[0] = beside(row, kept[0])
-
-        for k in range(4):
-            chunk = 4 * i + k
-            work = [(0, 0, chunk, (0, 1, 2)), (1, 2, chunk, (0, 1, 2))]
-            others = [functools.partial(other, ROWS * chunk + j) for j in range(ROWS)] if beside else ()
-            grad_step(accs, turned, three, work, k % 2, others)
+    lead, step = 4, 4
+    outer_groups, inner_groups = (0, 2, 3), (1, 0, 2)
+
+    def sides(chunk, stage, others):
+        work = [(0, 0, chunk, outer_groups), (1, 2, chunk, outer_groups)]
+        grad_step(accs, turned, three, work, stage, others)
+
+    first = list(first)
+    for chunk, share in enumerate(interleave(len(first), lead)):
+        sides(chunk, chunk % 2, [first.pop(0) for _ in range(share)])
+    beside, carry = more() or (None, 0)
+    kept = [carry]
+
+    def other(row):
+        kept[0] = beside(row, kept[0])
+
+    def loop(i, carry):
+        kept[0] = carry
+        for k in range(step):
+            at = step * i + k
+            sides(lead + at, k % 2, [functools.partial(other, ROWS * at + j) for j in range(ROWS)] if beside else ())
         return kept[0]
 
     if beside:
-        carry = lax.fori_loop(0, chunks // 4, outer, carry)
+        kept[0] = lax.fori_loop(0, (chunks - lead) // step, loop, carry)
     else:
-        for i in range(chunks // 4):
-            outer(i, carry)
+        for i in range((chunks - lead) // step):
+            loop(i, carry)
 
     def store(tap, piece, value):
         store_flat(flat, (tap * channels + piece * PIECE) * 2, value)
 
-    def side(unit, column, row, piece):
-        store(3 * row + 2 - column, piece, pltpu.matmul_pop(accs[unit][row][piece]))
+    def side(unit, row, piece):
+        store(3 * row + 2 - 2 * unit, piece, pltpu.matmul_pop(accs[unit][outer_groups[row]][piece]))
 
     for row in range(2):
-        for unit, column in ((0, 0), (1, 2)):
+        for unit in range(UNITS):
             for piece in range(ROWS):
-                side(unit, column, row, piece)
+                side(unit, row, piece)
     half = chunks // UNITS
-    for chunk in range(half):
-        work = [(unit, 1, unit * half + chunk, (3, 0, 1)) for unit in range(UNITS)]
-        others = [functools.partial(side, unit, 2 * unit, 2, piece) for unit in range(UNITS) for piece in range(ROWS)]
-        grad_step(accs, turned, three, work, chunk % 2, others if chunk == 0 else ())
-    for row, group in enumerate((3, 0, 1)):
+    rest = [functools.partial(other, row) for row in range(ROWS * (chunks - lead), height)] if beside else []
+    for chunk, share in enumerate(interleave(len(rest), half)):
+        work = [(unit, 1, unit * half + chunk, inner_groups) for unit in range(UNITS)]
+        others = [functools.partial(side, unit, 2, piece) for unit in range(UNITS) for piece in range(ROWS)]
+        more_rows = [rest.pop(0) for _ in range(share)]
+        grad_step(accs, turned, three, work, chunk % 2, (others if chunk == 0 else []) + more_rows)
+    for row, group in enumerate(inner_groups):
         for piece in range(ROWS):
             store(3 * row + 1, piece, pltpu.matmul_pop(accs[0][group][piece]) + pltpu.matmul_pop(accs[1][group][piece]))
-    return carry
+    return kept[0]
 
 
 def store_flat(flat, start, value):
@@ -326,15 +339,15 @@
     height, width, channels = x.shape
     pixels = height * width
     per_group = channels // GROUPS
-    mean, scale, shift = stats[0:1, :], stats[1:2, :] * vec[0:1, :], vec[1:2, :]
+    mean, scale, shift = stats[0:1, :], 0.5 * stats[1:2, :] * vec[0:1, :], 0.5 * vec[1:2, :]
     offset = vec[2:3, :] + time[...]
     sums = Sums(channels, 2)
     pivot = []
     clear_edges(three)
 
     def activate(row):
-        h = (x[row].astype(F32) - mean) * scale + shift
-        store_three(three, row, h * sigmoid(h))
+        half = (x[row].astype(F32) - mean) * scale + shift
+        store_three(three, row, half * (1.0 + jnp.tanh(half)))
         if row % ROWS == ROWS - 1:
             store_turned(turned, three.at[1], row + 1 - ROWS)
 
@@ -375,7 +388,7 @@
     height, width, channels = act.shape[0] - 2, act.shape[1], act.shape[2]
     count = height * width * (channels // GROUPS)
     move, inv, gain, shift = stats[0:1, :], stats[1:2, :], vec[3:4, :], vec[4:5, :]
-    scale = inv * gain
+    scale, shift = 0.5 * inv * gain, 0.5 * shift
     both = Sums(channels, 2)
     act[0:1] = jnp.zeros((1, width, channels), BF16)
     act[height + 1 : height + 2] = jnp.zeros((1, width, channels), BF16)
@@ -384,62 +397,72 @@
     def use(row, v):
         at = slice(row * width, (row + 1) * width)
         c = raw[at, :] + move
-        h = c * scale + shift
-        sig = sigmoid(h)
-        a = h * sig
+        half = c * scale + shift
+        t = jnp.tanh(half)
+        u = 1.0 + t
+        a = half * u
         act[row + 1] = a.astype(BF16)
-        d = v * (sig + a * (1.0 - sig))
+        d = v * (u + a * (1.0 - t))
         dh[at, :] = d
         both.add(d, d * c)
         if row % ROWS == ROWS - 1:
             store_turned(turned, act, row + 1 - ROWS)
 
-    conv_all(accs, g_three, kernel, True, use)
-    turn_end(turned, act)
-    s, sc = both.totals()
-    sn = sc * inv
-    sums[0:1, :] = sn
-    sums[1:2, :] = s
-    base = inv * (group_sum(s * gain) / count)
-    slope = inv * inv * (group_sum(sn * gain) / count)
-
-    def back(row, dc):
-        at = pl.ds(times(row, width), width)
-        d = dh[at, :] * scale - base - (raw[at, :] + move) * slope
-        store_three(three, row, d)
-        return dc + fold(d)
-
-    dc_sum[...] = total(kernel_grad(accs, turned, g_three, flat, back, jnp.zeros((8, channels), F32)))
-
-
-def third_kernel(three, x, stats, vec, kernel, dh, sums):
-    accumulators(third_body, three, x, stats, vec, kernel, dh, sums)
-
-
-def third_body(three, x, stats, vec, kernel, dh, sums, accs):
+    last = conv_all(accs, g_three, kernel, True, use)
+
+    def more():
+        turn_end(turned, act)
+        s, sc = [0.5 * v for v in both.totals()]
+        sn = sc * inv
+        sums[0:1, :] = sn
+        sums[1:2, :] = s
+        base = inv * (group_sum(s * gain) / count)
+        slope = inv * inv * (group_sum(sn * gain) / count)
+        base = base + move * slope
+
+        def back(row, dc):
+            at = pl.ds(times(row, width), width)
+            d = dh[at, :] * scale - raw[at, :] * slope - base
+            store_three(three, row, d)
+            return dc + fold(d)
+
+        return back, jnp.zeros((8, channels), F32)
+
+    dc_sum[...] = total(kernel_grad(accs, turned, g_three, flat, last, more))
+
+
+def third_kernel(turned, three, x, stats, vec, kernel, dh, sums, flat):
+    accumulators(third_body, turned, three, x, stats, vec, kernel, dh, sums, flat)
+
+
+def third_body(turned, three, x, stats, vec, kernel, dh, sums, flat, accs):
     height, width, channels = x.shape
-    mean, scale, shift = stats[0:1, :], stats[1:2, :] * vec[0:1, :], vec[1:2, :]
+    mean, scale, shift = stats[0:1, :], 0.5 * stats[1:2, :] * vec[0:1, :], 0.5 * vec[1:2, :]
     both = Sums(channels, 2)
 
     def use(row, v):
         c = x[row].astype(F32) - mean
-        h = c * scale + shift
-        sig = sigmoid(h)
-        d = v * (sig + h * sig * (1.0 - sig))
+        half = c * scale + shift
+        t = jnp.tanh(half)
+        d = v * ((1.0 + t) * (1.0 + half * (1.0 - t)))
         dh[row * width : (row + 1) * width, :] = d
         both.add(d, d * c)
 
-    conv_all(accs, three, kernel, True, use)
-    s, sn = both.totals()
-    sums[0:1, :] = sn * stats[1:2, :]
-    sums[1:2, :] = s
+    last = conv_all(accs, three, kernel, True, use)
+
+    def more():
+        s, sn = [0.5 * v for v in both.totals()]
+        sums[0:1, :] = sn * stats[1:2, :]
+        sums[1:2, :] = s
+
+    kernel_grad(accs, turned, three, flat, last, more)
 
 
 def input_kernel(dh, x, g, stats, sums, vec, dc_sum, kernel, embedding, result, emb_grad, done):
     height, width, channels = x.shape
     count = height * width * (channels // GROUPS)
     mean, inv, gain = stats[0:1, :], stats[1:2, :], vec[0:1, :]
-    scale = inv * gain
+    scale = 0.5 * inv * gain
     base = inv * (group_sum(sums[1:2, :] * gain) / count)
     slope = inv * inv * (group_sum(sums[0:1, :] * gain) / count)
 
@@ -598,10 +621,6 @@
 def arrange_second_kernel(wires, cuts, mine, got, second, flat_two):
     place_blocks(wires, cuts, mine, got, (flat_two,))
     unflatten(flat_two, second, 0)
-
-
-def grad_kernel(turned, three, flat):
-    accumulators(lambda *refs: kernel_grad(refs[-1], *refs[:-1], None, 0), turned, three, flat)
 
 
 def take_blocks(wires, cuts, flats, send, keep):
@@ -842,8 +861,9 @@
     last = wires.stages
     two_send, two = pack_second(wires, cuts[1:], grad_two, embedding, dc_sum)
     two_got = wires.swap(two_send, last)
-    dh_one, sums_one = call(third_kernel, [flat, pair], e_three, x_near, stats, vec, first, flops=conv_flops)
-    grad_one, = call(grad_kernel, [taps], turned_one, e_three, flops=conv_flops)
+    dh_one, sums_one, grad_one = call(
+        third_kernel, [flat, pair, taps], turned_one, e_three, x_near, stats, vec, first
+    )
     one_send, one, two_send, two = pack_first(
         wires, cuts[:1], grad_one, dc_sum, sums_one, sums_two, g_sum, two, two_got
     )

time: 95.3 us -> 94.4 us (level)
  Pallas kernels: 49.6 us -> 48.4 us
    pallas_call x23 -> x22, Pallas kernels: 49.6 us -> 48.4 us  [call(): pl.pallas_call(run, out_shape=[pltpu.HBM(shape, dtype) if i in far_outs e...]
  transfers between devices with their start and end apart: 14 -> 14, of which waited for: 9 -> 9; matrix products, arithmetic and copies ran while one was open for 0% -> 0% of each run, Pallas kernels for 38% -> 37%
where the time goes in v6:
time: 94.4 us; the launch traced here: 94.2 us
  Pallas kernels  48.4 us (51%)
  waiting for transfers between devices  22.1 us (23%)
  starting transfers between devices  21.2 us (22%)
    pallas_call x22, Pallas kernels, call(): pl.pallas_call(run, out_shape=[pltpu.HBM(shape, dtype) if i in far_outs e...  48.4 us
    ppermute x14, waiting for transfers between devices, swap(): lax.ppermute(value, AXES, [(i, i ^ 1 << bit(i & 1)) for i in range(self.n)])  22.1 us
    ppermute x14, starting transfers between devices, swap(): lax.ppermute(value, AXES, [(i, i ^ 1 << bit(i & 1)) for i in range(self.n)])  21.2 us
  transfers between devices with their start and end apart: 14, of which 9 were waited for; matrix products, arithmetic and copies ran while one was open for 0% of the time, Pallas kernels for 37%

profile of v6, /device:TPU:0, one launch (start us, length us, event | category | flops | bytes accessed | tf_op | source)
XLA Modules:
  0.0 94.2 jit_solution(5066428781552615968)
XLA Ops:
  2.2 4.0 %collective-permute-start = (bf16[336,128]{1,0:T(8,128)(2,1)S(1)}, bf16[336,128]{1,0:T(8,128)(2,1)S(1)}, u32[]{:S(2)}, u32[]{:S(2)}) collective-permute-start(bf16[336,128]{1,0:T(8,128)(2,1)S(1)} %pad_maximum_fusion.refs_0_), channel_id=1, source_target_pairs={{0,8},{1,5},{2,10},{3,7},{4,12},{5,1},{6,14},{7,3},{8,0},{9,13},{1... | collective-permute-start | bytes 258056 | tf_op jit(solution)/shard_map/ppermute | solution.py:35
  6.2 2.5 %collective-permute-done.refs_1_ = bf16[336,128]{1,0:T(8,128)(2,1)S(1)} collective-permute-done((bf16[336,128]{1,0:T(8,128)(2,1)S(1)}, bf16[336,128]{1,0:T(8,128)(2,1)S(1)}, u32[]{:S(2)}, u32[]{:S(2)}) %collective-permute-start) | collective-permute-done | bytes 86048 | tf_op jit(solution)/shard_map/ppermute | solution.py:35
  8.7 2.0 %collective-permute-start.1 = (bf16[656,128]{1,0:T(8,128)(2,1)S(1)}, bf16[656,128]{1,0:T(8,128)(2,1)S(1)}, u32[]{:S(2)}, u32[]{:S(2)}) collective-permute-start(bf16[656,128]{1,0:T(8,128)(2,1)S(1)} %shard_map.128.refs_0_), channel_id=1, source_target_pairs={{0,4},{1,9},{2,6},{3,11},{4,0},{5,13},{6,2},{7,15},{8,12},{9,1},{1... | collective-permute-start | bytes 503816 | tf_op jit(solution)/shard_map/ppermute | solution.py:35
  10.7 4.1 %collective-permute-done.1.refs_1_ = bf16[656,128]{1,0:T(8,128)(2,1)S(1)} collective-permute-done((bf16[656,128]{1,0:T(8,128)(2,1)S(1)}, bf16[656,128]{1,0:T(8,128)(2,1)S(1)}, u32[]{:S(2)}, u32[]{:S(2)}) %collective-permute-start.1) | collective-permute-done | bytes 167968 | tf_op jit(solution)/shard_map/ppermute | solution.py:35
  14.8 1.9 %collective-permute-start.2 = (bf16[1296,128]{1,0:T(8,128)(2,1)S(1)}, bf16[1296,128]{1,0:T(8,128)(2,1)S(1)}, u32[]{:S(2)}, u32[]{:S(2)}) collective-permute-start(bf16[1296,128]{1,0:T(8,128)(2,1)S(1)} %shard_map.129.refs_0_), channel_id=1, source_target_pairs={{0,2},{1,17},{2,0},{3,19},{4,6},{5,21},{6,4},{7,23},{8,10},{9,25},... | collective-permute-start | bytes 995336 | tf_op jit(solution)/shard_map/ppermute | solution.py:35
  16.7 4.0 %shard_map.126 = (bf16[3,66,64,256]{3,2,1,0:T(8,128)(2,1)}, f32[1,256]{1,0:T(1,128)S(1)}) custom-call(bf16[64,64,256]{2,1,0:T(8,128)(2,1)} %bitcast.13), custom_call_target="tpu_custom_call" | custom-call | tf_op jit(solution)/shard_map/pallas_call | solution.py:691
  22.0 2.0 %collective-permute-start.3 = (bf16[1424,128]{1,0:T(8,128)(2,1)S(1)}, bf16[1424,128]{1,0:T(8,128)(2,1)S(1)}, u32[]{:S(2)}, u32[]{:S(2)}) collective-permute-start(bf16[1424,128]{1,0:T(8,128)(2,1)S(1)} %get-tuple-element.58.refs_0_), channel_id=1, source_target_pairs={{0,16},{1,3},{2,18},{3,1},{4,20},{5,7},{6,22},{7,5},{8,24},{9,11},... | collective-permute-start | bytes 1093640 | tf_op jit(solution)/shard_map/ppermute | solution.py:35
  24.1 2.8 %shard_map.127 = (f32[2,256]{1,0:T(2,128)S(1)}, bf16[64,64,256]{2,1,0:T(8,128)(2,1)S(1)}) custom-call(bf16[64,64,256]{2,1,0:T(8,128)(2,1)} %bitcast.15), custom_call_target="tpu_custom_call" | custom-call | tf_op jit(solution)/shard_map/pallas_call | solution.py:691
  26.9 2.6 %collective-permute-done.3.refs_1_ = bf16[1424,128]{1,0:T(8,128)(2,1)S(1)} collective-permute-done((bf16[1424,128]{1,0:T(8,128)(2,1)S(1)}, bf16[1424,128]{1,0:T(8,128)(2,1)S(1)}, u32[]{:S(2)}, u32[]{:S(2)}) %collective-permute-start.3) | collective-permute-done | bytes 364576 | tf_op jit(solution)/shard_map/ppermute | solution.py:35
  29.7 3.0 %collective-permute-done.5.refs_1_ = bf16[1152,128]{1,0:T(8,128)(2,1)S(1)} collective-permute-done((bf16[1152,128]{1,0:T(8,128)(2,1)S(1)}, bf16[1152,128]{1,0:T(8,128)(2,1)S(1)}, u32[]{:S(2)}, u32[]{:S(2)}) %collective-permute-start.5) | collective-permute-done | bytes 294944 | tf_op jit(solution)/shard_map/ppermute | solution.py:35
  33.4 6.2 %shard_map.134 = (bf16[2,256,4224]{2,1,0:T(8,128)(2,1)S(1)}, f32[4096,256]{1,0:T(8,128)S(1)}, f32[2,256]{1,0:T(2,128)S(1)}) custom-call(bf16[64,64,256]{2,1,0:T(8,128)(2,1)S(1)} %get-tuple-element.55.refs_0_.refs_1_.refs_2_, f32[2,256]{1,0:T(2,128)S(1)} %get-tuple-element.56.refs_2_.refs_1_.refs_3_, ...), custom_call_target="tpu_custom_call" | custom-call | tf_op jit(solution)/shard_map/pallas_call | solution.py:691
  39.9 11.8 %shard_map.136 = (bf16[66,64,256]{2,1,0:T(8,128)(2,1)S(1)}, f32[2,256]{1,0:T(2,128)S(1)}, f32[4608,128]{1,0:T(8,128)S(1)}, bf16[3,66,64,256]{3,2,1,0:T(8,128)(2,1)S(1)}, f32[1,256]{1,0:T(1,128)S(1)}) custom-call(bf16[3,66,64,256]{3,2,1,0:T(8,128)(2,1)S(1)} %copy-done.2, f32[4096,256]{1,0:T(8,128)S(1)} %get-tuple-element.64.refs_1_, ...), custom_call_target="tpu_custom_call" | custom-call | tf_op jit(solution)/shard_map/pallas_call | solution.py:691
  52.5 10.7 %shard_map.139 = (f32[4096,256]{1,0:T(8,128)S(1)}, f32[2,256]{1,0:T(2,128)S(1)}, f32[4608,128]{1,0:T(8,128)S(1)}) custom-call(bf16[2,256,4224]{2,1,0:T(8,128)(2,1)S(1)} %get-tuple-element.70.refs_0_, bf16[3,66,64,256]{3,2,1,0:T(8,128)(2,1)S(1)} %get-tuple-element.71.refs_1_, bf16[64,64,256]{2,1,0:T(8,128)(2,1)S(1)} %get-tuple-element.55.refs_0_.refs_1_.refs_2_, ...), custom_call_target="tpu_custom_call" | custom-call | tf_op jit(solution)/shard_map/pallas_call | solution.py:691
  63.6 2.0 %collective-permute-start.10 = (bf16[1408,128]{1,0:T(8,128)(2,1)S(1)}, bf16[1408,128]{1,0:T(8,128)(2,1)S(1)}, u32[]{:S(2)}, u32[]{:S(2)}) collective-permute-start(bf16[1408,128]{1,0:T(8,128)(2,1)S(1)} %get-tuple-element.87), channel_id=1, source_target_pairs={{0,16},{1,3},{2,18},{3,1},{4,20},{5,7},{6,22},{7,5},{8,24},{9,11},... | collective-permute-start | bytes 1081352 | tf_op jit(solution)/shard_map/ppermute | solution.py:35
  65.8 2.0 %collective-permute-start.9 = (bf16[1168,128]{1,0:T(8,128)(2,1)S(1)}, bf16[1168,128]{1,0:T(8,128)(2,1)S(1)}, u32[]{:S(2)}, u32[]{:S(2)}) collective-permute-start(bf16[1168,128]{1,0:T(8,128)(2,1)S(1)} %get-tuple-element.85), channel_id=1, source_target_pairs={{0,16},{1,3},{2,18},{3,1},{4,20},{5,7},{6,22},{7,5},{8,24},{9,11},... | collective-permute-start | bytes 897032 | tf_op jit(solution)/shard_map/ppermute | solution.py:35
  67.7 3.4 %shard_map.137 = (bf16[64,64,256]{2,1,0:T(8,128)(2,1)}, f32[1,256]{1,0:T(1,128)S(1)}) custom-call(bf16[66,64,256]{2,1,0:T(8,128)(2,1)S(1)} %get-tuple-element.67.refs_0_, bf16[64,64,256]{2,1,0:T(8,128)(2,1)S(1)} %get-tuple-element.55.refs_0_.refs_1_.refs_2_, f32[8,256]{1,0:T(8,128)S(1)} %get-tuple-element.61.refs_2_.refs_3_.refs_4_.refs_5_, ...), custom_call_target="tpu_custom_call" | custom-call | tf_op jit(solution)/shard_map/pallas_call | solution.py:691
  71.2 3.1 %collective-permute-done.9.refs_1_ = bf16[1168,128]{1,0:T(8,128)(2,1)S(1)} collective-permute-done((bf16[1168,128]{1,0:T(8,128)(2,1)S(1)}, bf16[1168,128]{1,0:T(8,128)(2,1)S(1)}, u32[]{:S(2)}, u32[]{:S(2)}) %collective-permute-start.9) | collective-permute-done | bytes 299040 | tf_op jit(solution)/shard_map/ppermute | solution.py:35
  74.5 1.9 %collective-permute-start.11 = (bf16[1296,128]{1,0:T(8,128)(2,1)S(1)}, bf16[1296,128]{1,0:T(8,128)(2,1)S(1)}, u32[]{:S(2)}, u32[]{:S(2)}) collective-permute-start(bf16[1296,128]{1,0:T(8,128)(2,1)S(1)} %get-tuple-element.90), channel_id=1, source_target_pairs={{0,2},{1,17},{2,0},{3,19},{4,6},{5,21},{6,4},{7,23},{8,10},{9,25},... | collective-permute-start | bytes 995336 | tf_op jit(solution)/shard_map/ppermute | solution.py:35
  76.4 3.4 %shard_map.138 = (bf16[64,64,256]{2,1,0:T(8,128)(2,1)}, f32[1,256]{1,0:T(1,128)S(1)}) custom-call(bf16[66,64,256]{2,1,0:T(8,128)(2,1)S(1)} %get-tuple-element.67.refs_0_, bf16[64,64,256]{2,1,0:T(8,128)(2,1)S(1)} %get-tuple-element.55.refs_0_.refs_1_.refs_2_, ...), custom_call_target="tpu_custom_call", output_to_operand_aliasing={{0}: (4, {})} | custom-call | tf_op jit(solution)/shard_map/pallas_call | solution.py:691
  79.9 1.8 %collective-permute-done.11.refs_1_ = bf16[1296,128]{1,0:T(8,128)(2,1)S(1)} collective-permute-done((bf16[1296,128]{1,0:T(8,128)(2,1)S(1)}, bf16[1296,128]{1,0:T(8,128)(2,1)S(1)}, u32[]{:S(2)}, u32[]{:S(2)}) %collective-permute-start.11) | collective-permute-done | bytes 331808 | tf_op jit(solution)/shard_map/ppermute | solution.py:35
  81.7 1.3 %collective-permute-start.12 = (bf16[656,128]{1,0:T(8,128)(2,1)S(1)}, bf16[656,128]{1,0:T(8,128)(2,1)S(1)}, u32[]{:S(2)}, u32[]{:S(2)}) collective-permute-start(bf16[656,128]{1,0:T(8,128)(2,1)S(1)} %get-tuple-element.93), channel_id=1, source_target_pairs={{0,4},{1,9},{2,6},{3,11},{4,0},{5,13},{6,2},{7,15},{8,12},{9,1},{1... | collective-permute-start | bytes 503816 | tf_op jit(solution)/shard_map/ppermute | solution.py:35
  83.1 3.5 %shard_map.140 = (f32[64,64,256]{2,1,0:T(8,128)}, f32[1,512]{1,0:T(1,128)}, f32[1,256]{1,0:T(1,128)S(1)}) custom-call(f32[4096,256]{1,0:T(8,128)S(1)} %get-tuple-element.72.refs_0_, bf16[64,64,256]{2,1,0:T(8,128)(2,1)S(1)} %bitcast.16, bf16[64,64,256]{2,1,0:T(8,128)(2,1)S(1)} %bitcast.14, f32[2,256]{1,0:T(2,128)S(1)} %get-tuple-element.56.refs_2_.refs_1_.refs_3_, ...), custom_call_target="tpu_custom_call" | custom-call | tf_op jit(solution)/shard_map/pallas_call | solution.py:691
  87.8 3.2 %collective-permute-start.13 = (bf16[336,128]{1,0:T(8,128)(2,1)S(1)}, bf16[336,128]{1,0:T(8,128)(2,1)S(1)}, u32[]{:S(2)}, u32[]{:S(2)}) collective-permute-start(bf16[336,128]{1,0:T(8,128)(2,1)S(1)} %get-tuple-element.96), channel_id=1, source_target_pairs={{0,8},{1,5},{2,10},{3,7},{4,12},{5,1},{6,14},{7,3},{8,0},{9,13},{1... | collective-permute-start | bytes 258056 | tf_op jit(solution)/shard_map/ppermute | solution.py:35
  91.0 2.5 %collective-permute-done.13.refs_1_ = bf16[336,128]{1,0:T(8,128)(2,1)S(1)} collective-permute-done((bf16[336,128]{1,0:T(8,128)(2,1)S(1)}, bf16[336,128]{1,0:T(8,128)(2,1)S(1)}, u32[]{:S(2)}, u32[]{:S(2)}) %collective-permute-start.13) | collective-permute-done | bytes 86048 | tf_op jit(solution)/shard_map/ppermute | solution.py:35
  (36 shorter events, 7.5 us)
Async XLA Ops:
  2.2 6.5 %collective-permute-start = (bf16[336,128]{1,0:T(8,128)(2,1)S(1)}, bf16[336,128]{1,0:T(8,128)(2,1)S(1)}, u32[]{:S(2)}, u32[]{:S(2)}) collective-permute-start(bf16[336,128]{1,0:T(8,128)(2,1)S(1)} %pad_maximum_fusion.refs_0_), channel_id=1, source_target_pairs={{0,8},{1,5},{2,10},{3,7},{4,12},{5,1},{6,14},{7,3},{8,0},{9,13},{1... | collective-permute-start | bytes 258056 | tf_op jit(solution)/shard_map/ppermute | solution.py:35
  8.7 6.1 %collective-permute-start.1 = (bf16[656,128]{1,0:T(8,128)(2,1)S(1)}, bf16[656,128]{1,0:T(8,128)(2,1)S(1)}, u32[]{:S(2)}, u32[]{:S(2)}) collective-permute-start(bf16[656,128]{1,0:T(8,128)(2,1)S(1)} %shard_map.128.refs_0_), channel_id=1, source_target_pairs={{0,4},{1,9},{2,6},{3,11},{4,0},{5,13},{6,2},{7,15},{8,12},{9,1},{1... | collective-permute-start | bytes 503816 | tf_op jit(solution)/shard_map/ppermute | solution.py:35
  14.8 7.2 %collective-permute-start.2 = (bf16[1296,128]{1,0:T(8,128)(2,1)S(1)}, bf16[1296,128]{1,0:T(8,128)(2,1)S(1)}, u32[]{:S(2)}, u32[]{:S(2)}) collective-permute-start(bf16[1296,128]{1,0:T(8,128)(2,1)S(1)} %shard_map.129.refs_0_), channel_id=1, source_target_pairs={{0,2},{1,17},{2,0},{3,19},{4,6},{5,21},{6,4},{7,23},{8,10},{9,25},... | collective-permute-start | bytes 995336 | tf_op jit(solution)/shard_map/ppermute | solution.py:35
  22.0 10.8 %copy-start.3 = (bf16[1,512]{1,0:T(2,128)(2,1)S(1)}, bf16[1,512]{1,0:T(2,128)(2,1)}, u32[]{:S(2)}) copy-start(bf16[1,512]{1,0:T(2,128)(2,1)} %refs_1_.1) | copy-start | bytes 3076
  22.0 7.5 %collective-permute-start.3 = (bf16[1424,128]{1,0:T(8,128)(2,1)S(1)}, bf16[1424,128]{1,0:T(8,128)(2,1)S(1)}, u32[]{:S(2)}, u32[]{:S(2)}) collective-permute-start(bf16[1424,128]{1,0:T(8,128)(2,1)S(1)} %get-tuple-element.58.refs_0_), channel_id=1, source_target_pairs={{0,16},{1,3},{2,18},{3,1},{4,20},{5,7},{6,22},{7,5},{8,24},{9,11},... | collective-permute-start | bytes 1093640 | tf_op jit(solution)/shard_map/ppermute | solution.py:35
  24.0 8.7 %collective-permute-start.5 = (bf16[1152,128]{1,0:T(8,128)(2,1)S(1)}, bf16[1152,128]{1,0:T(8,128)(2,1)S(1)}, u32[]{:S(2)}, u32[]{:S(2)}) collective-permute-start(bf16[1152,128]{1,0:T(8,128)(2,1)S(1)} %get-tuple-element.59.refs_0_), channel_id=1, source_target_pairs={{0,16},{1,3},{2,18},{3,1},{4,20},{5,7},{6,22},{7,5},{8,24},{9,11},... | collective-permute-start | bytes 884744 | tf_op jit(solution)/shard_map/ppermute | solution.py:35
  29.6 3.2 %collective-permute-start.4 = (bf16[2832,128]{1,0:T(8,128)(2,1)S(1)}, bf16[2832,128]{1,0:T(8,128)(2,1)S(1)}, u32[]{:S(2)}, u32[]{:S(2)}) collective-permute-start(bf16[2832,128]{1,0:T(8,128)(2,1)S(1)} %shard_map.131.refs_0_), channel_id=1, source_target_pairs={{0,1},{1,0},{2,3},{3,2},{4,5},{5,4},{6,7},{7,6},{8,9},{9,8},{10,11... | collective-permute-start | bytes 2174984 | tf_op jit(solution)/shard_map/ppermute | solution.py:35
  32.8 6.8 %collective-permute-start.6 = (bf16[2304,128]{1,0:T(8,128)(2,1)S(1)}, bf16[2304,128]{1,0:T(8,128)(2,1)S(1)}, u32[]{:S(2)}, u32[]{:S(2)}) collective-permute-start(bf16[2304,128]{1,0:T(8,128)(2,1)S(1)} %get-tuple-element.66.refs_0_), channel_id=1, source_target_pairs={{0,1},{1,0},{2,3},{3,2},{4,5},{5,4},{6,7},{7,6},{8,9},{9,8},{10,11... | collective-permute-start | bytes 1769480 | tf_op jit(solution)/shard_map/ppermute | solution.py:35
  32.9 7.0 %copy-start.2 = (bf16[3,66,64,256]{3,2,1,0:T(8,128)(2,1)S(1)}, bf16[3,66,64,256]{3,2,1,0:T(8,128)(2,1)}, u32[]{:S(2)}) copy-start(bf16[3,66,64,256]{3,2,1,0:T(8,128)(2,1)} %get-tuple-element.54.refs_0_) | copy-start | bytes 19464196
  52.0 11.3 %collective-permute-start.7 = (bf16[2816,128]{1,0:T(8,128)(2,1)S(1)}, bf16[2816,128]{1,0:T(8,128)(2,1)S(1)}, u32[]{:S(2)}, u32[]{:S(2)}) collective-permute-start(bf16[2816,128]{1,0:T(8,128)(2,1)S(1)} %get-tuple-element.81), channel_id=1, source_target_pairs={{0,1},{1,0},{2,3},{3,2},{4,5},{5,4},{6,7},{7,6},{8,9},{9,8},{10,11... | collective-permute-start | bytes 2162696 | tf_op jit(solution)/shard_map/ppermute | solution.py:35
  63.6 2.1 %collective-permute-start.8 = (bf16[2320,128]{1,0:T(8,128)(2,1)S(1)}, bf16[2320,128]{1,0:T(8,128)(2,1)S(1)}, u32[]{:S(2)}, u32[]{:S(2)}) collective-permute-start(bf16[2320,128]{1,0:T(8,128)(2,1)S(1)} %get-tuple-element.83), channel_id=1, source_target_pairs={{0,1},{1,0},{2,3},{3,2},{4,5},{5,4},{6,7},{7,6},{8,9},{9,8},{10,11... | collective-permute-start | bytes 1781768 | tf_op jit(solution)/shard_map/ppermute | solution.py:35
  63.6 7.5 %collective-permute-start.10 = (bf16[1408,128]{1,0:T(8,128)(2,1)S(1)}, bf16[1408,128]{1,0:T(8,128)(2,1)S(1)}, u32[]{:S(2)}, u32[]{:S(2)}) collective-permute-start(bf16[1408,128]{1,0:T(8,128)(2,1)S(1)} %get-tuple-element.87), channel_id=1, source_target_pairs={{0,16},{1,3},{2,18},{3,1},{4,20},{5,7},{6,22},{7,5},{8,24},{9,11},... | collective-permute-start | bytes 1081352 | tf_op jit(solution)/shard_map/ppermute | solution.py:35
  65.8 8.6 %collective-permute-start.9 = (bf16[1168,128]{1,0:T(8,128)(2,1)S(1)}, bf16[1168,128]{1,0:T(8,128)(2,1)S(1)}, u32[]{:S(2)}, u32[]{:S(2)}) collective-permute-start(bf16[1168,128]{1,0:T(8,128)(2,1)S(1)} %get-tuple-element.85), channel_id=1, source_target_pairs={{0,16},{1,3},{2,18},{3,1},{4,20},{5,7},{6,22},{7,5},{8,24},{9,11},... | collective-permute-start | bytes 897032 | tf_op jit(solution)/shard_map/ppermute | solution.py:35
  74.5 7.2 %collective-permute-start.11 = (bf16[1296,128]{1,0:T(8,128)(2,1)S(1)}, bf16[1296,128]{1,0:T(8,128)(2,1)S(1)}, u32[]{:S(2)}, u32[]{:S(2)}) collective-permute-start(bf16[1296,128]{1,0:T(8,128)(2,1)S(1)} %get-tuple-element.90), channel_id=1, source_target_pairs={{0,2},{1,17},{2,0},{3,19},{4,6},{5,21},{6,4},{7,23},{8,10},{9,25},... | collective-permute-start | bytes 995336 | tf_op jit(solution)/shard_map/ppermute | solution.py:35
  76.4 6.7 %copy-start = (bf16[1,64,64,256]{3,2,1,0:T(8,128)(2,1)S(1)}, bf16[1,64,64,256]{3,2,1,0:T(8,128)(2,1)}, u32[]{:S(2)}) copy-start(bf16[1,64,64,256]{3,2,1,0:T(8,128)(2,1)} %param.13) | copy-start | bytes 6291460
  76.4 6.7 %copy-start.1 = (bf16[1,64,64,256]{3,2,1,0:T(8,128)(2,1)S(1)}, bf16[1,64,64,256]{3,2,1,0:T(8,128)(2,1)}, u32[]{:S(2)}) copy-start(bf16[1,64,64,256]{3,2,1,0:T(8,128)(2,1)} %param.7) | copy-start | bytes 6291460
  81.7 6.0 %collective-permute-start.12 = (bf16[656,128]{1,0:T(8,128)(2,1)S(1)}, bf16[656,128]{1,0:T(8,128)(2,1)S(1)}, u32[]{:S(2)}, u32[]{:S(2)}) collective-permute-start(bf16[656,128]{1,0:T(8,128)(2,1)S(1)} %get-tuple-element.93), channel_id=1, source_target_pairs={{0,4},{1,9},{2,6},{3,11},{4,0},{5,13},{6,2},{7,15},{8,12},{9,1},{1... | collective-permute-start | bytes 503816 | tf_op jit(solution)/shard_map/ppermute | solution.py:35
  87.8 5.7 %collective-permute-start.13 = (bf16[336,128]{1,0:T(8,128)(2,1)S(1)}, bf16[336,128]{1,0:T(8,128)(2,1)S(1)}, u32[]{:S(2)}, u32[]{:S(2)}) collective-permute-start(bf16[336,128]{1,0:T(8,128)(2,1)S(1)} %get-tuple-element.96), channel_id=1, source_target_pairs={{0,8},{1,5},{2,10},{3,7},{4,12},{5,1},{6,14},{7,3},{8,0},{9,13},{1... | collective-permute-start | bytes 258056 | tf_op jit(solution)/shard_map/ppermute | solution.py:35

commit v7 on v6

--- a/solution.py
+++ b/solution.py
@@ -534,6 +534,28 @@
         copy.wait()
 
 
+def start_kernel(wires, n_vec, *refs):
+    *parts, vectors, out, own, arrived = refs
+    copies, at = [], 0
+    for i, part in enumerate(parts):
+        copies.append(pltpu.make_async_copy(part, out.at[pl.ds(at, part.shape[0])], arrived.at[i]))
+        at += part.shape[0]
+    copies.append(pltpu.make_async_copy(vectors, own, arrived.at[len(parts)]))
+    for copy in copies:
+        copy.start()
+    copies[-1].wait()
+    first = wires.me() * n_vec
+    row, lane = first // LANES, first % LANES
+    values = jnp.concatenate([own[...].astype(F32), jnp.zeros((1, LANES - n_vec), F32)], axis=1)
+    values = jnp.broadcast_to(pltpu.roll(values, lane, 1), (VEC_ROWS, LANES))
+    place = lax.broadcasted_iota(jnp.int32, values.shape, 0)
+    column = lax.broadcasted_iota(jnp.int32, values.shape, 1)
+    here = ((place == row) & (column >= lane)) | ((place == row + 1) & (column < lane))
+    out[at : at + VEC_ROWS, :] = jnp.where(here, values, 0.0).astype(BF16)
+    for copy in copies[:-1]:
+        copy.wait()
+
+
 def join_kernel(mine, got, out, tail=VEC_ROWS):
     rows = mine.shape[0] - tail
     out[0:rows, :] = mine[0:rows, :]
@@ -836,9 +858,21 @@
     g_three, g_sum = call(
         spread_kernel, [three, line], g, scratch=[maps, three], far=(0,), far_outs=(0,), semaphores=(4, 4)
     )
-    wide = VEC_ROWS * LANES
-    placed = lax.dynamic_slice(jnp.pad(vectors, (wide, wide - n_vec)), (wide - wires.me() * n_vec,), (wide,))
-    start = jnp.concatenate([v.reshape(-1, LANES) for v in (conv_first, projection, conv_second, placed)])
+    order = (conv_first, projection, conv_second)
+    if all(rows % 16 == 0 for rows in cuts):
+        start, = call(
+            functools.partial(start_kernel, wires, n_vec),
+            [((sum(cuts) + VEC_ROWS, LANES), BF16)],
+            *[v.reshape(-1, LANES) for v in order],
+            vectors.reshape(1, n_vec),
+            scratch=[((1, n_vec), BF16)],
+            far=(0, 1, 2, 3),
+            semaphores=(4,),
+        )
+    else:
+        wide = VEC_ROWS * LANES
+        placed = lax.dynamic_slice(jnp.pad(vectors, (wide, wide - n_vec)), (wide - wires.me() * n_vec,), (wide,))
+        start = jnp.concatenate([v.reshape(-1, LANES) for v in (*order, placed)])
     beside = {wires.stages - 2: (g_sum,), wires.stages - 1: (stats,)}
     one, one_got, two, two_got, mark = gather_start(wires, (cuts[0], cuts[2], cuts[1]), start, beside)
     first, vec, time = arrange_first(wires, (cuts[0], cuts[2]), one, one_got, embedding, (mark,))

time: 94.4 us -> 93.7 us (level)
    pallas_call x22 -> x23, Pallas kernels: 48.4 us -> 49.3 us  [call(): pl.pallas_call(run, out_shape=[pltpu.HBM(shape, dtype) if i in far_outs e...]
where the time goes in v7:
time: 93.7 us; the launch traced here: 93.5 us
  Pallas kernels  49.3 us (53%)
  waiting for transfers between devices  22.1 us (24%)
  starting transfers between devices  21.2 us (23%)
    pallas_call x23, Pallas kernels, call(): pl.pallas_call(run, out_shape=[pltpu.HBM(shape, dtype) if i in far_outs e...  49.3 us
    ppermute x14, waiting for transfers between devices, swap(): lax.ppermute(value, AXES, [(i, i ^ 1 << bit(i & 1)) for i in range(self.n)])  22.1 us
    ppermute x14, starting transfers between devices, swap(): lax.ppermute(value, AXES, [(i, i ^ 1 << bit(i & 1)) for i in range(self.n)])  21.2 us
  transfers between devices with their start and end apart: 14, of which 9 were waited for; matrix products, arithmetic and copies ran while one was open for 0% of the time, Pallas kernels for 37%

profile of v7, /device:TPU:0, one launch (start us, length us, event | category | flops | bytes accessed | tf_op | source)
XLA Modules:
  0.0 93.5 jit_solution(16373283370085486067)
XLA Ops:
  1.5 4.1 %collective-permute-start = (bf16[336,128]{1,0:T(8,128)(2,1)S(1)}, bf16[336,128]{1,0:T(8,128)(2,1)S(1)}, u32[]{:S(2)}, u32[]{:S(2)}) collective-permute-start(bf16[336,128]{1,0:T(8,128)(2,1)S(1)} %shard_map.128.refs_0_), channel_id=1, source_target_pairs={{0,8},{1,5},{2,10},{3,7},{4,12},{5,1},{6,14},{7,3},{8,0},{9,13},{1... | collective-permute-start | bytes 258056 | tf_op jit(solution)/shard_map/ppermute | solution.py:35
  5.6 2.5 %collective-permute-done.refs_1_ = bf16[336,128]{1,0:T(8,128)(2,1)S(1)} collective-permute-done((bf16[336,128]{1,0:T(8,128)(2,1)S(1)}, bf16[336,128]{1,0:T(8,128)(2,1)S(1)}, u32[]{:S(2)}, u32[]{:S(2)}) %collective-permute-start) | collective-permute-done | bytes 86048 | tf_op jit(solution)/shard_map/ppermute | solution.py:35
  8.1 2.0 %collective-permute-start.1 = (bf16[656,128]{1,0:T(8,128)(2,1)S(1)}, bf16[656,128]{1,0:T(8,128)(2,1)S(1)}, u32[]{:S(2)}, u32[]{:S(2)}) collective-permute-start(bf16[656,128]{1,0:T(8,128)(2,1)S(1)} %shard_map.129.refs_0_), channel_id=1, source_target_pairs={{0,4},{1,9},{2,6},{3,11},{4,0},{5,13},{6,2},{7,15},{8,12},{9,1},{1... | collective-permute-start | bytes 503816 | tf_op jit(solution)/shard_map/ppermute | solution.py:35
  10.1 4.1 %collective-permute-done.1.refs_1_ = bf16[656,128]{1,0:T(8,128)(2,1)S(1)} collective-permute-done((bf16[656,128]{1,0:T(8,128)(2,1)S(1)}, bf16[656,128]{1,0:T(8,128)(2,1)S(1)}, u32[]{:S(2)}, u32[]{:S(2)}) %collective-permute-start.1) | collective-permute-done | bytes 167968 | tf_op jit(solution)/shard_map/ppermute | solution.py:35
  14.2 1.9 %collective-permute-start.2 = (bf16[1296,128]{1,0:T(8,128)(2,1)S(1)}, bf16[1296,128]{1,0:T(8,128)(2,1)S(1)}, u32[]{:S(2)}, u32[]{:S(2)}) collective-permute-start(bf16[1296,128]{1,0:T(8,128)(2,1)S(1)} %shard_map.130.refs_0_), channel_id=1, source_target_pairs={{0,2},{1,17},{2,0},{3,19},{4,6},{5,21},{6,4},{7,23},{8,10},{9,25},... | collective-permute-start | bytes 995336 | tf_op jit(solution)/shard_map/ppermute | solution.py:35
  16.1 4.0 %shard_map.126 = (bf16[3,66,64,256]{3,2,1,0:T(8,128)(2,1)}, f32[1,256]{1,0:T(1,128)S(1)}) custom-call(bf16[64,64,256]{2,1,0:T(8,128)(2,1)} %bitcast.12), custom_call_target="tpu_custom_call" | custom-call | tf_op jit(solution)/shard_map/pallas_call | solution.py:713
  21.4 2.0 %collective-permute-start.3 = (bf16[1424,128]{1,0:T(8,128)(2,1)S(1)}, bf16[1424,128]{1,0:T(8,128)(2,1)S(1)}, u32[]{:S(2)}, u32[]{:S(2)}) collective-permute-start(bf16[1424,128]{1,0:T(8,128)(2,1)S(1)} %get-tuple-element.58.refs_0_), channel_id=1, source_target_pairs={{0,16},{1,3},{2,18},{3,1},{4,20},{5,7},{6,22},{7,5},{8,24},{9,11},... | collective-permute-start | bytes 1093640 | tf_op jit(solution)/shard_map/ppermute | solution.py:35
  23.5 2.8 %shard_map.127 = (f32[2,256]{1,0:T(2,128)S(1)}, bf16[64,64,256]{2,1,0:T(8,128)(2,1)S(1)}) custom-call(bf16[64,64,256]{2,1,0:T(8,128)(2,1)} %bitcast.14), custom_call_target="tpu_custom_call" | custom-call | tf_op jit(solution)/shard_map/pallas_call | solution.py:713
  26.3 2.6 %collective-permute-done.3.refs_1_ = bf16[1424,128]{1,0:T(8,128)(2,1)S(1)} collective-permute-done((bf16[1424,128]{1,0:T(8,128)(2,1)S(1)}, bf16[1424,128]{1,0:T(8,128)(2,1)S(1)}, u32[]{:S(2)}, u32[]{:S(2)}) %collective-permute-start.3) | collective-permute-done | bytes 364576 | tf_op jit(solution)/shard_map/ppermute | solution.py:35
  29.1 3.0 %collective-permute-done.5.refs_1_ = bf16[1152,128]{1,0:T(8,128)(2,1)S(1)} collective-permute-done((bf16[1152,128]{1,0:T(8,128)(2,1)S(1)}, bf16[1152,128]{1,0:T(8,128)(2,1)S(1)}, u32[]{:S(2)}, u32[]{:S(2)}) %collective-permute-start.5) | collective-permute-done | bytes 294944 | tf_op jit(solution)/shard_map/ppermute | solution.py:35
  32.7 6.2 %shard_map.135 = (bf16[2,256,4224]{2,1,0:T(8,128)(2,1)S(1)}, f32[4096,256]{1,0:T(8,128)S(1)}, f32[2,256]{1,0:T(2,128)S(1)}) custom-call(bf16[64,64,256]{2,1,0:T(8,128)(2,1)S(1)} %get-tuple-element.55.refs_0_.refs_1_.refs_2_, f32[2,256]{1,0:T(2,128)S(1)} %get-tuple-element.56.refs_2_.refs_1_.refs_3_, ...), custom_call_target="tpu_custom_call" | custom-call | tf_op jit(solution)/shard_map/pallas_call | solution.py:713
  39.3 11.8 %shard_map.137 = (bf16[66,64,256]{2,1,0:T(8,128)(2,1)S(1)}, f32[2,256]{1,0:T(2,128)S(1)}, f32[4608,128]{1,0:T(8,128)S(1)}, bf16[3,66,64,256]{3,2,1,0:T(8,128)(2,1)S(1)}, f32[1,256]{1,0:T(1,128)S(1)}) custom-call(bf16[3,66,64,256]{3,2,1,0:T(8,128)(2,1)S(1)} %copy-done.2, f32[4096,256]{1,0:T(8,128)S(1)} %get-tuple-element.64.refs_1_, ...), custom_call_target="tpu_custom_call" | custom-call | tf_op jit(solution)/shard_map/pallas_call | solution.py:713
  51.9 10.7 %shard_map.140 = (f32[4096,256]{1,0:T(8,128)S(1)}, f32[2,256]{1,0:T(2,128)S(1)}, f32[4608,128]{1,0:T(8,128)S(1)}) custom-call(bf16[2,256,4224]{2,1,0:T(8,128)(2,1)S(1)} %get-tuple-element.70.refs_0_, bf16[3,66,64,256]{3,2,1,0:T(8,128)(2,1)S(1)} %get-tuple-element.71.refs_1_, bf16[64,64,256]{2,1,0:T(8,128)(2,1)S(1)} %get-tuple-element.55.refs_0_.refs_1_.refs_2_, ...), custom_call_target="tpu_custom_call" | custom-call | tf_op jit(solution)/shard_map/pallas_call | solution.py:713
  63.0 1.9 %collective-permute-start.10 = (bf16[1408,128]{1,0:T(8,128)(2,1)S(1)}, bf16[1408,128]{1,0:T(8,128)(2,1)S(1)}, u32[]{:S(2)}, u32[]{:S(2)}) collective-permute-start(bf16[1408,128]{1,0:T(8,128)(2,1)S(1)} %get-tuple-element.87), channel_id=1, source_target_pairs={{0,16},{1,3},{2,18},{3,1},{4,20},{5,7},{6,22},{7,5},{8,24},{9,11},... | collective-permute-start | bytes 1081352 | tf_op jit(solution)/shard_map/ppermute | solution.py:35
  65.1 2.0 %collective-permute-start.9 = (bf16[1168,128]{1,0:T(8,128)(2,1)S(1)}, bf16[1168,128]{1,0:T(8,128)(2,1)S(1)}, u32[]{:S(2)}, u32[]{:S(2)}) collective-permute-start(bf16[1168,128]{1,0:T(8,128)(2,1)S(1)} %get-tuple-element.85), channel_id=1, source_target_pairs={{0,16},{1,3},{2,18},{3,1},{4,20},{5,7},{6,22},{7,5},{8,24},{9,11},... | collective-permute-start | bytes 897032 | tf_op jit(solution)/shard_map/ppermute | solution.py:35
  67.1 3.4 %shard_map.138 = (bf16[64,64,256]{2,1,0:T(8,128)(2,1)}, f32[1,256]{1,0:T(1,128)S(1)}) custom-call(bf16[66,64,256]{2,1,0:T(8,128)(2,1)S(1)} %get-tuple-element.67.refs_0_, bf16[64,64,256]{2,1,0:T(8,128)(2,1)S(1)} %get-tuple-element.55.refs_0_.refs_1_.refs_2_, f32[8,256]{1,0:T(8,128)S(1)} %get-tuple-element.61.refs_2_.refs_3_.refs_4_.refs_5_, ...), custom_call_target="tpu_custom_call" | custom-call | tf_op jit(solution)/shard_map/pallas_call | solution.py:713
  70.5 3.1 %collective-permute-done.9.refs_1_ = bf16[1168,128]{1,0:T(8,128)(2,1)S(1)} collective-permute-done((bf16[1168,128]{1,0:T(8,128)(2,1)S(1)}, bf16[1168,128]{1,0:T(8,128)(2,1)S(1)}, u32[]{:S(2)}, u32[]{:S(2)}) %collective-permute-start.9) | collective-permute-done | bytes 299040 | tf_op jit(solution)/shard_map/ppermute | solution.py:35
  73.8 1.9 %collective-permute-start.11 = (bf16[1296,128]{1,0:T(8,128)(2,1)S(1)}, bf16[1296,128]{1,0:T(8,128)(2,1)S(1)}, u32[]{:S(2)}, u32[]{:S(2)}) collective-permute-start(bf16[1296,128]{1,0:T(8,128)(2,1)S(1)} %get-tuple-element.90), channel_id=1, source_target_pairs={{0,2},{1,17},{2,0},{3,19},{4,6},{5,21},{6,4},{7,23},{8,10},{9,25},... | collective-permute-start | bytes 995336 | tf_op jit(solution)/shard_map/ppermute | solution.py:35
  75.8 3.4 %shard_map.139 = (bf16[64,64,256]{2,1,0:T(8,128)(2,1)}, f32[1,256]{1,0:T(1,128)S(1)}) custom-call(bf16[66,64,256]{2,1,0:T(8,128)(2,1)S(1)} %get-tuple-element.67.refs_0_, bf16[64,64,256]{2,1,0:T(8,128)(2,1)S(1)} %get-tuple-element.55.refs_0_.refs_1_.refs_2_, ...), custom_call_target="tpu_custom_call", output_to_operand_aliasing={{0}: (4, {})} | custom-call | tf_op jit(solution)/shard_map/pallas_call | solution.py:713
  79.2 1.8 %collective-permute-done.11.refs_1_ = bf16[1296,128]{1,0:T(8,128)(2,1)S(1)} collective-permute-done((bf16[1296,128]{1,0:T(8,128)(2,1)S(1)}, bf16[1296,128]{1,0:T(8,128)(2,1)S(1)}, u32[]{:S(2)}, u32[]{:S(2)}) %collective-permute-start.11) | collective-permute-done | bytes 331808 | tf_op jit(solution)/shard_map/ppermute | solution.py:35
  81.1 1.3 %collective-permute-start.12 = (bf16[656,128]{1,0:T(8,128)(2,1)S(1)}, bf16[656,128]{1,0:T(8,128)(2,1)S(1)}, u32[]{:S(2)}, u32[]{:S(2)}) collective-permute-start(bf16[656,128]{1,0:T(8,128)(2,1)S(1)} %get-tuple-element.93), channel_id=1, source_target_pairs={{0,4},{1,9},{2,6},{3,11},{4,0},{5,13},{6,2},{7,15},{8,12},{9,1},{1... | collective-permute-start | bytes 503816 | tf_op jit(solution)/shard_map/ppermute | solution.py:35
  82.4 3.5 %shard_map.141 = (f32[64,64,256]{2,1,0:T(8,128)}, f32[1,512]{1,0:T(1,128)}, f32[1,256]{1,0:T(1,128)S(1)}) custom-call(f32[4096,256]{1,0:T(8,128)S(1)} %get-tuple-element.72.refs_0_, bf16[64,64,256]{2,1,0:T(8,128)(2,1)S(1)} %bitcast.15, bf16[64,64,256]{2,1,0:T(8,128)(2,1)S(1)} %bitcast.13, f32[2,256]{1,0:T(2,128)S(1)} %get-tuple-element.56.refs_2_.refs_1_.refs_3_, ...), custom_call_target="tpu_custom_call" | custom-call | tf_op jit(solution)/shard_map/pallas_call | solution.py:713
  87.2 3.2 %collective-permute-start.13 = (bf16[336,128]{1,0:T(8,128)(2,1)S(1)}, bf16[336,128]{1,0:T(8,128)(2,1)S(1)}, u32[]{:S(2)}, u32[]{:S(2)}) collective-permute-start(bf16[336,128]{1,0:T(8,128)(2,1)S(1)} %get-tuple-element.96), channel_id=1, source_target_pairs={{0,8},{1,5},{2,10},{3,7},{4,12},{5,1},{6,14},{7,3},{8,0},{9,13},{1... | collective-permute-start | bytes 258056 | tf_op jit(solution)/shard_map/ppermute | solution.py:35
  90.4 2.5 %collective-permute-done.13.refs_1_ = bf16[336,128]{1,0:T(8,128)(2,1)S(1)} collective-permute-done((bf16[336,128]{1,0:T(8,128)(2,1)S(1)}, bf16[336,128]{1,0:T(8,128)(2,1)S(1)}, u32[]{:S(2)}, u32[]{:S(2)}) %collective-permute-start.13) | collective-permute-done | bytes 86048 | tf_op jit(solution)/shard_map/ppermute | solution.py:35
  (35 shorter events, 6.8 us)
Async XLA Ops:
  1.5 6.6 %collective-permute-start = (bf16[336,128]{1,0:T(8,128)(2,1)S(1)}, bf16[336,128]{1,0:T(8,128)(2,1)S(1)}, u32[]{:S(2)}, u32[]{:S(2)}) collective-permute-start(bf16[336,128]{1,0:T(8,128)(2,1)S(1)} %shard_map.128.refs_0_), channel_id=1, source_target_pairs={{0,8},{1,5},{2,10},{3,7},{4,12},{5,1},{6,14},{7,3},{8,0},{9,13},{1... | collective-permute-start | bytes 258056 | tf_op jit(solution)/shard_map/ppermute | solution.py:35
  8.1 6.1 %collective-permute-start.1 = (bf16[656,128]{1,0:T(8,128)(2,1)S(1)}, bf16[656,128]{1,0:T(8,128)(2,1)S(1)}, u32[]{:S(2)}, u32[]{:S(2)}) collective-permute-start(bf16[656,128]{1,0:T(8,128)(2,1)S(1)} %shard_map.129.refs_0_), channel_id=1, source_target_pairs={{0,4},{1,9},{2,6},{3,11},{4,0},{5,13},{6,2},{7,15},{8,12},{9,1},{1... | collective-permute-start | bytes 503816 | tf_op jit(solution)/shard_map/ppermute | solution.py:35
  14.2 7.2 %collective-permute-start.2 = (bf16[1296,128]{1,0:T(8,128)(2,1)S(1)}, bf16[1296,128]{1,0:T(8,128)(2,1)S(1)}, u32[]{:S(2)}, u32[]{:S(2)}) collective-permute-start(bf16[1296,128]{1,0:T(8,128)(2,1)S(1)} %shard_map.130.refs_0_), channel_id=1, source_target_pairs={{0,2},{1,17},{2,0},{3,19},{4,6},{5,21},{6,4},{7,23},{8,10},{9,25},... | collective-permute-start | bytes 995336 | tf_op jit(solution)/shard_map/ppermute | solution.py:35
  21.4 10.8 %copy-start.3 = (bf16[1,512]{1,0:T(2,128)(2,1)S(1)}, bf16[1,512]{1,0:T(2,128)(2,1)}, u32[]{:S(2)}) copy-start(bf16[1,512]{1,0:T(2,128)(2,1)} %refs_1_.1) | copy-start | bytes 3076
  21.4 7.5 %collective-permute-start.3 = (bf16[1424,128]{1,0:T(8,128)(2,1)S(1)}, bf16[1424,128]{1,0:T(8,128)(2,1)S(1)}, u32[]{:S(2)}, u32[]{:S(2)}) collective-permute-start(bf16[1424,128]{1,0:T(8,128)(2,1)S(1)} %get-tuple-element.58.refs_0_), channel_id=1, source_target_pairs={{0,16},{1,3},{2,18},{3,1},{4,20},{5,7},{6,22},{7,5},{8,24},{9,11},... | collective-permute-start | bytes 1093640 | tf_op jit(solution)/shard_map/ppermute | solution.py:35
  23.4 8.7 %collective-permute-start.5 = (bf16[1152,128]{1,0:T(8,128)(2,1)S(1)}, bf16[1152,128]{1,0:T(8,128)(2,1)S(1)}, u32[]{:S(2)}, u32[]{:S(2)}) collective-permute-start(bf16[1152,128]{1,0:T(8,128)(2,1)S(1)} %get-tuple-element.59.refs_0_), channel_id=1, source_target_pairs={{0,16},{1,3},{2,18},{3,1},{4,20},{5,7},{6,22},{7,5},{8,24},{9,11},... | collective-permute-start | bytes 884744 | tf_op jit(solution)/shard_map/ppermute | solution.py:35
  29.0 3.2 %collective-permute-start.4 = (bf16[2832,128]{1,0:T(8,128)(2,1)S(1)}, bf16[2832,128]{1,0:T(8,128)(2,1)S(1)}, u32[]{:S(2)}, u32[]{:S(2)}) collective-permute-start(bf16[2832,128]{1,0:T(8,128)(2,1)S(1)} %shard_map.132.refs_0_), channel_id=1, source_target_pairs={{0,1},{1,0},{2,3},{3,2},{4,5},{5,4},{6,7},{7,6},{8,9},{9,8},{10,11... | collective-permute-start | bytes 2174984 | tf_op jit(solution)/shard_map/ppermute | solution.py:35
  32.1 6.8 %collective-permute-start.6 = (bf16[2304,128]{1,0:T(8,128)(2,1)S(1)}, bf16[2304,128]{1,0:T(8,128)(2,1)S(1)}, u32[]{:S(2)}, u32[]{:S(2)}) collective-permute-start(bf16[2304,128]{1,0:T(8,128)(2,1)S(1)} %get-tuple-element.66.refs_0_), channel_id=1, source_target_pairs={{0,1},{1,0},{2,3},{3,2},{4,5},{5,4},{6,7},{7,6},{8,9},{9,8},{10,11... | collective-permute-start | bytes 1769480 | tf_op jit(solution)/shard_map/ppermute | solution.py:35
  32.2 7.0 %copy-start.2 = (bf16[3,66,64,256]{3,2,1,0:T(8,128)(2,1)S(1)}, bf16[3,66,64,256]{3,2,1,0:T(8,128)(2,1)}, u32[]{:S(2)}) copy-start(bf16[3,66,64,256]{3,2,1,0:T(8,128)(2,1)} %get-tuple-element.54.refs_0_) | copy-start | bytes 19464196
  51.4 11.3 %collective-permute-start.7 = (bf16[2816,128]{1,0:T(8,128)(2,1)S(1)}, bf16[2816,128]{1,0:T(8,128)(2,1)S(1)}, u32[]{:S(2)}, u32[]{:S(2)}) collective-permute-start(bf16[2816,128]{1,0:T(8,128)(2,1)S(1)} %get-tuple-element.81), channel_id=1, source_target_pairs={{0,1},{1,0},{2,3},{3,2},{4,5},{5,4},{6,7},{7,6},{8,9},{9,8},{10,11... | collective-permute-start | bytes 2162696 | tf_op jit(solution)/shard_map/ppermute | solution.py:35
  62.9 2.1 %collective-permute-start.8 = (bf16[2320,128]{1,0:T(8,128)(2,1)S(1)}, bf16[2320,128]{1,0:T(8,128)(2,1)S(1)}, u32[]{:S(2)}, u32[]{:S(2)}) collective-permute-start(bf16[2320,128]{1,0:T(8,128)(2,1)S(1)} %get-tuple-element.83), channel_id=1, source_target_pairs={{0,1},{1,0},{2,3},{3,2},{4,5},{5,4},{6,7},{7,6},{8,9},{9,8},{10,11... | collective-permute-start | bytes 1781768 | tf_op jit(solution)/shard_map/ppermute | solution.py:35
  63.0 7.5 %collective-permute-start.10 = (bf16[1408,128]{1,0:T(8,128)(2,1)S(1)}, bf16[1408,128]{1,0:T(8,128)(2,1)S(1)}, u32[]{:S(2)}, u32[]{:S(2)}) collective-permute-start(bf16[1408,128]{1,0:T(8,128)(2,1)S(1)} %get-tuple-element.87), channel_id=1, source_target_pairs={{0,16},{1,3},{2,18},{3,1},{4,20},{5,7},{6,22},{7,5},{8,24},{9,11},... | collective-permute-start | bytes 1081352 | tf_op jit(solution)/shard_map/ppermute | solution.py:35
  65.1 8.6 %collective-permute-start.9 = (bf16[1168,128]{1,0:T(8,128)(2,1)S(1)}, bf16[1168,128]{1,0:T(8,128)(2,1)S(1)}, u32[]{:S(2)}, u32[]{:S(2)}) collective-permute-start(bf16[1168,128]{1,0:T(8,128)(2,1)S(1)} %get-tuple-element.85), channel_id=1, source_target_pairs={{0,16},{1,3},{2,18},{3,1},{4,20},{5,7},{6,22},{7,5},{8,24},{9,11},... | collective-permute-start | bytes 897032 | tf_op jit(solution)/shard_map/ppermute | solution.py:35
  73.8 7.2 %collective-permute-start.11 = (bf16[1296,128]{1,0:T(8,128)(2,1)S(1)}, bf16[1296,128]{1,0:T(8,128)(2,1)S(1)}, u32[]{:S(2)}, u32[]{:S(2)}) collective-permute-start(bf16[1296,128]{1,0:T(8,128)(2,1)S(1)} %get-tuple-element.90), channel_id=1, source_target_pairs={{0,2},{1,17},{2,0},{3,19},{4,6},{5,21},{6,4},{7,23},{8,10},{9,25},... | collective-permute-start | bytes 995336 | tf_op jit(solution)/shard_map/ppermute | solution.py:35
  75.7 6.7 %copy-start = (bf16[1,64,64,256]{3,2,1,0:T(8,128)(2,1)S(1)}, bf16[1,64,64,256]{3,2,1,0:T(8,128)(2,1)}, u32[]{:S(2)}) copy-start(bf16[1,64,64,256]{3,2,1,0:T(8,128)(2,1)} %param.13) | copy-start | bytes 6291460
  75.8 6.7 %copy-start.1 = (bf16[1,64,64,256]{3,2,1,0:T(8,128)(2,1)S(1)}, bf16[1,64,64,256]{3,2,1,0:T(8,128)(2,1)}, u32[]{:S(2)}) copy-start(bf16[1,64,64,256]{3,2,1,0:T(8,128)(2,1)} %param.7) | copy-start | bytes 6291460
  81.1 6.0 %collective-permute-start.12 = (bf16[656,128]{1,0:T(8,128)(2,1)S(1)}, bf16[656,128]{1,0:T(8,128)(2,1)S(1)}, u32[]{:S(2)}, u32[]{:S(2)}) collective-permute-start(bf16[656,128]{1,0:T(8,128)(2,1)S(1)} %get-tuple-element.93), channel_id=1, source_target_pairs={{0,4},{1,9},{2,6},{3,11},{4,0},{5,13},{6,2},{7,15},{8,12},{9,1},{1... | collective-permute-start | bytes 503816 | tf_op jit(solution)/shard_map/ppermute | solution.py:35
  87.2 5.6 %collective-permute-start.13 = (bf16[336,128]{1,0:T(8,128)(2,1)S(1)}, bf16[336,128]{1,0:T(8,128)(2,1)S(1)}, u32[]{:S(2)}, u32[]{:S(2)}) collective-permute-start(bf16[336,128]{1,0:T(8,128)(2,1)S(1)} %get-tuple-element.96), channel_id=1, source_target_pairs={{0,8},{1,5},{2,10},{3,7},{4,12},{5,1},{6,14},{7,3},{8,0},{9,13},{1... | collective-permute-start | bytes 258056 | tf_op jit(solution)/shard_map/ppermute | solution.py:35

commit v8 on v7

--- a/solution.py
+++ b/solution.py
@@ -124,13 +124,13 @@
     return value * size if isinstance(value, int) else pl.multiple_of(value * size, size)
 
 
-def conv_step(accs, three, kernel, step, parity, back, others=()):
+def conv_step(accs, three, kernel, step, parity, back, others=(), turn=True):
     others = list(others)
     for tap, share in enumerate(interleave(len(others), 9)):
         at = (8 - tap if back else tap) * three.shape[3]
         stage = (parity + tap) % 2
         for unit in range(UNITS):
-            pltpu.matmul_push_rhs(kernel[at : at + three.shape[3], :], stage, unit, transpose=back)
+            pltpu.matmul_push_rhs(kernel[at : at + three.shape[3], :], stage, unit, transpose=back and turn)
         for piece in range(ROWS):
             for unit in range(UNITS):
                 row = (UNITS * step + unit) * ROWS + piece + tap // 3
@@ -148,11 +148,11 @@
     return [functools.partial(one, unit, piece) for unit in range(UNITS) for piece in range(ROWS)]
 
 
-def conv_all(accs, three, kernel, back, use):
+def conv_all(accs, three, kernel, back, use, turn=True):
     steps = (three.shape[1] - 2) // (UNITS * ROWS)
     for step in range(steps):
         others = conv_rows(accs, step - 1, (step - 1) % 2, use) if step else ()
-        conv_step(accs, three, kernel, step, step % 2, back, others)
+        conv_step(accs, three, kernel, step, step % 2, back, others, turn)
     assert steps % 2 == 0
     return conv_rows(accs, steps - 1, 1, use)
 
@@ -331,11 +331,11 @@
         away.wait()
 
 
-def first_kernel(x, stats, vec, time, kernel, turned, raw, stats_out, three):
-    accumulators(first_body, x, stats, vec, time, kernel, turned, raw, stats_out, three)
-
-
-def first_body(x, stats, vec, time, kernel, turned, raw, stats_out, three, accs):
+def first_kernel(x, stats, vec, time, kernel, turned, raw, stats_out, flipped, three):
+    accumulators(first_body, x, stats, vec, time, kernel, turned, raw, stats_out, flipped, three)
+
+
+def first_body(x, stats, vec, time, kernel, turned, raw, stats_out, flipped, three, accs):
     height, width, channels = x.shape
     pixels = height * width
     per_group = channels // GROUPS
@@ -358,6 +358,10 @@
         d = v - pivot[0]
         sums.add(d, d * d)
 
+    def flip(tap):
+        at = slice(tap * channels, (tap + 1) * channels)
+        flipped[at, :] = kernel[at, :].T
+
     per_step = UNITS * ROWS
     steps = height // per_step
     for row in range(per_step + 1):
@@ -365,8 +369,10 @@
     for step in range(steps):
         ahead = range((step + 1) * per_step + 1, min((step + 2) * per_step + 1, height))
         others = [functools.partial(activate, row) for row in ahead]
+        if step == steps - 1:
+            others = [functools.partial(flip, tap) for tap in range(9)]
         done = conv_rows(accs, step - 1, (step - 1) % 2, use) if step else []
-        mixed = [f for i in range(per_step) for f in (*others[i : i + 1], *done[i : i + 1])]
+        mixed = [f for i in range(per_step + 1) for f in (*others[i : i + 1], *done[i : i + 1])]
         conv_step(accs, three, kernel, step, step % 2, False, mixed)
     turn_end(turned, three.at[1])
     for other in conv_rows(accs, steps - 1, (steps - 1) % 2, use):
@@ -448,7 +454,7 @@
         dh[row * width : (row + 1) * width, :] = d
         both.add(d, d * c)
 
-    last = conv_all(accs, three, kernel, True, use)
+    last = conv_all(accs, three, kernel, True, use, False)
 
     def more():
         s, sn = [0.5 * v for v in both.totals()]
@@ -877,8 +883,8 @@
     one, one_got, two, two_got, mark = gather_start(wires, (cuts[0], cuts[2], cuts[1]), start, beside)
     first, vec, time = arrange_first(wires, (cuts[0], cuts[2]), one, one_got, embedding, (mark,))
 
-    turned_one, raw, stats_two = call(
-        first_kernel, [turned, flat, pair], x_near, stats, vec, time, first, scratch=[three], flops=conv_flops
+    turned_one, raw, stats_two, flipped = call(
+        first_kernel, [turned, flat, pair, ((9 * channels, channels), BF16)], x_near, stats, vec, time, first, scratch=[three], flops=conv_flops
     )
     kernel_two = arrange_second(wires, cuts[1:2], two, two_got, (stats_two,))
     act_two, sums_two, grad_two, e_three, dc_sum = call(
@@ -896,7 +902,7 @@
     two_send, two = pack_second(wires, cuts[1:], grad_two, embedding, dc_sum)
     two_got = wires.swap(two_send, last)
     dh_one, sums_one, grad_one = call(
-        third_kernel, [flat, pair, taps], turned_one, e_three, x_near, stats, vec, first
+        third_kernel, [flat, pair, taps], turned_one, e_three, x_near, stats, vec, flipped
     )
     one_send, one, two_send, two = pack_first(
         wires, cuts[:1], grad_one, dc_sum, sums_one, sums_two, g_sum, two, two_got

time: 93.7 us -> 93.5 us (level)
  no operation moved by 1% of the time
where the time goes in v8:
time: 93.5 us; the launch traced here: 93.3 us
  Pallas kernels  49.3 us (53%)
  waiting for transfers between devices  21.9 us (23%)
  starting transfers between devices  21.2 us (23%)
    pallas_call x23, Pallas kernels, call(): pl.pallas_call(run, out_shape=[pltpu.HBM(shape, dtype) if i in far_outs e...  49.3 us
    ppermute x14, waiting for transfers between devices, swap(): lax.ppermute(value, AXES, [(i, i ^ 1 << bit(i & 1)) for i in range(self.n)])  21.9 us
    ppermute x14, starting transfers between devices, swap(): lax.ppermute(value, AXES, [(i, i ^ 1 << bit(i & 1)) for i in range(self.n)])  21.2 us
  transfers between devices with their start and end apart: 14, of which 9 were waited for; matrix products, arithmetic and copies ran while one was open for 0% of the time, Pallas kernels for 37%

profile of v8, /device:TPU:0, one launch (start us, length us, event | category | flops | bytes accessed | tf_op | source)
XLA Modules:
  0.0 93.3 jit_solution(15383555289048298359)
XLA Ops:
  1.5 4.1 %collective-permute-start = (bf16[336,128]{1,0:T(8,128)(2,1)S(1)}, bf16[336,128]{1,0:T(8,128)(2,1)S(1)}, u32[]{:S(2)}, u32[]{:S(2)}) collective-permute-start(bf16[336,128]{1,0:T(8,128)(2,1)S(1)} %shard_map.128.refs_0_), channel_id=1, source_target_pairs={{0,8},{1,5},{2,10},{3,7},{4,12},{5,1},{6,14},{7,3},{8,0},{9,13},{1... | collective-permute-start | bytes 258056 | tf_op jit(solution)/shard_map/ppermute | solution.py:35
  5.6 2.5 %collective-permute-done.refs_1_ = bf16[336,128]{1,0:T(8,128)(2,1)S(1)} collective-permute-done((bf16[336,128]{1,0:T(8,128)(2,1)S(1)}, bf16[336,128]{1,0:T(8,128)(2,1)S(1)}, u32[]{:S(2)}, u32[]{:S(2)}) %collective-permute-start) | collective-permute-done | bytes 86048 | tf_op jit(solution)/shard_map/ppermute | solution.py:35
  8.1 2.0 %collective-permute-start.1 = (bf16[656,128]{1,0:T(8,128)(2,1)S(1)}, bf16[656,128]{1,0:T(8,128)(2,1)S(1)}, u32[]{:S(2)}, u32[]{:S(2)}) collective-permute-start(bf16[656,128]{1,0:T(8,128)(2,1)S(1)} %shard_map.129.refs_0_), channel_id=1, source_target_pairs={{0,4},{1,9},{2,6},{3,11},{4,0},{5,13},{6,2},{7,15},{8,12},{9,1},{1... | collective-permute-start | bytes 503816 | tf_op jit(solution)/shard_map/ppermute | solution.py:35
  10.1 4.1 %collective-permute-done.1.refs_1_ = bf16[656,128]{1,0:T(8,128)(2,1)S(1)} collective-permute-done((bf16[656,128]{1,0:T(8,128)(2,1)S(1)}, bf16[656,128]{1,0:T(8,128)(2,1)S(1)}, u32[]{:S(2)}, u32[]{:S(2)}) %collective-permute-start.1) | collective-permute-done | bytes 167968 | tf_op jit(solution)/shard_map/ppermute | solution.py:35
  14.2 1.9 %collective-permute-start.2 = (bf16[1296,128]{1,0:T(8,128)(2,1)S(1)}, bf16[1296,128]{1,0:T(8,128)(2,1)S(1)}, u32[]{:S(2)}, u32[]{:S(2)}) collective-permute-start(bf16[1296,128]{1,0:T(8,128)(2,1)S(1)} %shard_map.130.refs_0_), channel_id=1, source_target_pairs={{0,2},{1,17},{2,0},{3,19},{4,6},{5,21},{6,4},{7,23},{8,10},{9,25},... | collective-permute-start | bytes 995336 | tf_op jit(solution)/shard_map/ppermute | solution.py:35
  16.1 4.0 %shard_map.126 = (bf16[3,66,64,256]{3,2,1,0:T(8,128)(2,1)}, f32[1,256]{1,0:T(1,128)S(1)}) custom-call(bf16[64,64,256]{2,1,0:T(8,128)(2,1)} %bitcast.12), custom_call_target="tpu_custom_call" | custom-call | tf_op jit(solution)/shard_map/pallas_call | solution.py:719
  21.4 2.0 %collective-permute-start.3 = (bf16[1424,128]{1,0:T(8,128)(2,1)S(1)}, bf16[1424,128]{1,0:T(8,128)(2,1)S(1)}, u32[]{:S(2)}, u32[]{:S(2)}) collective-permute-start(bf16[1424,128]{1,0:T(8,128)(2,1)S(1)} %get-tuple-element.59.refs_0_), channel_id=1, source_target_pairs={{0,16},{1,3},{2,18},{3,1},{4,20},{5,7},{6,22},{7,5},{8,24},{9,11},... | collective-permute-start | bytes 1093640 | tf_op jit(solution)/shard_map/ppermute | solution.py:35
  23.5 2.8 %shard_map.127 = (f32[2,256]{1,0:T(2,128)S(1)}, bf16[64,64,256]{2,1,0:T(8,128)(2,1)S(1)}) custom-call(bf16[64,64,256]{2,1,0:T(8,128)(2,1)} %bitcast.14), custom_call_target="tpu_custom_call" | custom-call | tf_op jit(solution)/shard_map/pallas_call | solution.py:719
  26.3 2.6 %collective-permute-done.3.refs_1_ = bf16[1424,128]{1,0:T(8,128)(2,1)S(1)} collective-permute-done((bf16[1424,128]{1,0:T(8,128)(2,1)S(1)}, bf16[1424,128]{1,0:T(8,128)(2,1)S(1)}, u32[]{:S(2)}, u32[]{:S(2)}) %collective-permute-start.3) | collective-permute-done | bytes 364576 | tf_op jit(solution)/shard_map/ppermute | solution.py:35
  29.1 3.0 %collective-permute-done.5.refs_1_ = bf16[1152,128]{1,0:T(8,128)(2,1)S(1)} collective-permute-done((bf16[1152,128]{1,0:T(8,128)(2,1)S(1)}, bf16[1152,128]{1,0:T(8,128)(2,1)S(1)}, u32[]{:S(2)}, u32[]{:S(2)}) %collective-permute-start.5) | collective-permute-done | bytes 294944 | tf_op jit(solution)/shard_map/ppermute | solution.py:35
  32.7 6.2 %shard_map.135 = (bf16[2,256,4224]{2,1,0:T(8,128)(2,1)S(1)}, f32[4096,256]{1,0:T(8,128)S(1)}, f32[2,256]{1,0:T(2,128)S(1)}, bf16[2304,256]{1,0:T(8,128)(2,1)S(1)}) custom-call(bf16[64,64,256]{2,1,0:T(8,128)(2,1)S(1)} %get-tuple-element.56.refs_0_.refs_1_.refs_2_, f32[2,256]{1,0:T(2,128)S(1)} %get-tuple-element.57.refs_2_.refs_1_.refs_3_, ...), custom_call_target="tpu_custom_call" | custom-call | tf_op jit(solution)/shard_map/pallas_call | solution.py:719
  39.2 11.8 %shard_map.137 = (bf16[66,64,256]{2,1,0:T(8,128)(2,1)S(1)}, f32[2,256]{1,0:T(2,128)S(1)}, f32[4608,128]{1,0:T(8,128)S(1)}, bf16[3,66,64,256]{3,2,1,0:T(8,128)(2,1)S(1)}, f32[1,256]{1,0:T(1,128)S(1)}) custom-call(bf16[3,66,64,256]{3,2,1,0:T(8,128)(2,1)S(1)} %copy-done.2, f32[4096,256]{1,0:T(8,128)S(1)} %get-tuple-element.65.refs_1_, ...), custom_call_target="tpu_custom_call" | custom-call | tf_op jit(solution)/shard_map/pallas_call | solution.py:719
  51.9 10.5 %shard_map.140 = (f32[4096,256]{1,0:T(8,128)S(1)}, f32[2,256]{1,0:T(2,128)S(1)}, f32[4608,128]{1,0:T(8,128)S(1)}) custom-call(bf16[2,256,4224]{2,1,0:T(8,128)(2,1)S(1)} %get-tuple-element.71.refs_0_, bf16[3,66,64,256]{3,2,1,0:T(8,128)(2,1)S(1)} %get-tuple-element.72.refs_1_, bf16[64,64,256]{2,1,0:T(8,128)(2,1)S(1)} %get-tuple-element.56.refs_0_.refs_1_.refs_2_, ...), custom_call_target="tpu_custom_call" | custom-call | tf_op jit(solution)/shard_map/pallas_call | solution.py:719
  62.8 1.9 %collective-permute-start.10 = (bf16[1408,128]{1,0:T(8,128)(2,1)S(1)}, bf16[1408,128]{1,0:T(8,128)(2,1)S(1)}, u32[]{:S(2)}, u32[]{:S(2)}) collective-permute-start(bf16[1408,128]{1,0:T(8,128)(2,1)S(1)} %get-tuple-element.89), channel_id=1, source_target_pairs={{0,16},{1,3},{2,18},{3,1},{4,20},{5,7},{6,22},{7,5},{8,24},{9,11},... | collective-permute-start | bytes 1081352 | tf_op jit(solution)/shard_map/ppermute | solution.py:35
  64.9 2.0 %collective-permute-start.9 = (bf16[1168,128]{1,0:T(8,128)(2,1)S(1)}, bf16[1168,128]{1,0:T(8,128)(2,1)S(1)}, u32[]{:S(2)}, u32[]{:S(2)}) collective-permute-start(bf16[1168,128]{1,0:T(8,128)(2,1)S(1)} %get-tuple-element.87), channel_id=1, source_target_pairs={{0,16},{1,3},{2,18},{3,1},{4,20},{5,7},{6,22},{7,5},{8,24},{9,11},... | collective-permute-start | bytes 897032 | tf_op jit(solution)/shard_map/ppermute | solution.py:35
  66.9 3.4 %shard_map.138 = (bf16[64,64,256]{2,1,0:T(8,128)(2,1)}, f32[1,256]{1,0:T(1,128)S(1)}) custom-call(bf16[66,64,256]{2,1,0:T(8,128)(2,1)S(1)} %get-tuple-element.68.refs_0_, bf16[64,64,256]{2,1,0:T(8,128)(2,1)S(1)} %get-tuple-element.56.refs_0_.refs_1_.refs_2_, f32[8,256]{1,0:T(8,128)S(1)} %get-tuple-element.62.refs_2_.refs_3_.refs_4_.refs_5_, ...), custom_call_target="tpu_custom_call" | custom-call | tf_op jit(solution)/shard_map/pallas_call | solution.py:719
  70.3 3.1 %collective-permute-done.9.refs_1_ = bf16[1168,128]{1,0:T(8,128)(2,1)S(1)} collective-permute-done((bf16[1168,128]{1,0:T(8,128)(2,1)S(1)}, bf16[1168,128]{1,0:T(8,128)(2,1)S(1)}, u32[]{:S(2)}, u32[]{:S(2)}) %collective-permute-start.9) | collective-permute-done | bytes 299040 | tf_op jit(solution)/shard_map/ppermute | solution.py:35
  73.6 1.9 %collective-permute-start.11 = (bf16[1296,128]{1,0:T(8,128)(2,1)S(1)}, bf16[1296,128]{1,0:T(8,128)(2,1)S(1)}, u32[]{:S(2)}, u32[]{:S(2)}) collective-permute-start(bf16[1296,128]{1,0:T(8,128)(2,1)S(1)} %get-tuple-element.92), channel_id=1, source_target_pairs={{0,2},{1,17},{2,0},{3,19},{4,6},{5,21},{6,4},{7,23},{8,10},{9,25},... | collective-permute-start | bytes 995336 | tf_op jit(solution)/shard_map/ppermute | solution.py:35
  75.5 3.7 %shard_map.139 = (bf16[64,64,256]{2,1,0:T(8,128)(2,1)}, f32[1,256]{1,0:T(1,128)S(1)}) custom-call(bf16[66,64,256]{2,1,0:T(8,128)(2,1)S(1)} %get-tuple-element.68.refs_0_, bf16[64,64,256]{2,1,0:T(8,128)(2,1)S(1)} %get-tuple-element.56.refs_0_.refs_1_.refs_2_, ...), custom_call_target="tpu_custom_call", output_to_operand_aliasing={{0}: (4, {})} | custom-call | tf_op jit(solution)/shard_map/pallas_call | solution.py:719
  79.2 1.6 %collective-permute-done.11.refs_1_ = bf16[1296,128]{1,0:T(8,128)(2,1)S(1)} collective-permute-done((bf16[1296,128]{1,0:T(8,128)(2,1)S(1)}, bf16[1296,128]{1,0:T(8,128)(2,1)S(1)}, u32[]{:S(2)}, u32[]{:S(2)}) %collective-permute-start.11) | collective-permute-done | bytes 331808 | tf_op jit(solution)/shard_map/ppermute | solution.py:35
  80.9 1.3 %collective-permute-start.12 = (bf16[656,128]{1,0:T(8,128)(2,1)S(1)}, bf16[656,128]{1,0:T(8,128)(2,1)S(1)}, u32[]{:S(2)}, u32[]{:S(2)}) collective-permute-start(bf16[656,128]{1,0:T(8,128)(2,1)S(1)} %get-tuple-element.95), channel_id=1, source_target_pairs={{0,4},{1,9},{2,6},{3,11},{4,0},{5,13},{6,2},{7,15},{8,12},{9,1},{1... | collective-permute-start | bytes 503816 | tf_op jit(solution)/shard_map/ppermute | solution.py:35
  82.2 3.5 %shard_map.141 = (f32[64,64,256]{2,1,0:T(8,128)}, f32[1,512]{1,0:T(1,128)}, f32[1,256]{1,0:T(1,128)S(1)}) custom-call(f32[4096,256]{1,0:T(8,128)S(1)} %get-tuple-element.74.refs_0_, bf16[64,64,256]{2,1,0:T(8,128)(2,1)S(1)} %bitcast.15, bf16[64,64,256]{2,1,0:T(8,128)(2,1)S(1)} %bitcast.13, f32[2,256]{1,0:T(2,128)S(1)} %get-tuple-element.57.refs_2_.refs_1_.refs_3_, ...), custom_call_target="tpu_custom_call" | custom-call | tf_op jit(solution)/shard_map/pallas_call | solution.py:719
  86.9 3.2 %collective-permute-start.13 = (bf16[336,128]{1,0:T(8,128)(2,1)S(1)}, bf16[336,128]{1,0:T(8,128)(2,1)S(1)}, u32[]{:S(2)}, u32[]{:S(2)}) collective-permute-start(bf16[336,128]{1,0:T(8,128)(2,1)S(1)} %get-tuple-element.98), channel_id=1, source_target_pairs={{0,8},{1,5},{2,10},{3,7},{4,12},{5,1},{6,14},{7,3},{8,0},{9,13},{1... | collective-permute-start | bytes 258056 | tf_op jit(solution)/shard_map/ppermute | solution.py:35
  90.1 2.5 %collective-permute-done.13.refs_1_ = bf16[336,128]{1,0:T(8,128)(2,1)S(1)} collective-permute-done((bf16[336,128]{1,0:T(8,128)(2,1)S(1)}, bf16[336,128]{1,0:T(8,128)(2,1)S(1)}, u32[]{:S(2)}, u32[]{:S(2)}) %collective-permute-start.13) | collective-permute-done | bytes 86048 | tf_op jit(solution)/shard_map/ppermute | solution.py:35
  (35 shorter events, 6.8 us)
Async XLA Ops:
  1.5 6.6 %collective-permute-start = (bf16[336,128]{1,0:T(8,128)(2,1)S(1)}, bf16[336,128]{1,0:T(8,128)(2,1)S(1)}, u32[]{:S(2)}, u32[]{:S(2)}) collective-permute-start(bf16[336,128]{1,0:T(8,128)(2,1)S(1)} %shard_map.128.refs_0_), channel_id=1, source_target_pairs={{0,8},{1,5},{2,10},{3,7},{4,12},{5,1},{6,14},{7,3},{8,0},{9,13},{1... | collective-permute-start | bytes 258056 | tf_op jit(solution)/shard_map/ppermute | solution.py:35
  8.1 6.1 %collective-permute-start.1 = (bf16[656,128]{1,0:T(8,128)(2,1)S(1)}, bf16[656,128]{1,0:T(8,128)(2,1)S(1)}, u32[]{:S(2)}, u32[]{:S(2)}) collective-permute-start(bf16[656,128]{1,0:T(8,128)(2,1)S(1)} %shard_map.129.refs_0_), channel_id=1, source_target_pairs={{0,4},{1,9},{2,6},{3,11},{4,0},{5,13},{6,2},{7,15},{8,12},{9,1},{1... | collective-permute-start | bytes 503816 | tf_op jit(solution)/shard_map/ppermute | solution.py:35
  14.2 7.2 %collective-permute-start.2 = (bf16[1296,128]{1,0:T(8,128)(2,1)S(1)}, bf16[1296,128]{1,0:T(8,128)(2,1)S(1)}, u32[]{:S(2)}, u32[]{:S(2)}) collective-permute-start(bf16[1296,128]{1,0:T(8,128)(2,1)S(1)} %shard_map.130.refs_0_), channel_id=1, source_target_pairs={{0,2},{1,17},{2,0},{3,19},{4,6},{5,21},{6,4},{7,23},{8,10},{9,25},... | collective-permute-start | bytes 995336 | tf_op jit(solution)/shard_map/ppermute | solution.py:35
  21.4 10.8 %copy-start.3 = (bf16[1,512]{1,0:T(2,128)(2,1)S(1)}, bf16[1,512]{1,0:T(2,128)(2,1)}, u32[]{:S(2)}) copy-start(bf16[1,512]{1,0:T(2,128)(2,1)} %refs_1_.1) | copy-start | bytes 3076
  21.4 7.5 %collective-permute-start.3 = (bf16[1424,128]{1,0:T(8,128)(2,1)S(1)}, bf16[1424,128]{1,0:T(8,128)(2,1)S(1)}, u32[]{:S(2)}, u32[]{:S(2)}) collective-permute-start(bf16[1424,128]{1,0:T(8,128)(2,1)S(1)} %get-tuple-element.59.refs_0_), channel_id=1, source_target_pairs={{0,16},{1,3},{2,18},{3,1},{4,20},{5,7},{6,22},{7,5},{8,24},{9,11},... | collective-permute-start | bytes 1093640 | tf_op jit(solution)/shard_map/ppermute | solution.py:35
  23.4 8.7 %collective-permute-start.5 = (bf16[1152,128]{1,0:T(8,128)(2,1)S(1)}, bf16[1152,128]{1,0:T(8,128)(2,1)S(1)}, u32[]{:S(2)}, u32[]{:S(2)}) collective-permute-start(bf16[1152,128]{1,0:T(8,128)(2,1)S(1)} %get-tuple-element.60.refs_0_), channel_id=1, source_target_pairs={{0,16},{1,3},{2,18},{3,1},{4,20},{5,7},{6,22},{7,5},{8,24},{9,11},... | collective-permute-start | bytes 884744 | tf_op jit(solution)/shard_map/ppermute | solution.py:35
  29.0 3.2 %collective-permute-start.4 = (bf16[2832,128]{1,0:T(8,128)(2,1)S(1)}, bf16[2832,128]{1,0:T(8,128)(2,1)S(1)}, u32[]{:S(2)}, u32[]{:S(2)}) collective-permute-start(bf16[2832,128]{1,0:T(8,128)(2,1)S(1)} %shard_map.132.refs_0_), channel_id=1, source_target_pairs={{0,1},{1,0},{2,3},{3,2},{4,5},{5,4},{6,7},{7,6},{8,9},{9,8},{10,11... | collective-permute-start | bytes 2174984 | tf_op jit(solution)/shard_map/ppermute | solution.py:35
  32.1 6.8 %collective-permute-start.6 = (bf16[2304,128]{1,0:T(8,128)(2,1)S(1)}, bf16[2304,128]{1,0:T(8,128)(2,1)S(1)}, u32[]{:S(2)}, u32[]{:S(2)}) collective-permute-start(bf16[2304,128]{1,0:T(8,128)(2,1)S(1)} %get-tuple-element.67.refs_0_), channel_id=1, source_target_pairs={{0,1},{1,0},{2,3},{3,2},{4,5},{5,4},{6,7},{7,6},{8,9},{9,8},{10,11... | collective-permute-start | bytes 1769480 | tf_op jit(solution)/shard_map/ppermute | solution.py:35
  32.2 7.0 %copy-start.2 = (bf16[3,66,64,256]{3,2,1,0:T(8,128)(2,1)S(1)}, bf16[3,66,64,256]{3,2,1,0:T(8,128)(2,1)}, u32[]{:S(2)}) copy-start(bf16[3,66,64,256]{3,2,1,0:T(8,128)(2,1)} %get-tuple-element.55.refs_0_) | copy-start | bytes 19464196
  51.3 11.1 %collective-permute-start.7 = (bf16[2816,128]{1,0:T(8,128)(2,1)S(1)}, bf16[2816,128]{1,0:T(8,128)(2,1)S(1)}, u32[]{:S(2)}, u32[]{:S(2)}) collective-permute-start(bf16[2816,128]{1,0:T(8,128)(2,1)S(1)} %get-tuple-element.83), channel_id=1, source_target_pairs={{0,1},{1,0},{2,3},{3,2},{4,5},{5,4},{6,7},{7,6},{8,9},{9,8},{10,11... | collective-permute-start | bytes 2162696 | tf_op jit(solution)/shard_map/ppermute | solution.py:35
  62.7 2.1 %collective-permute-start.8 = (bf16[2320,128]{1,0:T(8,128)(2,1)S(1)}, bf16[2320,128]{1,0:T(8,128)(2,1)S(1)}, u32[]{:S(2)}, u32[]{:S(2)}) collective-permute-start(bf16[2320,128]{1,0:T(8,128)(2,1)S(1)} %get-tuple-element.85), channel_id=1, source_target_pairs={{0,1},{1,0},{2,3},{3,2},{4,5},{5,4},{6,7},{7,6},{8,9},{9,8},{10,11... | collective-permute-start | bytes 1781768 | tf_op jit(solution)/shard_map/ppermute | solution.py:35
  62.8 7.5 %collective-permute-start.10 = (bf16[1408,128]{1,0:T(8,128)(2,1)S(1)}, bf16[1408,128]{1,0:T(8,128)(2,1)S(1)}, u32[]{:S(2)}, u32[]{:S(2)}) collective-permute-start(bf16[1408,128]{1,0:T(8,128)(2,1)S(1)} %get-tuple-element.89), channel_id=1, source_target_pairs={{0,16},{1,3},{2,18},{3,1},{4,20},{5,7},{6,22},{7,5},{8,24},{9,11},... | collective-permute-start | bytes 1081352 | tf_op jit(solution)/shard_map/ppermute | solution.py:35
  64.9 8.6 %collective-permute-start.9 = (bf16[1168,128]{1,0:T(8,128)(2,1)S(1)}, bf16[1168,128]{1,0:T(8,128)(2,1)S(1)}, u32[]{:S(2)}, u32[]{:S(2)}) collective-permute-start(bf16[1168,128]{1,0:T(8,128)(2,1)S(1)} %get-tuple-element.87), channel_id=1, source_target_pairs={{0,16},{1,3},{2,18},{3,1},{4,20},{5,7},{6,22},{7,5},{8,24},{9,11},... | collective-permute-start | bytes 897032 | tf_op jit(solution)/shard_map/ppermute | solution.py:35
  73.6 7.2 %collective-permute-start.11 = (bf16[1296,128]{1,0:T(8,128)(2,1)S(1)}, bf16[1296,128]{1,0:T(8,128)(2,1)S(1)}, u32[]{:S(2)}, u32[]{:S(2)}) collective-permute-start(bf16[1296,128]{1,0:T(8,128)(2,1)S(1)} %get-tuple-element.92), channel_id=1, source_target_pairs={{0,2},{1,17},{2,0},{3,19},{4,6},{5,21},{6,4},{7,23},{8,10},{9,25},... | collective-permute-start | bytes 995336 | tf_op jit(solution)/shard_map/ppermute | solution.py:35
  75.5 6.7 %copy-start = (bf16[1,64,64,256]{3,2,1,0:T(8,128)(2,1)S(1)}, bf16[1,64,64,256]{3,2,1,0:T(8,128)(2,1)}, u32[]{:S(2)}) copy-start(bf16[1,64,64,256]{3,2,1,0:T(8,128)(2,1)} %param.13) | copy-start | bytes 6291460
  75.5 6.7 %copy-start.1 = (bf16[1,64,64,256]{3,2,1,0:T(8,128)(2,1)S(1)}, bf16[1,64,64,256]{3,2,1,0:T(8,128)(2,1)}, u32[]{:S(2)}) copy-start(bf16[1,64,64,256]{3,2,1,0:T(8,128)(2,1)} %param.7) | copy-start | bytes 6291460
  80.9 6.0 %collective-permute-start.12 = (bf16[656,128]{1,0:T(8,128)(2,1)S(1)}, bf16[656,128]{1,0:T(8,128)(2,1)S(1)}, u32[]{:S(2)}, u32[]{:S(2)}) collective-permute-start(bf16[656,128]{1,0:T(8,128)(2,1)S(1)} %get-tuple-element.95), channel_id=1, source_target_pairs={{0,4},{1,9},{2,6},{3,11},{4,0},{5,13},{6,2},{7,15},{8,12},{9,1},{1... | collective-permute-start | bytes 503816 | tf_op jit(solution)/shard_map/ppermute | solution.py:35
  86.9 5.7 %collective-permute-start.13 = (bf16[336,128]{1,0:T(8,128)(2,1)S(1)}, bf16[336,128]{1,0:T(8,128)(2,1)S(1)}, u32[]{:S(2)}, u32[]{:S(2)}) collective-permute-start(bf16[336,128]{1,0:T(8,128)(2,1)S(1)} %get-tuple-element.98), channel_id=1, source_target_pairs={{0,8},{1,5},{2,10},{3,7},{4,12},{5,1},{6,14},{7,3},{8,0},{9,13},{1... | collective-permute-start | bytes 258056 | tf_op jit(solution)/shard_map/ppermute | solution.py:35
